TPU v7x, 32 devices: a whole 2x2x4 slice. The times are simulated.
32 devices in a mesh: dp: 4 (over z), row: 4 (over y, core), col: 2 (over x).
Axes of the slice: x: 2, y: 2, z: 4, core: 2. Of those that a mesh axis runs over, the one named last changes fastest.
Arguments:
- inputs: bfloat16 [8192, 2048], P(('dp', 'row'), 'col'), may hold values from -6 to 6
- segments: int32 [8, 1024], P('dp'), may hold values from 0 to 6, as said below
- norm1_gain: bfloat16 [2048], P('col'), may hold values from 0.25 to 1.75
- query_weight: bfloat16 [2048, 2048], P('col', 'row'), may hold values from -0.125 to 0.125
- key_weight: bfloat16 [2048, 256], P('col', 'row'), may hold values from -0.125 to 0.125
- value_weight: bfloat16 [2048, 256], P('col', 'row'), may hold values from -0.125 to 0.125
- out_weight: bfloat16 [2048, 2048], P('row', 'col'), may hold values from -0.5 to 0.5
- norm2_gain: bfloat16 [2048], P('col'), may hold values from 0.25 to 1.75
- gate_weight: bfloat16 [2048, 5632], P('col', 'row'), may hold values from -0.125 to 0.125
- up_weight: bfloat16 [2048, 5632], P('col', 'row'), may hold values from -0.125 to 0.125
- down_weight: bfloat16 [5632, 2048], P('row', 'col'), may hold values from -0.109375 to 0.109375
- cotangent: bfloat16 [8192, 2048], P(('dp', 'row'), 'col'), may hold values from -6 to 6
Outputs:
- outputs: bfloat16 [8192, 2048], P(('dp', 'row'), 'col')
- grad_inputs: float32 [8192, 2048], P(('dp', 'row'), 'col')
- grad_norm1: float32 [2048], P('col')
- grad_query: float32 [2048, 2048], P('col', 'row')
- grad_key: float32 [2048, 256], P('col', 'row')
- grad_value: float32 [2048, 256], P('col', 'row')
- grad_out: float32 [2048, 2048], P('row', 'col')
- grad_norm2: float32 [2048], P('col')
- grad_gate: float32 [2048, 5632], P('col', 'row')
- grad_up: float32 [2048, 5632], P('col', 'row')
- grad_down: float32 [5632, 2048], P('row', 'col')
Inputs may be any that keep to these rules, and one draw needn't show every extreme that they name: `segments`: within each sequence the numbers start at 0 and rise by 0 or 1 from one token to the next; equal numbers mark one document.
All inputs are finite; a program needn't handle non-finite values.
Results may differ from a plain program's by a relative error of at most 0.018.
Values may be sent and summed in bfloat16 or wider, within the bound.
No kernel may reach another device: no remote copies, remote signals or barrier semaphores. Data moves between devices by JAX's collectives and lax.ppermute only.
A program may use at most 320 MiB of HBM per device.

v0:
```python
import jax
import jax.numpy as jnp
from jax import lax
from jax.sharding import PartitionSpec as P

HD = 64


epsilon = 1e-05
rope_base = 10000.0


def positions_of(segment_row):
    indices = jnp.arange(segment_row.shape[0], dtype=jnp.int32)
    previous = jnp.concatenate([segment_row[:1] - 1, segment_row[:-1]])
    start_index = lax.cummax(jnp.where(segment_row != previous, indices, 0), axis=0)
    return indices - start_index


def rotate(vectors, positions):
    half_width = vectors.shape[-1] // 2
    frequency = rope_base ** (-jnp.arange(half_width).astype(jnp.float32) * 2.0 / vectors.shape[-1])
    angles = positions.astype(jnp.float32)[..., None] * frequency
    cosine = jnp.concatenate([jnp.cos(angles), jnp.cos(angles)], -1)[..., None, :]
    sine_table = jnp.concatenate([jnp.sin(angles), jnp.sin(angles)], -1)[..., None, :]
    turned = jnp.concatenate([-vectors[..., half_width:], vectors[..., :half_width]], -1)
    return vectors * cosine + turned * sine_table


def width_sum(partial_sums):
    return lax.psum(partial_sums, "col")


def norm_forward(values, gain, full_width):
    squares = width_sum(jnp.sum(values * values, -1, keepdims=True))
    scale = lax.rsqrt(squares / full_width + epsilon)
    normed = values * scale
    return (normed, scale, (normed * gain).astype(jnp.bfloat16))


def norm_backward(grad_hidden, normed, scale, gain, full_width):
    grad_normed = grad_hidden * gain
    inner_sum = width_sum(jnp.sum(grad_normed * normed, -1, keepdims=True))
    return (
        scale * (grad_normed - normed * inner_sum / full_width),
        jnp.sum(grad_hidden * normed, 0),
    )


def contract(leading, weight, flipped):
    if flipped:
        return lax.dot_general(
            leading, weight, (((1,), (1,)), ((), ())), preferred_element_type=jnp.float32
        )
    return jnp.dot(leading, weight, preferred_element_type=jnp.float32)


def outer_sum(leading, trailing):
    return lax.dot_general(
        leading, trailing, (((0,), (0,)), ((), ())), preferred_element_type=jnp.float32
    )


def section_in(local_rows, weight, flipped):
    gathered = lax.all_gather(local_rows, "row", axis=0, tiled=True)
    portion = gathered.shape[0] // lax.axis_size("col")

    def partial_rows(first_row, row_count):
        return contract(gathered, weight, flipped)

    return (
        gathered,
        lax.psum_scatter(
            partial_rows(jnp.int32(0), lax.axis_size("col") * portion),
            "col",
            scatter_dimension=0,
            tiled=True,
        ),
    )


def section_out(local_rows, weight, flipped):
    gathered = lax.all_gather(local_rows, "col", axis=0, tiled=True)
    portion = gathered.shape[0] // lax.axis_size("row")

    def partial_rows(first_row, row_count):
        return contract(gathered, weight, flipped)

    return (
        gathered,
        lax.psum_scatter(
            partial_rows(jnp.int32(0), lax.axis_size("row") * portion),
            "row",
            scatter_dimension=0,
            tiled=True,
        ),
    )


def score_block(queries, key_rows, segment_row):
    length = queries.shape[0]
    pair_heads = key_rows.shape[1] // HD
    grouped = queries.reshape(length, pair_heads, -1, HD)
    keyed = key_rows.reshape(length, pair_heads, HD)
    scores = jnp.einsum(
        "qkgd,skd->kgqs", grouped, keyed, preferred_element_type=jnp.float32
    ) * HD ** (-0.5)
    indices = jnp.arange(length, dtype=jnp.int32)
    allowed = (segment_row[:, None] == segment_row[None, :]) & (
        indices[:, None] >= indices[None, :]
    )
    return (grouped, keyed, jnp.where(allowed, scores, -1e30), allowed)


def attention_forward(packed):
    queries, key_rows, value_rows, segment_row = packed
    grouped, keyed, scores, allowed = score_block(queries, key_rows, segment_row)
    highest_score = jnp.max(scores, -1, keepdims=True)
    weights = jnp.exp(scores - highest_score)
    totals = jnp.sum(weights, -1, keepdims=True)
    weights_low = (weights / totals).astype(jnp.bfloat16)
    valued = value_rows.reshape(keyed.shape)
    mixture = jnp.einsum("kgqs,skd->qkgd", weights_low, valued, preferred_element_type=jnp.float32)
    return (mixture.reshape(queries.shape).astype(jnp.bfloat16), highest_score + jnp.log(totals))


def attention_backward(packed):
    queries, key_rows, value_rows, segment_row, log_total, grad_mixture = packed
    grouped, keyed, scores, allowed = score_block(queries, key_rows, segment_row)
    weights = jnp.where(allowed, jnp.exp(scores - log_total), 0.0)
    valued = value_rows.reshape(keyed.shape)
    grad_grouped = grad_mixture.reshape(grouped.shape)
    grad_weights = jnp.einsum(
        "qkgd,skd->kgqs", grad_grouped, valued, preferred_element_type=jnp.float32
    )
    row_inner = jnp.sum(weights * grad_weights, -1, keepdims=True)
    grad_scores = (weights * (grad_weights - row_inner)).astype(jnp.bfloat16)
    scale_factor = HD ** (-0.5)
    grad_queries = (
        jnp.einsum("kgqs,skd->qkgd", grad_scores, keyed, preferred_element_type=jnp.float32)
        * scale_factor
    )
    grad_keys = (
        jnp.einsum("kgqs,qkgd->skd", grad_scores, grouped, preferred_element_type=jnp.float32)
        * scale_factor
    )
    grad_values = jnp.einsum(
        "kgqs,qkgd->skd",
        weights.astype(jnp.bfloat16),
        grad_grouped,
        preferred_element_type=jnp.float32,
    )
    return (grad_queries.reshape(queries.shape[0], -1, HD), grad_keys, grad_values)


def body(
    inputs,
    segments,
    norm1_gain,
    query_weight,
    key_weight,
    value_weight,
    out_weight,
    norm2_gain,
    gate_weight,
    up_weight,
    down_weight,
    cotangent,
):
    full_width = norm1_gain.shape[0] * lax.axis_size("col")
    query_width = query_weight.shape[1]
    pair_width = key_weight.shape[1]
    hidden_width = gate_weight.shape[1]
    per_column = segments.shape[0] // lax.axis_size("col")
    seq_length = segments.shape[1]
    local_segments = lax.dynamic_slice_in_dim(
        segments, lax.axis_index("col") * per_column, per_column, 0
    )
    positions = jax.vmap(positions_of)(local_segments).reshape(-1)
    local_tokens = positions.shape[0]
    features = inputs.astype(jnp.float32)
    gain_one = norm1_gain.astype(jnp.float32)
    gain_two = norm2_gain.astype(jnp.float32)
    normed_one, scale_one, hidden_one = norm_forward(features, gain_one, full_width)
    qkv_weight = jnp.concatenate([query_weight, key_weight, value_weight], 1)
    hidden_one_all, projected = section_in(hidden_one, qkv_weight, False)
    queries = (
        rotate(projected[:, :query_width].reshape(local_tokens, -1, HD), positions)
        .reshape(local_tokens, query_width)
        .astype(jnp.bfloat16)
    )
    key_rows = (
        rotate(
            projected[:, query_width : query_width + pair_width].reshape(local_tokens, -1, HD),
            positions,
        )
        .reshape(local_tokens, pair_width)
        .astype(jnp.bfloat16)
    )
    value_rows = projected[:, query_width + pair_width :].astype(jnp.bfloat16)
    by_sequence = (
        queries.reshape(per_column, seq_length, query_width),
        key_rows.reshape(per_column, seq_length, pair_width),
        value_rows.reshape(per_column, seq_length, pair_width),
        local_segments,
    )
    attended, log_totals = lax.map(attention_forward, by_sequence)
    attended = attended.reshape(local_tokens, query_width)
    attended_all, attn_branch = section_out(attended, out_weight, False)
    middle = features + attn_branch
    normed_two, scale_two, hidden_two = norm_forward(middle, gain_two, full_width)
    gate_up_weight = jnp.concatenate([gate_weight, up_weight], 1)
    hidden_two_all, gate_up = section_in(hidden_two, gate_up_weight, False)
    gate_part = gate_up[:, :hidden_width]
    up_part = gate_up[:, hidden_width:]
    sigmoid_gate = jax.nn.sigmoid(gate_part)
    activated = (gate_part * sigmoid_gate * up_part).astype(jnp.bfloat16)
    activated_all, ffn_branch = section_out(activated, down_weight, False)
    outputs = (middle + ffn_branch).astype(jnp.bfloat16)
    cotangent_all, grad_activated = section_in(cotangent, down_weight, True)
    grad_down = outer_sum(activated_all, cotangent_all)
    grad_gate_part = (
        grad_activated * up_part * sigmoid_gate * (1.0 + gate_part * (1.0 - sigmoid_gate))
    )
    grad_up_part = grad_activated * gate_part * sigmoid_gate
    grad_gate_up = jnp.concatenate([grad_gate_part, grad_up_part], 1).astype(jnp.bfloat16)
    grad_gate_up_all, grad_hidden_two = section_out(grad_gate_up, gate_up_weight, True)
    grad_gate_up_weight = outer_sum(hidden_two_all, grad_gate_up_all)
    grad_gate = grad_gate_up_weight[:, :hidden_width]
    grad_up = grad_gate_up_weight[:, hidden_width:]
    ffn_reduced = (grad_gate, grad_up, grad_down)
    grad_norm_two, grad_gain_two = norm_backward(
        grad_hidden_two, normed_two, scale_two, gain_two, full_width
    )
    grad_middle = cotangent.astype(jnp.float32) + grad_norm_two
    branch_low = grad_middle.astype(jnp.bfloat16)
    middle_all, grad_attended = section_in(branch_low, out_weight, True)
    grad_out = outer_sum(attended_all, middle_all)
    grad_packed = by_sequence + (
        log_totals,
        grad_attended.astype(jnp.bfloat16).reshape(per_column, seq_length, query_width),
    )
    grad_queries, grad_keys, grad_values = lax.map(attention_backward, grad_packed)
    grad_queries = rotate(grad_queries.reshape(local_tokens, -1, HD), -positions).reshape(
        local_tokens, query_width
    )
    grad_keys = rotate(grad_keys.reshape(local_tokens, -1, HD), -positions).reshape(
        local_tokens, pair_width
    )
    grad_projected = jnp.concatenate(
        [grad_queries, grad_keys, grad_values.reshape(local_tokens, pair_width)], 1
    ).astype(jnp.bfloat16)
    projected_all, grad_hidden_one = section_out(grad_projected, qkv_weight, True)
    grad_qkv_weight = outer_sum(hidden_one_all, projected_all)
    grad_query = grad_qkv_weight[:, :query_width]
    grad_key = grad_qkv_weight[:, query_width : query_width + pair_width]
    grad_value = grad_qkv_weight[:, query_width + pair_width :]
    grad_norm_one, grad_gain_one = norm_backward(
        grad_hidden_one, normed_one, scale_one, gain_one, full_width
    )
    grad_inputs = grad_middle + grad_norm_one
    reduced = (
        lax.psum_scatter(
            grad_query.astype(jnp.bfloat16), "dp", scatter_dimension=0, tiled=True
        ).astype(jnp.float32),
        lax.psum_scatter(
            grad_key.astype(jnp.bfloat16), "dp", scatter_dimension=0, tiled=True
        ).astype(jnp.float32),
        lax.psum_scatter(
            grad_value.astype(jnp.bfloat16), "dp", scatter_dimension=0, tiled=True
        ).astype(jnp.float32),
        lax.psum_scatter(
            grad_out.astype(jnp.bfloat16), "dp", scatter_dimension=1, tiled=True
        ).astype(jnp.float32),
        lax.psum_scatter(
            ffn_reduced[0].astype(jnp.bfloat16), "dp", scatter_dimension=0, tiled=True
        ).astype(jnp.float32),
        lax.psum_scatter(
            ffn_reduced[1].astype(jnp.bfloat16), "dp", scatter_dimension=0, tiled=True
        ).astype(jnp.float32),
        lax.psum_scatter(
            ffn_reduced[2].astype(jnp.bfloat16), "dp", scatter_dimension=1, tiled=True
        ).astype(jnp.float32),
    )
    shared = (
        lax.all_gather(reduced[0].astype(jnp.bfloat16), "dp", axis=0, tiled=True).astype(
            jnp.float32
        ),
        lax.all_gather(reduced[1].astype(jnp.bfloat16), "dp", axis=0, tiled=True).astype(
            jnp.float32
        ),
        lax.all_gather(reduced[2].astype(jnp.bfloat16), "dp", axis=0, tiled=True).astype(
            jnp.float32
        ),
        lax.all_gather(reduced[3].astype(jnp.bfloat16), "dp", axis=1, tiled=True).astype(
            jnp.float32
        ),
        lax.all_gather(reduced[4].astype(jnp.bfloat16), "dp", axis=0, tiled=True).astype(
            jnp.float32
        ),
        lax.all_gather(reduced[5].astype(jnp.bfloat16), "dp", axis=0, tiled=True).astype(
            jnp.float32
        ),
        lax.all_gather(reduced[6].astype(jnp.bfloat16), "dp", axis=1, tiled=True).astype(
            jnp.float32
        ),
    )
    gain_grads = lax.psum((grad_gain_one, grad_gain_two), ("dp", "row"))
    return (
        outputs,
        grad_inputs,
        gain_grads[0],
        shared[0],
        shared[1],
        shared[2],
        shared[3],
        gain_grads[1],
        shared[4],
        shared[5],
        shared[6],
    )


def solution(mesh):
    in_specs = (
        P(("dp", "row"), "col"),
        P("dp", None),
        P("col"),
        P("col", "row"),
        P("col", "row"),
        P("col", "row"),
        P("row", "col"),
        P("col"),
        P("col", "row"),
        P("col", "row"),
        P("row", "col"),
        P(("dp", "row"), "col"),
    )
    out_specs = (
        P(("dp", "row"), "col"),
        P(("dp", "row"), "col"),
        P("col"),
        P("col", "row"),
        P("col", "row"),
        P("col", "row"),
        P("row", "col"),
        P("col"),
        P("col", "row"),
        P("col", "row"),
        P("row", "col"),
    )
    return jax.shard_map(body, mesh=mesh, in_specs=in_specs, out_specs=out_specs, check_vma=False)
```

profile of v0, /device:TPU:0, one launch (start us, length us, event | category | flops | bytes accessed | tf_op | source)
XLA Modules:
  0.0 1948.7 jit_solution(7776806837381916122)
XLA Ops:
  18.4 36.0 %all-gather.14.cloned.1.call-done = bf16[2048,1024]{1,0:T(8,128)(2,1)} async-done(((bf16[512,1024]{1,0:T(8,128)(2,1)}), bf16[2048,1024]{1,0:T(8,128)(2,1)}) %all-gather.14.cloned.1.call-update) | async-done | bytes 4194320 | tf_op jit(solution)/shard_map/all_gather | solution.py:65
  72.6 56.0 %reduce-scatter.16.cloned.1.call-done = f32[1024,640]{1,0:T(8,128)} async-done(((f32[2048,640]{1,0:T(8,128)}), f32[1024,640]{1,0:T(8,128)}) %reduce-scatter.16.cloned.1.call-update) | async-done | bytes 2621456 | tf_op jit(solution)/shard_map/reduce_scatter | solution.py:73
  203.3 33.0 %all-gather.16.cloned.1.call-done = bf16[2048,512]{0,1:T(8,128)(2,1)} async-done(((bf16[1024,512]{0,1:T(8,128)(2,1)}), bf16[2048,512]{0,1:T(8,128)(2,1)}) %all-gather.16.cloned.1.call-update) | async-done | bytes 2097168 | tf_op jit(solution)/shard_map/all_gather | solution.py:83
  244.4 71.2 %reduce-scatter.18.cloned.1.call-done = f32[512,1024]{1,0:T(8,128)} async-done(((f32[2048,1024]{1,0:T(8,128)}), f32[512,1024]{1,0:T(8,128)}) %reduce-scatter.18.cloned.1.call-update) | async-done | bytes 2097168 | tf_op jit(solution)/shard_map/reduce_scatter | solution.py:91
  408.3 115.3 %reduce-scatter.24.cloned.1.call-done = f32[1024,1408]{1,0:T(8,128)} async-done(((f32[2048,1408]{1,0:T(8,128)}), f32[1024,1408]{1,0:T(8,128)}) %reduce-scatter.24.cloned.1.call-update) | async-done | bytes 5767184 | tf_op jit(solution)/shard_map/reduce_scatter | solution.py:73
  523.6 259.1 %reduce-scatter.20.cloned.1.call-done = f32[1024,2816]{1,0:T(8,128)} async-done(((f32[2048,2816]{1,0:T(8,128)}), f32[1024,2816]{1,0:T(8,128)}) %reduce-scatter.20.cloned.1.call-update) | async-done | bytes 11534352 | tf_op jit(solution)/shard_map/reduce_scatter | solution.py:73
  794.3 141.1 %all-gather.24.cloned.1.call-done = bf16[2048,2816]{1,0:T(8,128)(2,1)} async-done(((bf16[1024,2816]{1,0:T(8,128)(2,1)}), bf16[2048,2816]{1,0:T(8,128)(2,1)}) %all-gather.24.cloned.1.call-update) | async-done | bytes 11534352 | tf_op jit(solution)/shard_map/all_gather | solution.py:83
  953.5 71.8 %reduce-scatter.26.cloned.1.call-done = f32[512,1024]{1,0:T(8,128)} async-done(((f32[2048,1024]{1,0:T(8,128)}), f32[512,1024]{1,0:T(8,128)}) %reduce-scatter.26.cloned.1.call-update) | async-done | bytes 2097168 | tf_op jit(solution)/shard_map/reduce_scatter | solution.py:91
  1037.8 34.6 %all-gather.26.cloned.1.call-done = bf16[2048,1024]{1,0:T(8,128)(2,1)} async-done(((bf16[512,1024]{1,0:T(8,128)(2,1)}), bf16[2048,1024]{1,0:T(8,128)(2,1)}) %all-gather.26.cloned.1.call-update) | async-done | bytes 4194320 | tf_op jit(solution)/shard_map/all_gather | solution.py:65
  1085.5 48.3 %reduce-scatter.28.cloned.1.call-done = f32[1024,512]{1,0:T(8,128)} async-done(((f32[2048,512]{1,0:T(8,128)}), f32[1024,512]{1,0:T(8,128)}) %reduce-scatter.28.cloned.1.call-update) | async-done | bytes 2097168 | tf_op jit(solution)/shard_map/reduce_scatter | solution.py:73
  1138.7 29.2 %fusion = (f32[8,1024]{1,0:T(8,128)S(1)}, f32[1024,1024,8]{1,0,2:T(8,128)}) fusion(f32[1,8,1024,1024]{2,3,1,0:T(8,128)} %get-tuple-element.124, f32[8,1024]{1,0:T(8,128)S(1)} %log_add_fusion, pred[1024,1024]{0,1:T(8,128)(4,1)} %fusion.12, bf16[1024,8,64]{0,2,1:T(8,128)(2,1)} %bitcast.161, f32[1024,640]{1,0:T(8,128)} %reduce-scatter.16.cloned.1.call-done), kind=kOutput, calls=%fused_computation.3 | convolution fusion | flops 1107288064 | bytes 69533696 | tf_op jit(solution)/shard_map/while/body/eval_jaxpr/qkgd,skd->kgqs/dot_general | solution.py:133
  1167.9 28.6 %fusion.6 = bf16[8,1024,1024]{1,2,0:T(8,128)(2,1)} fusion(f32[1024,1024,8]{1,0,2:T(8,128)} %get-tuple-element.126, f32[1,8,1024,1024]{2,3,1,0:T(8,128)} %get-tuple-element.124, f32[8,1024]{1,0:T(8,128)S(1)} %get-tuple-element.125, f32[8,1024]{1,0:T(8,128)S(1)} %log_add_fusion, pred[1024,1024]{0,1:T(8,128)(4,1)} %fusion.12), kind=kLoop, calls=%fused_computation.12 | loop fusion | flops 41943040 | bytes 85000192 | tf_op jit(solution)/shard_map/reshape.78
  1282.9 50.9 %reduce-scatter.44.cloned.1.call-done = bf16[1408,256]{1,0:T(8,128)(2,1)} async-done(((bf16[1408,1024]{1,0:T(8,128)(2,1)}), bf16[1408,256]{1,0:T(8,128)(2,1)}) %reduce-scatter.44.cloned.1.call-update) | async-done | bytes 720912 | tf_op jit(solution)/shard_map/reduce_scatter | solution.py:281
  1333.8 58.7 %reduce-scatter.40.cloned.1.call-done = bf16[256,1408]{1,0:T(8,128)(2,1)} async-done(((bf16[1024,1408]{1,0:T(8,128)(2,1)}), bf16[256,1408]{1,0:T(8,128)(2,1)}) %reduce-scatter.40.cloned.1.call-update) | async-done | bytes 720912 | tf_op jit(solution)/shard_map/reduce_scatter | solution.py:275
  1392.6 58.7 %reduce-scatter.42.cloned.1.call-done = bf16[256,1408]{1,0:T(8,128)(2,1)} async-done(((bf16[1024,1408]{1,0:T(8,128)(2,1)}), bf16[256,1408]{1,0:T(8,128)(2,1)}) %reduce-scatter.42.cloned.1.call-update) | async-done | bytes 720912 | tf_op jit(solution)/shard_map/reduce_scatter | solution.py:278
  1451.4 29.7 %reduce-scatter.38.cloned.1.call-done = bf16[512,256]{1,0:T(8,128)(2,1)} async-done(((bf16[512,1024]{1,0:T(8,128)(2,1)}), bf16[512,256]{1,0:T(8,128)(2,1)}) %reduce-scatter.38.cloned.1.call-update) | async-done | bytes 262160 | tf_op jit(solution)/shard_map/reduce_scatter | solution.py:272
  1483.7 26.2 %reduce-scatter.32.cloned.1.call-done = bf16[256,512]{0,1:T(8,128)(2,1)} async-done(((bf16[1024,512]{0,1:T(8,128)(2,1)}), bf16[256,512]{0,1:T(8,128)(2,1)}) %reduce-scatter.32.cloned.1.call-update) | async-done | bytes 262160 | tf_op jit(solution)/shard_map/reduce_scatter | solution.py:263
  1529.6 39.5 %all-gather.38.cloned.1.call-done = bf16[1408,1024]{1,0:T(8,128)(2,1)} async-done(((bf16[1408,256]{1,0:T(8,128)(2,1)}), bf16[1408,1024]{1,0:T(8,128)(2,1)}) %all-gather.38.cloned.1.call-update) | async-done | bytes 2883600 | tf_op jit(solution)/shard_map/all_gather | solution.py:304
  1574.2 53.9 %all-gather.34.cloned.1.call-done = bf16[1024,1408]{1,0:T(8,128)(2,1)} async-done(((bf16[256,1408]{1,0:T(8,128)(2,1)}), bf16[1024,1408]{1,0:T(8,128)(2,1)}) %all-gather.34.cloned.1.call-update) | async-done | bytes 2883600 | tf_op jit(solution)/shard_map/all_gather | solution.py:298
  1632.8 54.7 %all-gather.36.cloned.1.call-done = bf16[1024,1408]{1,0:T(8,128)(2,1)} async-done(((bf16[256,1408]{1,0:T(8,128)(2,1)}), bf16[1024,1408]{1,0:T(8,128)(2,1)}) %all-gather.36.cloned.1.call-update) | async-done | bytes 2883600 | tf_op jit(solution)/shard_map/all_gather | solution.py:301
  1692.3 25.8 %all-gather.32.cloned.1.call-done = bf16[512,1024]{1,0:T(8,128)(2,1)} async-done(((bf16[512,256]{1,0:T(8,128)(2,1)}), bf16[512,1024]{1,0:T(8,128)(2,1)}) %all-gather.32.cloned.1.call-update) | async-done | bytes 1048592 | tf_op jit(solution)/shard_map/all_gather | solution.py:295
  1792.0 68.7 %reduce-scatter.30.cloned.1.call-done = f32[512,1024]{1,0:T(8,128)} async-done(((f32[2048,1024]{1,0:T(8,128)}), f32[512,1024]{1,0:T(8,128)}) %reduce-scatter.30.cloned.1.call-update) | async-done | bytes 2097168 | tf_op jit(solution)/shard_map/reduce_scatter | solution.py:91
  1868.2 32.5 %all-reduce = (f32[1024]{0:T(1024)}, f32[1024]{0:T(1024)}) all-reduce(f32[1024]{0:T(1024)S(1)} %get-tuple-element.86, f32[1024]{0:T(1024)S(1)} %copy-done.27), channel_id=1, replica_groups=mesh['dp'=4,'row'=4,'col'=2] {'dp','row'}, use_global_device_ids=true, to_apply=%region_22.23 | all-reduce | flops 2048 | bytes 16384 | tf_op jit(solution)/shard_map/psum | solution.py:308
  1900.7 35.0 %reduce-scatter.22.cloned.1.call-done = f32[512,1024]{1,0:T(8,128)} async-done(((f32[2048,1024]{1,0:T(8,128)}), f32[512,1024]{1,0:T(8,128)}) %reduce-scatter.22.cloned.1.call-update) | async-done | bytes 2097168 | tf_op jit(solution)/shard_map/reduce_scatter | solution.py:91
  (214 shorter events, 474.9 us)
Async XLA Ops:
  18.0 110.6 %reduce-scatter.16.cloned.1.call-start = ((), (), s32[]{:S(2)}) async-start(), calls=%async_computation.16 | async-start | bytes 7864320 | tf_op jit(solution)/shard_map/reduce_scatter | solution.py:73
  62.8 173.5 %all-gather.16.cloned.1.call-start = ((), (), s32[]{:S(2)}) async-start(), calls=%async_computation.17 | async-start | bytes 3145728 | tf_op jit(solution)/shard_map/all_gather | solution.py:83
  203.0 112.7 %reduce-scatter.18.cloned.1.call-start = ((), (), s32[]{:S(2)}) async-start(), calls=%async_computation.18 | async-start | bytes 10485760 | tf_op jit(solution)/shard_map/reduce_scatter | solution.py:91
  244.3 143.7 %all-gather.18.cloned.1.call-start = ((), (), s32[]{:S(2)}) async-start(), calls=%async_computation.19 | async-start | bytes 5242880 | tf_op jit(solution)/shard_map/all_gather | solution.py:65
  327.0 196.5 %reduce-scatter.24.cloned.1.call-start = ((), (), s32[]{:S(2)}) async-start(), calls=%async_computation.24 | async-start | bytes 17301504 | tf_op jit(solution)/shard_map/reduce_scatter | solution.py:73
  362.7 420.0 %reduce-scatter.20.cloned.1.call-start = ((), (), s32[]{:S(2)}) async-start(), calls=%async_computation.20 | async-start | bytes 34603008 | tf_op jit(solution)/shard_map/reduce_scatter | solution.py:73
  407.8 527.7 %all-gather.24.cloned.1.call-start = ((), (), s32[]{:S(2)}) async-start(), calls=%async_computation.25 | async-start | bytes 17301504 | tf_op jit(solution)/shard_map/all_gather | solution.py:83
  794.2 231.1 %reduce-scatter.26.cloned.1.call-start = ((), (), s32[]{:S(2)}) async-start(), calls=%async_computation.26 | async-start | bytes 10485760 | tf_op jit(solution)/shard_map/reduce_scatter | solution.py:91
  953.4 119.0 %all-gather.26.cloned.1.call-start = ((), (), s32[]{:S(2)}) async-start(), calls=%async_computation.27 | async-start | bytes 5242880 | tf_op jit(solution)/shard_map/all_gather | solution.py:65
  1079.3 156.4 %all-gather.20.cloned.1.call-start = ((), (), s32[]{:S(2)}) async-start(), calls=%async_computation.21 | async-start | bytes 8650752 | tf_op jit(solution)/shard_map/all_gather | solution.py:83
  1085.3 189.6 %all-gather.28.cloned.1.call-start = ((), (), s32[]{:S(2)}) async-start(), calls=%async_computation.29 | async-start | bytes 3932160 | tf_op jit(solution)/shard_map/all_gather | solution.py:83
  1246.6 146.0 %reduce-scatter.40.cloned.1.call-start = ((), (), s32[]{:S(2)}) async-start(), calls=%async_computation.37 | async-start | bytes 3604480 | tf_op jit(solution)/shard_map/reduce_scatter | solution.py:275
  1267.0 184.4 %reduce-scatter.42.cloned.1.call-start = ((), (), s32[]{:S(2)}) async-start(), calls=%async_computation.39 | async-start | bytes 3604480 | tf_op jit(solution)/shard_map/reduce_scatter | solution.py:278
  1267.6 213.5 %reduce-scatter.38.cloned.1.call-start = ((), (), s32[]{:S(2)}) async-start(), calls=%async_computation.35 | async-start | bytes 1310720 | tf_op jit(solution)/shard_map/reduce_scatter | solution.py:272
  1273.8 236.1 %reduce-scatter.32.cloned.1.call-start = ((), (), s32[]{:S(2)}) async-start(), calls=%async_computation.31 | async-start | bytes 1310720 | tf_op jit(solution)/shard_map/reduce_scatter | solution.py:263
  1282.8 286.3 %all-gather.38.cloned.1.call-start = ((), (), s32[]{:S(2)}) async-start(), calls=%async_computation.42 | async-start | bytes 3604480 | tf_op jit(solution)/shard_map/all_gather | solution.py:304
  1333.8 294.3 %all-gather.34.cloned.1.call-start = ((), (), s32[]{:S(2)}) async-start(), calls=%async_computation.38 | async-start | bytes 3604480 | tf_op jit(solution)/shard_map/all_gather | solution.py:298
  1392.6 295.0 %all-gather.36.cloned.1.call-start = ((), (), s32[]{:S(2)}) async-start(), calls=%async_computation.40 | async-start | bytes 3604480 | tf_op jit(solution)/shard_map/all_gather | solution.py:301
  1451.4 266.7 %all-gather.32.cloned.1.call-start = ((), (), s32[]{:S(2)}) async-start(), calls=%async_computation.36 | async-start | bytes 1310720 | tf_op jit(solution)/shard_map/all_gather | solution.py:295
  1481.1 257.0 %reduce-scatter.36.cloned.1.call-start = ((), (), s32[]{:S(2)}) async-start(), calls=%async_computation.34 | async-start | bytes 163840 | tf_op jit(solution)/shard_map/reduce_scatter | solution.py:269
  1482.9 275.6 %reduce-scatter.34.cloned.1.call-start = ((), (), s32[]{:S(2)}) async-start(), calls=%async_computation.33 | async-start | bytes 163840 | tf_op jit(solution)/shard_map/reduce_scatter | solution.py:266
  1483.7 305.8 %all-gather.30.cloned.1.call-start = ((), (), s32[]{:S(2)}) async-start(), calls=%async_computation.32 | async-start | bytes 1310720 | tf_op jit(solution)/shard_map/all_gather | solution.py:286
  1509.9 350.8 %reduce-scatter.30.cloned.1.call-start = ((), (), s32[]{:S(2)}) async-start(), calls=%async_computation.30 | async-start | bytes 10485760 | tf_op jit(solution)/shard_map/reduce_scatter | solution.py:91
  1518.9 416.8 %reduce-scatter.22.cloned.1.call-start = ((), (), s32[]{:S(2)}) async-start(), calls=%async_computation.22 | async-start | bytes 10485760 | tf_op jit(solution)/shard_map/reduce_scatter | solution.py:91
  (34 other events, 3680.8 us)
Sparse Core Ops, SparseCore 0:
  18.1 36.2 all-gather.13
  62.9 65.6 reduce-scatter.15
  203.1 33.1 all-gather.15
  243.9 71.7 reduce-scatter.17
  317.1 34.4 all-gather.21
  353.6 34.4 all-gather.17
  390.4 133.1 reduce-scatter.23
  525.9 256.7 reduce-scatter.19
  794.4 141.0 all-gather.23
  953.6 71.7 reduce-scatter.25
  1037.9 34.4 all-gather.25
  1079.5 54.2 reduce-scatter.27
  1135.9 74.4 all-gather.19
  1235.8 38.9 all-gather.27
  1277.5 56.1 reduce-scatter.43
  1336.5 56.0 reduce-scatter.39
  1395.3 56.0 reduce-scatter.41
  1511.3 57.7 all-gather.37
  1570.7 57.3 all-gather.33
  1629.7 57.8 all-gather.35
  1689.2 28.8 all-gather.31
  1760.0 29.4 all-gather.29
  1791.9 68.8 reduce-scatter.29
  1863.5 72.1 reduce-scatter.21
  (4 shorter events, 87.4 us)
where the time goes:
time: 1950 us
  waiting for transfers between devices  1450 us (74%)
  matrix products  221 us (11%)
  other arithmetic  128 us (7%)
  blocking collectives  81 us (4%)
  local copies, waits for them, and re-layouts  45.9 us (2%)
    reduce_scatter x4, waiting for transfers between devices, section_in(): lax.psum_scatter(partial_rows(jnp.int32(0), lax.axis_size('col') * portio...  479 us
    reduce_scatter x4, waiting for transfers between devices, section_out(): lax.psum_scatter(partial_rows(jnp.int32(0), lax.axis_size('row') * portio...  247 us
    all_gather x4, waiting for transfers between devices, section_out(): gathered = lax.all_gather(local_rows, 'col', axis=0, tiled=True)  175 us
    all_gather x4, waiting for transfers between devices, section_in(): gathered = lax.all_gather(local_rows, 'row', axis=0, tiled=True)  115 us
    reduce_scatter x1, waiting for transfers between devices, body(): lax.psum_scatter(ffn_reduced[0].astype(jnp.bfloat16), 'dp', scatter_dimen...  58.7 us
    reduce_scatter x1, waiting for transfers between devices, body(): lax.psum_scatter(ffn_reduced[1].astype(jnp.bfloat16), 'dp', scatter_dimen...  58.7 us
    all_gather x1, waiting for transfers between devices, body(): lax.all_gather(reduced[5].astype(jnp.bfloat16), 'dp', axis=0, tiled=True)  54.7 us
    all_gather x1, waiting for transfers between devices, body(): lax.all_gather(reduced[4].astype(jnp.bfloat16), 'dp', axis=0, tiled=True)  53.9 us
  transfers between devices with their start and end apart: 28, of which 27 were waited for; matrix products, arithmetic and copies ran while one was open for 13% of the time, Pallas kernels for 0%

commit v1 on v0

v1 whole, which is shorter than its diff:
```python
import jax
import jax.numpy as jnp
from jax import lax
from jax.sharding import PartitionSpec as P

HD = 64
LANES = 128

epsilon = 1e-05
rope_base = 10000.0
BF = jnp.bfloat16
F32 = jnp.float32


def positions_of(segment_row):
    indices = jnp.arange(segment_row.shape[0], dtype=jnp.int32)
    previous = jnp.concatenate([segment_row[:1] - 1, segment_row[:-1]])
    start_index = lax.cummax(jnp.where(segment_row != previous, indices, 0), axis=0)
    return indices - start_index


def rotary_tables(positions):
    half_width = HD // 2
    frequency = rope_base ** (-jnp.arange(half_width).astype(F32) * 2.0 / HD)
    angles = positions.astype(F32)[..., None] * frequency
    cosine = jnp.concatenate([jnp.cos(angles), jnp.cos(angles)], -1)
    sine = jnp.concatenate([jnp.sin(angles), jnp.sin(angles)], -1)
    return cosine, sine


def rotate(vectors, cosine, sine):
    half_width = HD // 2
    turned = jnp.concatenate([-vectors[..., half_width:], vectors[..., :half_width]], -1)
    return vectors * cosine[:, None, :] + turned * sine[:, None, :]


def swap(values, axis, bit):
    pairs = [(i, i ^ bit) for i in range(lax.axis_size(axis))]
    return lax.ppermute(values, axis, pairs)


def swap_sum(values):
    return values + swap(values, "col", 1)


def pick(values, index, axis):
    return lax.dynamic_index_in_dim(values, index, axis, keepdims=False)


def pair_up(own, other, first, axis):
    return jnp.concatenate([jnp.where(first, own, other), jnp.where(first, other, own)], axis)


def gather_row(block):
    size = lax.axis_size("row")
    blocks = {0: block}
    bit = size // 2
    while bit:
        for offset in list(blocks):
            blocks[offset | bit] = swap(blocks[offset], "row", bit)
        bit //= 2
    me = lax.axis_index("row")
    whole = jnp.zeros((size * block.shape[0],) + block.shape[1:], block.dtype)
    for offset, part in blocks.items():
        whole = lax.dynamic_update_slice_in_dim(whole, part, (me ^ offset) * block.shape[0], 0)
    return whole


def scatter_row(partial):
    size = lax.axis_size("row")
    me = lax.axis_index("row")
    current = partial
    while size > 1:
        block = partial.shape[0] // lax.axis_size("row")
        current = current.reshape(size // 2, 2, block, partial.shape[1])
        kept = pick(current, me & 1, 1).astype(F32)
        sent = pick(current, 1 - (me & 1), 1).astype(BF)
        bit = lax.axis_size("row") // size
        current = kept + swap(sent, "row", bit).astype(F32)
        me = me >> 1
        size //= 2
    return current.reshape(partial.shape[0] // lax.axis_size("row"), partial.shape[1])


def gather_plane(block):
    half = block.shape[0] // 2
    across = swap(block, "col", 1)
    along = swap(block, "row", 2)
    corner = jnp.concatenate([swap(along[:half], "col", 1), swap(across[half:], "row", 2)], 0)
    near = jnp.concatenate([block, across], 1)
    far = jnp.concatenate([along, corner], 1)
    near_sibling = jnp.concatenate([swap(block, "row", 1), swap(across, "row", 1)], 1)
    far_sibling = jnp.concatenate([swap(along, "row", 1), swap(corner, "row", 1)], 1)
    return jnp.concatenate([near, near_sibling, far, far_sibling], 0)


def scatter_plane(partial):
    rows = partial.shape[0] // 4
    width = partial.shape[1] // 2
    half = rows // 2
    blocks = partial.reshape(2, 2, rows, 2 * width)
    summed = blocks[:, 0].astype(F32) + swap(blocks[:, 1].astype(BF), "row", 1).astype(F32)
    first = summed[:, :half]
    second = summed[:, half:]
    first_sum = first[:, :, :width] + swap(first[:, :, width:].astype(BF), "col", 1).astype(F32)
    first_sum = first_sum[0] + swap(first_sum[1].astype(BF), "row", 2).astype(F32)
    second_sum = second[0] + swap(second[1].astype(BF), "row", 2).astype(F32)
    second_sum = second_sum[:, :width] + swap(second_sum[:, width:].astype(BF), "col", 1).astype(F32)
    return jnp.concatenate([first_sum, second_sum], 0)


def sum_dp(values):
    size = lax.axis_size("dp")
    if size != 4:
        mine = lax.psum_scatter(values, "dp", scatter_dimension=0, tiled=True)
        return lax.all_gather(mine, "dp", axis=0, tiled=True)
    place = lax.axis_index("dp")
    inward = lax.ppermute(values, "dp", [(0, 1), (3, 2)])
    half_sum = (values.astype(F32) + inward.astype(F32)).astype(BF)
    crossed = lax.ppermute(half_sum, "dp", [(1, 2), (2, 1)])
    total = (half_sum.astype(F32) + crossed.astype(F32)).astype(BF)
    outward = lax.ppermute(total, "dp", [(1, 0), (2, 3)])
    return jnp.where((place == 0) | (place == 3), outward, total)


def norm_forward(values, gain, full_width):
    squares = swap_sum(jnp.sum(values * values, -1, keepdims=True))
    scale = lax.rsqrt(squares / full_width + epsilon)
    normed = values * scale
    return (normed, scale, (normed * gain).astype(BF))


def norm_backward(grad_hidden, normed, scale, gain, full_width):
    grad_normed = grad_hidden * gain
    inner_sum = swap_sum(jnp.sum(grad_normed * normed, -1, keepdims=True))
    return (
        scale * (grad_normed - normed * inner_sum / full_width),
        jnp.sum(grad_hidden * normed, 0),
    )


def contract(leading, weight, kind=F32):
    return jnp.dot(leading, weight, preferred_element_type=F32).astype(kind)


def contract_flipped(leading, weight, kind=F32):
    return lax.dot_general(
        leading, weight, (((1,), (1,)), ((), ())), preferred_element_type=F32
    ).astype(kind)


def outer_sum(leading, trailing):
    return lax.dot_general(
        leading, trailing, (((0,), (0,)), ((), ())), preferred_element_type=F32
    ).astype(BF)


def score_block(queries, key_rows, segment_row):
    length = queries.shape[0]
    pair_heads = key_rows.shape[1] // HD
    grouped = queries.reshape(length, pair_heads, -1, HD)
    keyed = key_rows.reshape(length, pair_heads, HD)
    scores = jnp.einsum("qkgd,skd->kgqs", grouped, keyed, preferred_element_type=F32) * HD ** (-0.5)
    indices = jnp.arange(length, dtype=jnp.int32)
    allowed = (segment_row[:, None] == segment_row[None, :]) & (
        indices[:, None] >= indices[None, :]
    )
    return (grouped, keyed, jnp.where(allowed, scores, -1e30), allowed)


def attention_forward(packed):
    queries, key_rows, value_rows, segment_row = packed
    grouped, keyed, scores, allowed = score_block(queries, key_rows, segment_row)
    highest_score = jnp.max(scores, -1, keepdims=True)
    weights = jnp.exp(scores - highest_score)
    totals = jnp.sum(weights, -1, keepdims=True)
    weights_low = (weights / totals).astype(BF)
    valued = value_rows.reshape(keyed.shape)
    mixture = jnp.einsum("kgqs,skd->qkgd", weights_low, valued, preferred_element_type=F32)
    return (mixture.reshape(queries.shape).astype(BF), highest_score + jnp.log(totals))


def attention_backward(packed):
    queries, key_rows, value_rows, segment_row, log_total, grad_mixture = packed
    grouped, keyed, scores, allowed = score_block(queries, key_rows, segment_row)
    weights = jnp.where(allowed, jnp.exp(scores - log_total), 0.0)
    valued = value_rows.reshape(keyed.shape)
    grad_grouped = grad_mixture.reshape(grouped.shape)
    grad_weights = jnp.einsum("qkgd,skd->kgqs", grad_grouped, valued, preferred_element_type=F32)
    row_inner = jnp.sum(weights * grad_weights, -1, keepdims=True)
    grad_scores = (weights * (grad_weights - row_inner)).astype(BF)
    scale_factor = HD ** (-0.5)
    grad_queries = (
        jnp.einsum("kgqs,skd->qkgd", grad_scores, keyed, preferred_element_type=F32) * scale_factor
    )
    grad_keys = (
        jnp.einsum("kgqs,qkgd->skd", grad_scores, grouped, preferred_element_type=F32)
        * scale_factor
    )
    grad_values = jnp.einsum(
        "kgqs,qkgd->skd", weights.astype(BF), grad_grouped, preferred_element_type=F32
    )
    return (grad_queries.reshape(queries.shape[0], -1, HD), grad_keys, grad_values)


def body(
    inputs,
    segments,
    norm1_gain,
    query_weight,
    key_weight,
    value_weight,
    out_weight,
    norm2_gain,
    gate_weight,
    up_weight,
    down_weight,
    cotangent,
):
    columns = lax.axis_size("col")
    full_width = norm1_gain.shape[0] * columns
    width = norm1_gain.shape[0]
    query_width = query_weight.shape[1]
    pair_width = key_weight.shape[1]
    hidden_width = gate_weight.shape[1]
    per_column = segments.shape[0] // columns
    seq_length = segments.shape[1]
    column = lax.axis_index("col")
    first_column = column == 0

    part = -(-(hidden_width // 2) // LANES) * LANES
    overlap = 2 * part - hidden_width

    def cut(weight, axis):
        low = lax.slice_in_dim(weight, 0, part, axis=axis)
        high = lax.slice_in_dim(weight, hidden_width - part, hidden_width, axis=axis)
        inside = lax.broadcasted_iota(jnp.int32, high.shape, axis) >= overlap
        high = jnp.where(inside, high, jnp.zeros_like(high))
        kept = jnp.where(first_column, low, high)
        sent = jnp.where(first_column, high, low)
        return jnp.concatenate([kept, swap(sent, "col", 1)], 1 - axis)

    def uncut(grad, axis):
        own = lax.slice_in_dim(grad, 0, width, axis=1 - axis)
        other = swap(lax.slice_in_dim(grad, width, 2 * width, axis=1 - axis), "col", 1)
        low = jnp.where(first_column, own, other)
        high = lax.slice_in_dim(jnp.where(first_column, other, own), overlap, part, axis=axis)
        return jnp.concatenate([sum_dp(low), sum_dp(high)], axis).astype(F32)

    features = inputs.astype(F32)
    gain_one = norm1_gain.astype(F32)
    gain_two = norm2_gain.astype(F32)
    normed_one, scale_one, hidden_one = norm_forward(features, gain_one, full_width)
    hidden_one_all = gather_row(hidden_one)

    gate_full = cut(gate_weight, 1)
    up_full = cut(up_weight, 1)
    down_full = cut(down_weight, 0)
    cotangent_all = gather_plane(cotangent)

    qkv_weight = jnp.concatenate([query_weight, key_weight, value_weight], 1)
    local_segments = lax.dynamic_slice_in_dim(segments, column * per_column, per_column, 0)
    positions = jax.vmap(positions_of)(local_segments).reshape(-1)
    local_tokens = positions.shape[0]
    cosine, sine = rotary_tables(positions)

    def scatter_col(partial):
        split = partial.reshape(columns, local_tokens, partial.shape[1])
        return pick(split, column, 0) + swap(pick(split, 1 - column, 0).astype(BF), "col", 1).astype(F32)

    def gather_col(block):
        return pair_up(block, swap(block, "col", 1), first_column, 0)

    projected = scatter_col(contract(hidden_one_all, qkv_weight))
    queries = (
        rotate(projected[:, :query_width].reshape(local_tokens, -1, HD), cosine, sine)
        .reshape(local_tokens, query_width)
        .astype(BF)
    )
    key_rows = (
        rotate(
            projected[:, query_width : query_width + pair_width].reshape(local_tokens, -1, HD),
            cosine,
            sine,
        )
        .reshape(local_tokens, pair_width)
        .astype(BF)
    )
    value_rows = projected[:, query_width + pair_width :].astype(BF)
    by_sequence = (
        queries.reshape(per_column, seq_length, query_width),
        key_rows.reshape(per_column, seq_length, pair_width),
        value_rows.reshape(per_column, seq_length, pair_width),
        local_segments,
    )
    attended, log_totals = lax.map(attention_forward, by_sequence)
    attended_all = gather_col(attended.reshape(local_tokens, query_width))
    attn_branch = scatter_row(contract(attended_all, out_weight, BF))
    middle = features + attn_branch
    normed_two, scale_two, hidden_two = norm_forward(middle, gain_two, full_width)
    hidden_two_all = gather_plane(hidden_two)
    gate_part = contract(hidden_two_all, gate_full)
    up_part = contract(hidden_two_all, up_full)
    sigmoid_gate = jax.nn.sigmoid(gate_part)
    activated = (gate_part * sigmoid_gate * up_part).astype(BF)
    grad_activated = contract_flipped(cotangent_all, down_full)
    grad_gate_part = (
        grad_activated * up_part * sigmoid_gate * (1.0 + gate_part * (1.0 - sigmoid_gate))
    ).astype(BF)
    grad_up_part = (grad_activated * gate_part * sigmoid_gate).astype(BF)
    grad_hidden_two = scatter_plane(
        (
            contract_flipped(grad_gate_part, gate_full) + contract_flipped(grad_up_part, up_full)
        ).astype(BF)
    )
    outputs = (middle + scatter_plane(contract(activated, down_full, BF))).astype(BF)
    grad_down = uncut(outer_sum(activated, cotangent_all), 0)
    grad_gate = uncut(outer_sum(hidden_two_all, grad_gate_part), 1)
    grad_up = uncut(outer_sum(hidden_two_all, grad_up_part), 1)

    grad_norm_two, grad_gain_two = norm_backward(
        grad_hidden_two, normed_two, scale_two, gain_two, full_width
    )
    grad_middle = cotangent.astype(F32) + grad_norm_two
    branch_all = gather_row(grad_middle.astype(BF))
    grad_attended = scatter_col(contract_flipped(branch_all, out_weight)).astype(BF)
    grad_out = sum_dp(outer_sum(attended_all, branch_all)).astype(F32)
    grad_packed = by_sequence + (
        log_totals,
        grad_attended.reshape(per_column, seq_length, query_width),
    )
    grad_queries, grad_keys, grad_values = lax.map(attention_backward, grad_packed)
    grad_queries = rotate(grad_queries.reshape(local_tokens, -1, HD), cosine, -sine).reshape(
        local_tokens, query_width
    )
    grad_keys = rotate(grad_keys.reshape(local_tokens, -1, HD), cosine, -sine).reshape(
        local_tokens, pair_width
    )
    grad_projected = jnp.concatenate(
        [grad_queries, grad_keys, grad_values.reshape(local_tokens, pair_width)], 1
    ).astype(BF)
    projected_all = gather_col(grad_projected)
    grad_hidden_one = scatter_row(contract_flipped(projected_all, qkv_weight, BF))
    grad_qkv = sum_dp(outer_sum(hidden_one_all, projected_all)).astype(F32)
    grad_norm_one, grad_gain_one = norm_backward(
        grad_hidden_one, normed_one, scale_one, gain_one, full_width
    )
    grad_inputs = grad_middle + grad_norm_one
    gain_grads = lax.psum((grad_gain_one, grad_gain_two), ("dp", "row"))
    return (
        outputs,
        grad_inputs,
        gain_grads[0],
        grad_qkv[:, :query_width],
        grad_qkv[:, query_width : query_width + pair_width],
        grad_qkv[:, query_width + pair_width :],
        grad_out,
        gain_grads[1],
        grad_gate,
        grad_up,
        grad_down,
    )


def solution(mesh):
    in_specs = (
        P(("dp", "row"), "col"),
        P("dp", None),
        P("col"),
        P("col", "row"),
        P("col", "row"),
        P("col", "row"),
        P("row", "col"),
        P("col"),
        P("col", "row"),
        P("col", "row"),
        P("row", "col"),
        P(("dp", "row"), "col"),
    )
    out_specs = (
        P(("dp", "row"), "col"),
        P(("dp", "row"), "col"),
        P("col"),
        P("col", "row"),
        P("col", "row"),
        P("col", "row"),
        P("row", "col"),
        P("col"),
        P("col", "row"),
        P("col", "row"),
        P("row", "col"),
    )
    return jax.shard_map(body, mesh=mesh, in_specs=in_specs, out_specs=out_specs, check_vma=False)
```

time: 1950 us -> 1110 us (0.57)
  waiting for transfers between devices: 1450 us -> 464 us
  starting transfers between devices: 2.49 us -> 114 us
  local copies, waits for them, and re-layouts: 45.9 us -> 95.1 us
  other arithmetic: 128 us -> 169 us
  blocking collectives: 81 us -> 42 us
    reduce_scatter x15 -> x0, waiting for transfers between devices: 973 us -> none  [the longest x4 479 us: section_in(): lax.psum_scatter(partial_rows(jnp.int32(0), lax.axis_size('col') * portio...]
    all_gather x13 -> x0, waiting for transfers between devices: 480 us -> none  [the longest x4 175 us: section_out(): gathered = lax.all_gather(local_rows, 'col', axis=0, tiled=True)]
    ppermute x0 -> x74, waiting for transfers between devices: none -> 464 us  [the longest x50 290 us: swap(): return lax.ppermute(values, axis, pairs)]
    ppermute x0 -> x74, starting transfers between devices: none -> 114 us  [the longest x50 48.5 us: swap(): return lax.ppermute(values, axis, pairs)]
    unnamed x64 -> x202, local copies, waits for them, and re-layouts: 10.1 us -> 49.4 us
    all_gather x2 -> x0, blocking collectives: 27.9 us -> none  [the longest x1 14 us: body(): lax.all_gather(reduced[1].astype(jnp.bfloat16), 'dp', axis=0, tiled=True)]
    select_n x0 -> x16, other arithmetic: none -> 26 us  [the longest x6 9.24 us: sum_dp(): return jnp.where((place == 0) | (place == 3), outward, total)]
    psum x4 -> x0, blocking collectives: 20.6 us -> none  [width_sum(): return lax.psum(partial_sums, 'col')]
  transfers between devices with their start and end apart: 28 -> 74, of which waited for: 27 -> 27; matrix products, arithmetic and copies ran while one was open for 13% -> 31% of each run, Pallas kernels for 0% -> 0%
where the time goes in v1:
time: 1110 us; the launch traced here: 1100 us
  waiting for transfers between devices  464 us (42%)
  matrix products  214 us (19%)
  other arithmetic  169 us (15%)
  starting transfers between devices  114 us (10%)
  local copies, waits for them, and re-layouts  95.1 us (9%)
  blocking collectives  42 us (4%)
    ppermute x50, waiting for transfers between devices, swap(): return lax.ppermute(values, axis, pairs)  290 us
    ppermute x8, waiting for transfers between devices, sum_dp(): outward = lax.ppermute(total, 'dp', [(1, 0), (2, 3)])  122 us
    dot_general x5, matrix products, contract_flipped(): lax.dot_general(leading, weight, (((1,), (1,)), ((), ())), preferred_elem...  53.9 us
    ppermute x8, waiting for transfers between devices, sum_dp(): inward = lax.ppermute(values, 'dp', [(0, 1), (3, 2)])  51.6 us
    unnamed x202, local copies, waits for them, and re-layouts  49.4 us
    ppermute x50, starting transfers between devices, swap(): return lax.ppermute(values, axis, pairs)  48.5 us
    ppermute x8, starting transfers between devices, sum_dp(): inward = lax.ppermute(values, 'dp', [(0, 1), (3, 2)])  46.5 us
    dot_general x5, matrix products, outer_sum(): lax.dot_general(leading, trailing, (((0,), (0,)), ((), ())), preferred_el...  42.7 us
  transfers between devices with their start and end apart: 74, of which 27 were waited for; matrix products, arithmetic and copies ran while one was open for 31% of the time, Pallas kernels for 0%

profile of v1, /device:TPU:0, one launch (start us, length us, event | category | flops | bytes accessed | tf_op | source)
XLA Modules:
  0.0 1100.6 jit_solution(2615677805921110259)
XLA Ops:
  13.1 22.2 %collective-permute-done.1 = bf16[512,1024]{1,0:T(8,128)(2,1)S(1)} collective-permute-done((bf16[512,1024]{1,0:T(8,128)(2,1)}, bf16[512,1024]{1,0:T(8,128)(2,1)S(1)}, u32[]{:S(2)}, u32[]{:S(2)}) %collective-permute-start.1) | collective-permute-done | bytes 1048608 | tf_op jit(solution)/shard_map/ppermute | solution.py:39
  65.0 20.5 %collective-permute-done.4 = bf16[1024,640]{0,1:T(8,128)(2,1)} collective-permute-done((bf16[1024,640]{0,1:T(8,128)(2,1)}, bf16[1024,640]{0,1:T(8,128)(2,1)}, u32[]{:S(2)}, u32[]{:S(2)}) %collective-permute-start.4) | collective-permute-done | bytes 1310752 | tf_op jit(solution)/shard_map/ppermute | solution.py:39
  90.5 13.6 %fusion.93 = (f32[8,1024]{1,0:T(8,128)S(1)}, f32[1,8,1024,1024]{2,3,1,0:T(8,128)}) fusion(bf16[1024,64,1]{0,1,2:T(8,128)(2,1)S(1)} %get-tuple-element.138, bf16[1024,8,64]{0,2,1:T(8,128)(2,1)S(1)} %bitcast.248, pred[1024,1024]{0,1:T(8,128)(4,1)S(1)} %fusion.12), kind=kOutput, calls=%fused_computation.244 | convolution fusion | flops 1098899456 | bytes 35815424 | tf_op jit(solution)/shard_map/while/body/eval_jaxpr/qkgd,skd->kgqs/dot_general | solution.py:163
  117.2 13.9 %fusion.39 = bf16[64,8,1024]{2,0,1:T(8,128)(2,1)S(1)} fusion(f32[8,1024]{1,0:T(8,128)S(1)} %fusion.3, f32[1,8,1024,1024]{2,3,1,0:T(8,128)} %get-tuple-element.147, f32[8,1024]{1,0:T(8,128)S(1)} %get-tuple-element.146, f32[1024,640]{0,1:T(8,128)S(1)} %bitcast_add_fusion), kind=kOutput, calls=%fused_computation.134 | convolution fusion | flops 1099431936 | bytes 34799616 | tf_op jit(solution)/shard_map/while/body/eval_jaxpr/kgqs,skd->qkgd/dot_general | solution.py:179
  132.9 23.2 %collective-permute-done.5 = bf16[1024,512]{0,1:T(8,128)(2,1)} collective-permute-done((bf16[1024,512]{0,1:T(8,128)(2,1)S(1)}, bf16[1024,512]{0,1:T(8,128)(2,1)}, u32[]{:S(2)}, u32[]{:S(2)}) %collective-permute-start.5) | collective-permute-done | bytes 1048608 | tf_op jit(solution)/shard_map/ppermute | solution.py:39
  175.0 23.6 %collective-permute-done.7 = bf16[1,512,1024]{2,1,0:T(8,128)(2,1)} collective-permute-done((bf16[1,512,1024]{2,1,0:T(8,128)(2,1)S(1)}, bf16[1,512,1024]{2,1,0:T(8,128)(2,1)}, u32[]{:S(2)}, u32[]{:S(2)}) %collective-permute-start.7) | collective-permute-done | bytes 1048608 | tf_op jit(solution)/shard_map/ppermute | solution.py:39
  209.1 22.0 %collective-permute-done.12 = bf16[512,1024]{1,0:T(8,128)(2,1)S(1)} collective-permute-done((bf16[512,1024]{1,0:T(8,128)(2,1)S(1)}, bf16[512,1024]{1,0:T(8,128)(2,1)S(1)}, u32[]{:S(2)}, u32[]{:S(2)}) %collective-permute-start.12) | collective-permute-done | bytes 1048608 | tf_op jit(solution)/shard_map/ppermute | solution.py:39
  235.9 14.9 %collective-permute-done.28 = bf16[512,1024]{1,0:T(8,128)(2,1)S(1)} collective-permute-done((bf16[512,1024]{1,0:T(8,128)(2,1)}, bf16[512,1024]{1,0:T(8,128)(2,1)S(1)}, u32[]{:S(2)}, u32[]{:S(2)}) %collective-permute-start.28) | collective-permute-done | bytes 1048608 | tf_op jit(solution)/shard_map/ppermute | solution.py:39
  300.0 18.7 %collective-permute-done.18 = bf16[1024,768]{0,1:T(8,128)(2,1)S(1)} collective-permute-done((bf16[1024,768]{0,1:T(8,128)(2,1)S(1)}, bf16[1024,768]{0,1:T(8,128)(2,1)S(1)}, u32[]{:S(2)}, u32[]{:S(2)}) %collective-permute-start.18) | collective-permute-done | bytes 1572896 | tf_op jit(solution)/shard_map/ppermute | solution.py:39
  327.3 58.4 %collective-permute-done.17 = bf16[1024,768]{0,1:T(8,128)(2,1)S(1)} collective-permute-done((bf16[1024,768]{0,1:T(8,128)(2,1)S(1)}, bf16[1024,768]{0,1:T(8,128)(2,1)S(1)}, u32[]{:S(2)}, u32[]{:S(2)}) %collective-permute-start.17) | collective-permute-done | bytes 1572896 | tf_op jit(solution)/shard_map/ppermute | solution.py:39
  396.3 25.7 %multiply_convert_fusion.1 = (bf16[2048,768]{1,0:T(8,128)(2,1)}, bf16[2048,768]{1,0:T(8,128)(2,1)}, bf16[2048,768]{1,0:T(8,128)(2,1)}) fusion(f32[2048,768]{1,0:T(8,128)} %fusion.36, f32[2048,768]{1,0:T(8,128)} %fusion.35, bf16[768,1024]{1,0:T(8,128)(2,1)} %collective-permute-done.19, bf16[768,1024]{1,0:T(8,128)(2,1)S(1)} %get-tuple-element.116, ...), kind=kOutput, calls=%fused_computation.24 | convolution fusion | flops 6541017088 | bytes 33554432 | tf_op jit(solution)/shard_map/dot_general | solution.py:147
  422.1 16.3 %convolution_convert_fusion.3 = bf16[768,2048]{1,0:T(8,128)(2,1)} fusion(bf16[2048,768]{1,0:T(8,128)(2,1)} %get-tuple-element.102, bf16[512,1024]{1,0:T(8,128)(2,1)} %copy-done.88, bf16[512,1024]{1,0:T(8,128)(2,1)} %copy-done.87, bf16[512,1024]{1,0:T(8,128)(2,1)} %copy-done.68, bf16[512,1024]{1,0:T(8,128)(2,1)} %copy-done.66, ...), kind=kOutput, calls=%fused_computation.37 | convolution fusion | flops 6511132672 | bytes 14680064 | tf_op jit(solution)/shard_map/dot_general | solution.py:153
  520.6 25.1 %collective-permute-done.60 = bf16[1024,768]{0,1:T(8,128)(2,1)S(1)} collective-permute-done((bf16[1024,768]{0,1:T(8,128)(2,1)S(1)}, bf16[1024,768]{0,1:T(8,128)(2,1)S(1)}, u32[]{:S(2)}, u32[]{:S(2)}) %collective-permute-start.60) | collective-permute-done | bytes 1572896 | tf_op jit(solution)/shard_map/ppermute | solution.py:39
  575.6 17.3 %collective-permute-done.23 = bf16[256,2048]{1,0:T(8,128)(2,1)} collective-permute-done((bf16[256,2048]{1,0:T(8,128)(2,1)}, bf16[256,2048]{1,0:T(8,128)(2,1)}, u32[]{:S(2)}, u32[]{:S(2)}) %collective-permute-start.23) | collective-permute-done | bytes 1048608 | tf_op jit(solution)/shard_map/ppermute | solution.py:39
  599.5 16.6 %collective-permute-done.36 = bf16[256,2048]{1,0:T(8,128)(2,1)S(1)} collective-permute-done((bf16[256,2048]{1,0:T(8,128)(2,1)S(1)}, bf16[256,2048]{1,0:T(8,128)(2,1)S(1)}, u32[]{:S(2)}, u32[]{:S(2)}) %collective-permute-start.36) | collective-permute-done | bytes 1048608 | tf_op jit(solution)/shard_map/ppermute | solution.py:39
  653.5 15.6 %collective-permute-done.64 = bf16[1024,640]{0,1:T(8,128)(2,1)S(1)} collective-permute-done((bf16[1024,640]{0,1:T(8,128)(2,1)S(1)}, bf16[1024,640]{0,1:T(8,128)(2,1)S(1)}, u32[]{:S(2)}, u32[]{:S(2)}) %collective-permute-start.64) | collective-permute-done | bytes 1310752 | tf_op jit(solution)/shard_map/ppermute | solution.py:118
  678.0 23.3 %collective-permute-done.61 = bf16[1024,768]{0,1:T(8,128)(2,1)S(1)} collective-permute-done((bf16[1024,768]{0,1:T(8,128)(2,1)S(1)}, bf16[1024,768]{0,1:T(8,128)(2,1)S(1)}, u32[]{:S(2)}, u32[]{:S(2)}) %collective-permute-start.61) | collective-permute-done | bytes 1572896 | tf_op jit(solution)/shard_map/ppermute | solution.py:118
  725.4 46.2 %collective-permute-done.73 = bf16[640,1024]{1,0:T(8,128)(2,1)S(1)} collective-permute-done((bf16[640,1024]{1,0:T(8,128)(2,1)S(1)}, bf16[640,1024]{1,0:T(8,128)(2,1)S(1)}, u32[]{:S(2)}, u32[]{:S(2)}) %collective-permute-start.73) | collective-permute-done | bytes 1310752 | tf_op jit(solution)/shard_map/ppermute | solution.py:122
  792.3 22.6 %fusion = (f32[8,1024]{1,0:T(8,128)S(1)}, f32[1024,1024,8]{1,0,2:T(8,128)}) fusion(f32[1,8,1024,1024]{2,3,1,0:T(8,128)} %get-tuple-element.147, f32[8,1024]{1,0:T(8,128)S(1)} %log_add_fusion, pred[1024,1024]{0,1:T(8,128)(4,1)S(1)} %copy-done.2, bf16[1024,8,64]{0,2,1:T(8,128)(2,1)S(1)} %bitcast.258, f32[1024,640]{0,1:T(8,128)} %copy-done.7), kind=kOutput, calls=%fused_computation.3 | convolution fusion | flops 1107288064 | bytes 69402624 | tf_op jit(solution)/shard_map/while/body/eval_jaxpr/qkgd,skd->kgqs/dot_general | solution.py:189
  814.9 28.5 %fusion.6 = bf16[8,1024,1024]{1,2,0:T(8,128)(2,1)} fusion(f32[1024,1024,8]{1,0,2:T(8,128)} %get-tuple-element.149, f32[1,8,1024,1024]{2,3,1,0:T(8,128)} %get-tuple-element.147, f32[8,1024]{1,0:T(8,128)S(1)} %get-tuple-element.148, f32[8,1024]{1,0:T(8,128)S(1)} %log_add_fusion, pred[1024,1024]{0,1:T(8,128)(4,1)S(1)} %copy-done.2), kind=kLoop, calls=%fused_computation.12 | loop fusion | flops 41943040 | bytes 85000192 | tf_op jit(solution)/shard_map/reshape.92
  870.6 61.1 %collective-permute-done.63 = bf16[1024,768]{0,1:T(8,128)(2,1)} collective-permute-done((bf16[1024,768]{0,1:T(8,128)(2,1)}, bf16[1024,768]{0,1:T(8,128)(2,1)}, u32[]{:S(2)}, u32[]{:S(2)}) %collective-permute-start.63) | collective-permute-done | bytes 1572896 | tf_op jit(solution)/shard_map/ppermute | solution.py:122
  953.4 18.6 %collective-permute-start.47 = (bf16[1024,640]{0,1:T(8,128)(2,1)S(1)}, bf16[1024,640]{0,1:T(8,128)(2,1)S(1)}, u32[]{:S(2)}, u32[]{:S(2)}) collective-permute-start(bf16[1024,640]{0,1:T(8,128)(2,1)S(1)} %fusion.38), channel_id=1, source_target_pairs={{0,8},{24,16},{1,9},{25,17},{2,10},{26,18},{3,11},{27,19},{4,12},{... | collective-permute-start | bytes 3932168 | tf_op jit(solution)/shard_map/ppermute | solution.py:118
  1031.6 14.5 %collective-permute-done.52 = bf16[512,1024]{1,0:T(8,128)(2,1)S(1)} collective-permute-done((bf16[512,1024]{1,0:T(8,128)(2,1)S(1)}, bf16[512,1024]{1,0:T(8,128)(2,1)S(1)}, u32[]{:S(2)}, u32[]{:S(2)}) %collective-permute-start.52) | collective-permute-done | bytes 1048608 | tf_op jit(solution)/shard_map/ppermute | solution.py:122
  1049.3 42.0 %all-reduce = (f32[1024]{0:T(1024)}, f32[1024]{0:T(1024)}) all-reduce(f32[1024]{0:T(1024)S(1)} %get-tuple-element.84, f32[1024]{0:T(1024)S(1)} %get-tuple-element.86), channel_id=1, replica_groups=mesh['dp'=4,'row'=4,'col'=2] {'dp','row'}, use_global_device_ids=true, to_apply=%region_10.11 | all-reduce | flops 2048 | bytes 16384 | tf_op jit(solution)/shard_map/psum | solution.py:349
  (484 shorter events, 493.1 us)
Async XLA Ops:
  208.8 58.4 %collective-permute-start.25 = (bf16[512,1024]{1,0:T(8,128)(2,1)}, bf16[512,1024]{1,0:T(8,128)(2,1)}, u32[]{:S(2)}, u32[]{:S(2)}) collective-permute-start(bf16[512,1024]{1,0:T(8,128)(2,1)} %param.23), channel_id=1, source_target_pairs={{0,1},{1,0},{2,3},{3,2},{4,5},{5,4},{6,7},{7,6},{8,9},{9,8},{10,11... | collective-permute-start | bytes 3145736 | tf_op jit(solution)/shard_map/ppermute | solution.py:39
  284.2 110.1 %collective-permute-start.26 = (bf16[512,1024]{1,0:T(8,128)(2,1)}, bf16[512,1024]{1,0:T(8,128)(2,1)}, u32[]{:S(2)}, u32[]{:S(2)}) collective-permute-start(bf16[512,1024]{1,0:T(8,128)(2,1)} %param.23), channel_id=1, source_target_pairs={{0,2},{2,0},{4,6},{6,4},{1,3},{3,1},{5,7},{7,5},{8,10},{10,8},{12,... | collective-permute-start | bytes 3145736 | tf_op jit(solution)/shard_map/ppermute | solution.py:39
  284.5 109.8 %collective-permute-start.19 = (bf16[768,1024]{1,0:T(8,128)(2,1)S(1)}, bf16[768,1024]{1,0:T(8,128)(2,1)}, u32[]{:S(2)}, u32[]{:S(2)}) collective-permute-start(bf16[768,1024]{1,0:T(8,128)(2,1)S(1)} %get-tuple-element.117), channel_id=1, source_target_pairs={{0,1},{1,0},{2,3},{3,2},{4,5},{5,4},{6,7},{7,6},{8,9},{9,8},{10,11... | collective-permute-start | bytes 4718600 | tf_op jit(solution)/shard_map/ppermute | solution.py:39
  285.6 100.1 %collective-permute-start.17 = (bf16[1024,768]{0,1:T(8,128)(2,1)S(1)}, bf16[1024,768]{0,1:T(8,128)(2,1)S(1)}, u32[]{:S(2)}, u32[]{:S(2)}) collective-permute-start(bf16[1024,768]{0,1:T(8,128)(2,1)S(1)} %copy-done.46), channel_id=1, source_target_pairs={{0,1},{1,0},{2,3},{3,2},{4,5},{5,4},{6,7},{7,6},{8,9},{9,8},{10,11... | collective-permute-start | bytes 4718600 | tf_op jit(solution)/shard_map/ppermute | solution.py:39
  286.6 107.7 %collective-permute-start.27 = (bf16[512,1024]{1,0:T(8,128)(2,1)}, bf16[512,1024]{1,0:T(8,128)(2,1)}, u32[]{:S(2)}, u32[]{:S(2)}) collective-permute-start(bf16[512,1024]{1,0:T(8,128)(2,1)} %collective-permute-done.25), channel_id=1, source_target_pairs={{0,2},{2,0},{4,6},{6,4},{1,3},{3,1},{5,7},{7,5},{8,10},{10,8},{12,... | collective-permute-start | bytes 3145736 | tf_op jit(solution)/shard_map/ppermute | solution.py:39
  318.7 75.7 %collective-permute-start.31 = (bf16[512,1024]{1,0:T(8,128)(2,1)S(1)}, bf16[512,1024]{1,0:T(8,128)(2,1)S(1)}, u32[]{:S(2)}, u32[]{:S(2)}) collective-permute-start(bf16[512,1024]{1,0:T(8,128)(2,1)S(1)} %copy-done.67), channel_id=1, source_target_pairs={{0,2},{2,0},{4,6},{6,4},{1,3},{3,1},{5,7},{7,5},{8,10},{10,8},{12,... | collective-permute-start | bytes 3145736 | tf_op jit(solution)/shard_map/ppermute | solution.py:39
  441.3 67.4 %collective-permute-start.67 = (bf16[768,1024]{1,0:T(8,128)(2,1)}, bf16[768,1024]{1,0:T(8,128)(2,1)}, u32[]{:S(2)}, u32[]{:S(2)}) collective-permute-start(bf16[768,1024]{1,0:T(8,128)(2,1)} %slice.296), channel_id=1, source_target_pairs={{0,1},{1,0},{2,3},{3,2},{4,5},{5,4},{6,7},{7,6},{8,9},{9,8},{10,11... | collective-permute-start | bytes 4718600 | tf_op jit(solution)/shard_map/ppermute | solution.py:39
  454.5 60.9 %collective-permute-start.53 = (bf16[1024,768]{0,1:T(8,128)(2,1)}, bf16[1024,768]{0,1:T(8,128)(2,1)S(1)}, u32[]{:S(2)}, u32[]{:S(2)}) collective-permute-start(bf16[1024,768]{0,1:T(8,128)(2,1)} %slice.288), channel_id=1, source_target_pairs={{0,1},{1,0},{2,3},{3,2},{4,5},{5,4},{6,7},{7,6},{8,9},{9,8},{10,11... | collective-permute-start | bytes 4718600 | tf_op jit(solution)/shard_map/ppermute | solution.py:39
  469.8 87.4 %collective-permute-start.20 = (bf16[2,512,2048]{2,1,0:T(8,128)(2,1)}, bf16[2,512,2048]{2,1,0:T(8,128)(2,1)}, u32[]{:S(2)}, u32[]{:S(2)}) collective-permute-start(bf16[2,512,2048]{2,1,0:T(8,128)(2,1)} %slice_bitcast_fusion.2), channel_id=1, source_target_pairs={{0,2},{2,0},{4,6},{6,4},{1,3},{3,1},{5,7},{7,5},{8,10},{10,8},{12,... | collective-permute-start | bytes 12582920 | tf_op jit(solution)/shard_map/ppermute | solution.py:39
  497.4 70.9 %collective-permute-start.33 = (bf16[2,512,2048]{2,1,0:T(8,128)(2,1)}, bf16[2,512,2048]{2,1,0:T(8,128)(2,1)}, u32[]{:S(2)}, u32[]{:S(2)}) collective-permute-start(bf16[2,512,2048]{2,1,0:T(8,128)(2,1)} %slice_bitcast_fusion), channel_id=1, source_target_pairs={{0,2},{2,0},{4,6},{6,4},{1,3},{3,1},{5,7},{7,5},{8,10},{10,8},{12,... | collective-permute-start | bytes 12582920 | tf_op jit(solution)/shard_map/ppermute | solution.py:39
  515.4 155.7 %collective-permute-start.68 = (bf16[768,1024]{1,0:T(8,128)(2,1)}, bf16[768,1024]{1,0:T(8,128)(2,1)}, u32[]{:S(2)}, u32[]{:S(2)}) collective-permute-start(bf16[768,1024]{1,0:T(8,128)(2,1)} %get-tuple-element.110), channel_id=1, source_target_pairs={{0,8},{24,16},{1,9},{25,17},{2,10},{26,18},{3,11},{27,19},{4,12},{... | collective-permute-start | bytes 4718600 | tf_op jit(solution)/shard_map/ppermute | solution.py:118
  545.6 99.7 %collective-permute-start.57 = (bf16[1024,640]{0,1:T(8,128)(2,1)}, bf16[1024,640]{0,1:T(8,128)(2,1)}, u32[]{:S(2)}, u32[]{:S(2)}) collective-permute-start(bf16[1024,640]{0,1:T(8,128)(2,1)} %slice_select_fusion.3), channel_id=1, source_target_pairs={{0,8},{24,16},{1,9},{25,17},{2,10},{26,18},{3,11},{27,19},{4,12},{... | collective-permute-start | bytes 3932168 | tf_op jit(solution)/shard_map/ppermute | solution.py:118
  552.9 121.8 %collective-permute-start.54 = (bf16[1024,768]{0,1:T(8,128)(2,1)}, bf16[1024,768]{0,1:T(8,128)(2,1)}, u32[]{:S(2)}, u32[]{:S(2)}) collective-permute-start(bf16[1024,768]{0,1:T(8,128)(2,1)} %get-tuple-element.114), channel_id=1, source_target_pairs={{0,8},{24,16},{1,9},{25,17},{2,10},{26,18},{3,11},{27,19},{4,12},{... | collective-permute-start | bytes 4718600 | tf_op jit(solution)/shard_map/ppermute | solution.py:118
  642.1 59.2 %collective-permute-start.61 = (bf16[1024,768]{0,1:T(8,128)(2,1)S(1)}, bf16[1024,768]{0,1:T(8,128)(2,1)S(1)}, u32[]{:S(2)}, u32[]{:S(2)}) collective-permute-start(bf16[1024,768]{0,1:T(8,128)(2,1)S(1)} %copy-done.17), channel_id=1, source_target_pairs={{0,8},{24,16},{1,9},{25,17},{2,10},{26,18},{3,11},{27,19},{4,12},{... | collective-permute-start | bytes 4718600 | tf_op jit(solution)/shard_map/ppermute | solution.py:118
  649.0 53.8 %collective-permute-start.72 = (bf16[640,1024]{1,0:T(8,128)(2,1)S(1)}, bf16[640,1024]{1,0:T(8,128)(2,1)S(1)}, u32[]{:S(2)}, u32[]{:S(2)}) collective-permute-start(bf16[640,1024]{1,0:T(8,128)(2,1)S(1)} %copy-done.19), channel_id=1, source_target_pairs={{8,16},{16,8},{9,17},{17,9},{10,18},{18,10},{11,19},{19,11},{12,20... | collective-permute-start | bytes 3932168 | tf_op jit(solution)/shard_map/ppermute | solution.py:120
  708.8 62.7 %collective-permute-start.73 = (bf16[640,1024]{1,0:T(8,128)(2,1)S(1)}, bf16[640,1024]{1,0:T(8,128)(2,1)S(1)}, u32[]{:S(2)}, u32[]{:S(2)}) collective-permute-start(bf16[640,1024]{1,0:T(8,128)(2,1)S(1)} %add_convert_fusion.7), channel_id=1, source_target_pairs={{8,0},{16,24},{9,1},{17,25},{10,2},{18,26},{11,3},{19,27},{12,4},{... | collective-permute-start | bytes 3932168 | tf_op jit(solution)/shard_map/ppermute | solution.py:122
  710.3 155.4 %collective-permute-start.59 = (bf16[1024,640]{0,1:T(8,128)(2,1)}, bf16[1024,640]{0,1:T(8,128)(2,1)}, u32[]{:S(2)}, u32[]{:S(2)}) collective-permute-start(bf16[1024,640]{0,1:T(8,128)(2,1)} %add_convert_fusion.11), channel_id=1, source_target_pairs={{8,0},{16,24},{9,1},{17,25},{10,2},{18,26},{11,3},{19,27},{12,4},{... | collective-permute-start | bytes 3932168 | tf_op jit(solution)/shard_map/ppermute | solution.py:122
  714.3 59.9 %collective-permute-start.42 = (bf16[1024,512]{1,0:T(8,128)(2,1)S(1)}, bf16[1024,512]{1,0:T(8,128)(2,1)S(1)}, u32[]{:S(2)}, u32[]{:S(2)}) collective-permute-start(bf16[1024,512]{1,0:T(8,128)(2,1)S(1)} %fusion.53), channel_id=1, source_target_pairs={{0,1},{1,0},{2,3},{3,2},{4,5},{5,4},{6,7},{7,6},{8,9},{9,8},{10,11... | collective-permute-start | bytes 3145736 | tf_op jit(solution)/shard_map/ppermute | solution.py:39
  719.1 149.8 %collective-permute-start.66 = (bf16[1024,640]{0,1:T(8,128)(2,1)}, bf16[1024,640]{0,1:T(8,128)(2,1)}, u32[]{:S(2)}, u32[]{:S(2)}) collective-permute-start(bf16[1024,640]{0,1:T(8,128)(2,1)} %add_convert_fusion.9), channel_id=1, source_target_pairs={{8,0},{16,24},{9,1},{17,25},{10,2},{18,26},{11,3},{19,27},{12,4},{... | collective-permute-start | bytes 3932168 | tf_op jit(solution)/shard_map/ppermute | solution.py:122
  722.3 293.2 %collective-permute-start.70 = (bf16[768,1024]{1,0:T(8,128)(2,1)}, bf16[768,1024]{1,0:T(8,128)(2,1)}, u32[]{:S(2)}, u32[]{:S(2)}) collective-permute-start(bf16[768,1024]{1,0:T(8,128)(2,1)} %add_convert_fusion.1), channel_id=1, source_target_pairs={{8,0},{16,24},{9,1},{17,25},{10,2},{18,26},{11,3},{19,27},{12,4},{... | collective-permute-start | bytes 4718600 | tf_op jit(solution)/shard_map/ppermute | solution.py:122
  771.6 209.6 %collective-permute-start.56 = (bf16[1024,768]{0,1:T(8,128)(2,1)}, bf16[1024,768]{0,1:T(8,128)(2,1)}, u32[]{:S(2)}, u32[]{:S(2)}) collective-permute-start(bf16[1024,768]{0,1:T(8,128)(2,1)} %add_convert_fusion.5), channel_id=1, source_target_pairs={{8,0},{16,24},{9,1},{17,25},{10,2},{18,26},{11,3},{19,27},{12,4},{... | collective-permute-start | bytes 4718600 | tf_op jit(solution)/shard_map/ppermute | solution.py:122
  774.2 157.6 %collective-permute-start.63 = (bf16[1024,768]{0,1:T(8,128)(2,1)}, bf16[1024,768]{0,1:T(8,128)(2,1)}, u32[]{:S(2)}, u32[]{:S(2)}) collective-permute-start(bf16[1024,768]{0,1:T(8,128)(2,1)} %add_convert_fusion.3), channel_id=1, source_target_pairs={{8,0},{16,24},{9,1},{17,25},{10,2},{18,26},{11,3},{19,27},{12,4},{... | collective-permute-start | bytes 4718600 | tf_op jit(solution)/shard_map/ppermute | solution.py:122
  865.6 81.8 %collective-permute-start.43 = (bf16[1024,640]{0,1:T(8,128)(2,1)S(1)}, bf16[1024,640]{0,1:T(8,128)(2,1)S(1)}, u32[]{:S(2)}, u32[]{:S(2)}) collective-permute-start(bf16[1024,640]{0,1:T(8,128)(2,1)S(1)} %pad_maximum_fusion.19), channel_id=1, source_target_pairs={{0,1},{1,0},{2,3},{3,2},{4,5},{5,4},{6,7},{7,6},{8,9},{9,8},{10,11... | collective-permute-start | bytes 3932168 | tf_op jit(solution)/shard_map/ppermute | solution.py:39
  1026.8 69.1 %collective-permute-start.49 = (bf16[1024,640]{0,1:T(8,128)(2,1)S(1)}, bf16[1024,640]{0,1:T(8,128)(2,1)}, u32[]{:S(2)}, u32[]{:S(2)}) collective-permute-start(bf16[1024,640]{0,1:T(8,128)(2,1)S(1)} %add_convert_fusion.13), channel_id=1, source_target_pairs={{8,0},{16,24},{9,1},{17,25},{10,2},{18,26},{11,3},{19,27},{12,4},{... | collective-permute-start | bytes 3932168 | tf_op jit(solution)/shard_map/ppermute | solution.py:122
  (145 other events, 2880.3 us)

commit v2 on v1

v2 whole, which is shorter than its diff:
```python
import jax
import jax.numpy as jnp
from jax import lax
from jax.experimental import pallas as pl
from jax.experimental.pallas import tpu as pltpu
from jax.sharding import PartitionSpec as P

HD = 64
LANES = 128

epsilon = 1e-05
rope_base = 10000.0
BF = jnp.bfloat16
F32 = jnp.float32


def positions_of(segment_row):
    indices = jnp.arange(segment_row.shape[0], dtype=jnp.int32)
    previous = jnp.concatenate([segment_row[:1] - 1, segment_row[:-1]])
    start_index = lax.cummax(jnp.where(segment_row != previous, indices, 0), axis=0)
    return indices - start_index


def rotary_tables(positions):
    frequency = rope_base ** (-jnp.arange(HD // 2).astype(F32) * 2.0 / HD)
    angles = positions.astype(F32)[..., None] * frequency
    cosine = jnp.cos(angles)
    sine = jnp.sin(angles)
    return (
        jnp.concatenate([cosine] * 4, -1),
        jnp.concatenate([-sine, sine, -sine, sine], -1),
    )


def swap(values, axis, bit):
    pairs = [(i, i ^ bit) for i in range(lax.axis_size(axis))]
    return lax.ppermute(values, axis, pairs)


def swap_sum(values):
    return values + swap(values, "col", 1)


def pick(values, index, axis):
    return lax.dynamic_index_in_dim(values, index, axis, keepdims=False)


def pair_up(own, other, first, axis):
    return jnp.concatenate([jnp.where(first, own, other), jnp.where(first, other, own)], axis)


def gather_row(block):
    size = lax.axis_size("row")
    blocks = {0: block}
    bit = size // 2
    while bit:
        for offset in list(blocks):
            blocks[offset | bit] = swap(blocks[offset], "row", bit)
        bit //= 2
    me = lax.axis_index("row")
    whole = jnp.zeros((size * block.shape[0],) + block.shape[1:], block.dtype)
    for offset, part in blocks.items():
        whole = lax.dynamic_update_slice_in_dim(whole, part, (me ^ offset) * block.shape[0], 0)
    return whole


def scatter_row(leading, product):
    me = lax.axis_index("row")
    block = leading.shape[0] // 4
    split = leading.reshape(2, 2, block, leading.shape[1])
    sent = product(pick(split, 1 - (me & 1), 1).reshape(2 * block, -1)).astype(BF)
    arrived = swap(sent, "row", 1)
    kept = product(pick(split, me & 1, 1).reshape(2 * block, -1))
    both = (kept + arrived.astype(F32)).reshape(2, block, -1)
    return pick(both, me >> 1, 0) + swap(
        pick(both, 1 - (me >> 1), 0).astype(BF), "row", 2
    ).astype(F32)


def gather_plane(block):
    half = block.shape[0] // 2
    across, along = yield (swap(block, "col", 1), swap(block, "row", 2))
    corner_first, corner_second = yield (
        swap(along[:half], "col", 1),
        swap(across[half:], "row", 2),
    )
    own = jnp.concatenate([block, along], 0)
    other = jnp.concatenate([across, corner_first, corner_second], 0)
    yield (
        jnp.concatenate([own, swap(own, "row", 1)], 0),
        jnp.concatenate([other, swap(other, "row", 1)], 0),
    )


def scatter_plane(kept, sent):
    arrived = [swap(values, "row", 1) for values in sent]
    own, other = [
        (values.astype(F32) + more.astype(F32)).reshape(2, -1, values.shape[1])
        for values, more in zip(kept, arrived)
    ]
    half = own.shape[1] // 2
    first_own, first_other = own[:, :half], other[:, :half].astype(BF)
    second_own, second_other = own[:, half:], other[:, half:]
    first_got = swap(first_other, "col", 1)
    second_got_own = swap(second_own[1].astype(BF), "row", 2)
    second_got_other = swap(second_other[1].astype(BF), "row", 2)
    first_got, second_got_own, second_got_other = yield (
        first_got,
        second_got_own,
        second_got_other,
    )
    first_sum = first_own + first_got.astype(F32)
    second_mine = second_own[0] + second_got_own.astype(F32)
    second_theirs = (second_other[0] + second_got_other.astype(F32)).astype(BF)
    first_sum = first_sum[0] + swap(first_sum[1].astype(BF), "row", 2).astype(F32)
    second_sum = second_mine + swap(second_theirs, "col", 1).astype(F32)
    yield jnp.concatenate([first_sum, second_sum], 0)


def order(*values):
    return lax.optimization_barrier(values)


class LineSum:
    def __init__(self):
        self.line = lax.axis_size("dp") == 4
        self.flight = []

    def add(self, values, finish):
        if self.line:
            self.flight.append([0, values, None, finish])
        else:
            if values.dtype == F32:
                finish(lax.psum(values, "dp"))
                return
            mine = lax.psum_scatter(values, "dp", scatter_dimension=0, tiled=True)
            finish(lax.all_gather(mine, "dp", axis=0, tiled=True))

    def step(self, *anchors):
        moving = [item for item in self.flight if item[2] is not None]
        results = order(*anchors, *[item[2] for item in moving])
        for item, got in zip(moving, results[len(anchors) :]):
            item[2] = got
        place = lax.axis_index("dp")
        for item in list(self.flight):
            stage, values, got, finish = item
            if stage == 3:
                finish(jnp.where((place == 0) | (place == 3), got, values))
                self.flight.remove(item)
                continue
            if stage:
                values = (values.astype(F32) + got.astype(F32)).astype(values.dtype)
            pairs = ([(0, 1), (3, 2)], [(1, 2), (2, 1)], [(1, 0), (2, 3)])[stage]
            item[:3] = [stage + 1, values, lax.ppermute(values, "dp", pairs)]
        return results[: len(anchors)]

    def drain(self):
        while self.flight:
            self.step()


def norm_forward(values, gain, full_width):
    squares = swap_sum(jnp.sum(values * values, -1, keepdims=True))
    scale = lax.rsqrt(squares / full_width + epsilon)
    normed = values * scale
    return (normed, scale, (normed * gain).astype(BF))


def norm_backward(grad_hidden, normed, scale, gain, full_width):
    grad_normed = grad_hidden * gain
    inner_sum = swap_sum(jnp.sum(grad_normed * normed, -1, keepdims=True))
    return (
        scale * (grad_normed - normed * inner_sum / full_width),
        jnp.sum(grad_hidden * normed, 0),
    )


def contract(leading, weight):
    return jnp.dot(leading, weight, preferred_element_type=F32)


def contract_flipped(leading, weight):
    return lax.dot_general(
        leading, weight, (((1,), (1,)), ((), ())), preferred_element_type=F32
    )


def outer_sum(leading, trailing):
    return lax.dot_general(
        leading, trailing, (((0,), (0,)), ((), ())), preferred_element_type=F32
    ).astype(BF)


ROWS = 256
PAIR = 2 * HD


def dot_nt(leading, trailing):
    return lax.dot_general(leading, trailing, (((1,), (1,)), ((), ())), preferred_element_type=F32)


def dot_nn(leading, trailing):
    return jnp.dot(leading, trailing, preferred_element_type=F32)


def turn(vectors, cosine, sine, lane):
    ahead = pltpu.roll(vectors, PAIR - HD // 2, 1)
    behind = pltpu.roll(vectors, HD // 2, 1)
    return vectors * cosine + jnp.where(lane % HD < HD // 2, ahead, behind) * sine


def fill_bias(starts_ref, bias):
    length = bias.shape[0]
    for base in range(0, length, ROWS):
        key = lax.broadcasted_iota(jnp.int32, (ROWS, length), 0) + base
        query = lax.broadcasted_iota(jnp.int32, (ROWS, length), 1)
        allowed = (key <= query) & (key >= starts_ref[0])
        bias[base : base + ROWS, :] = jnp.where(allowed, 0.0, -1e30)


def split_heads(values, lane):
    low = jnp.where(lane < HD, values, 0.0)
    return low, pltpu.roll(low, HD, 1)


def forward_kernel(
    kept_ref, sent_ref, kept_kv_ref, sent_kv_ref, cos_ref, sin_ref, starts_ref, *rest, anchors
):
    att_ref, q_ref, kv_ref, lse_ref, keys, values_t, bias = rest[anchors:]
    length = kept_ref.shape[0]
    lane = lax.broadcasted_iota(jnp.int32, (length, PAIR), 1)

    @pl.when(pl.program_id(1) == 0)
    def _():
        joined = kept_kv_ref[...].astype(F32) + sent_kv_ref[...].astype(F32)
        turned = turn(joined, cos_ref[0], sin_ref[0], lane)
        low = jnp.where(lane < HD, turned, joined).astype(BF)
        kv_ref[...] = low
        wide = low.astype(F32)
        key_a, key_b = split_heads(wide, lane)
        keys[0] = key_a.astype(BF)
        keys[1] = key_b.astype(BF)
        value_a, value_b = split_heads(pltpu.roll(wide, HD, 1), lane)
        values_t[0] = value_a.T.astype(BF)
        values_t[1] = value_b.T.astype(BF)
        fill_bias(starts_ref, bias)

    joined = kept_ref[...].astype(F32) + sent_ref[...].astype(F32)
    queries = turn(joined, cos_ref[0], sin_ref[0], lane).astype(BF)
    q_ref[...] = queries
    queries = queries * jnp.asarray(HD**-0.5, BF)
    for base in range(0, length, ROWS):
        block = queries[base : base + ROWS]
        count = base + ROWS
        mixed = jnp.zeros((PAIR, ROWS), F32)
        for head in range(2):
            scores = dot_nt(keys[head, :count], block) + bias[:count, base:count]
            highest = jnp.max(scores, 0, keepdims=True)
            weights = jnp.exp(scores - highest)
            total = jnp.sum(weights, 0, keepdims=True)
            part = dot_nn(values_t[head, :, :count], weights.astype(BF))
            mixed = mixed + part / total
            lse_ref[0, head : head + 1, base:count] = highest + jnp.log(total)
        att_ref[base:count, :] = mixed.T.astype(BF)


def backward_kernel(
    kept_ref, sent_ref, q_ref, kv_ref, lse_ref, cos_ref, sin_ref, starts_ref, *rest, anchors
):
    grad_ref, keys, keys_t, values, bias, grad_keys, grad_values = rest[anchors:]
    length = kv_ref.shape[0]
    lane = lax.broadcasted_iota(jnp.int32, (length, PAIR), 1)
    step = pl.program_id(1)
    last = pl.num_programs(1) - 1

    @pl.when(step == 0)
    def _():
        wide = kv_ref[...].astype(F32)
        for head, part in enumerate(split_heads(wide, lane)):
            keys[head] = part.astype(BF)
            keys_t[head] = part.T.astype(BF)
        for head, part in enumerate(split_heads(pltpu.roll(wide, HD, 1), lane)):
            values[head] = part.astype(BF)
        fill_bias(starts_ref, bias)
        grad_keys[...] = jnp.zeros_like(grad_keys)
        grad_values[...] = jnp.zeros_like(grad_values)

    @pl.when(step < last)
    def _():
        given = (kept_ref[...].astype(F32) + sent_ref[...].astype(F32)).astype(BF)
        queries = q_ref[...] * jnp.asarray(HD**-0.5, BF)
        zero = jnp.zeros_like(given)
        for base in range(0, length, ROWS):
            count = base + ROWS
            block = queries[base:count]
            gave = given[base:count]
            side = lane[base:count] < HD
            grad_t = jnp.zeros((PAIR, ROWS), F32)
            for head in range(2):
                mine = side if head == 0 else jnp.logical_not(side)
                block_mine = jnp.where(mine, block, zero[:ROWS])
                gave_mine = jnp.where(mine, gave, zero[:ROWS])
                scores = dot_nt(keys[head, :count], block) + bias[:count, base:count]
                weights = jnp.exp(scores - lse_ref[0, head : head + 1, base:count])
                grad_weights = dot_nt(values[head, :count], gave)
                product = weights * grad_weights
                inner = jnp.sum(product, 0, keepdims=True)
                grad_scores = (product - weights * inner).astype(BF)
                grad_values[:count] += dot_nn(weights.astype(BF), gave_mine)
                grad_keys[:count] += dot_nn(grad_scores, block_mine)
                grad_t = grad_t + dot_nn(keys_t[head, :, :count], grad_scores)
            grad = grad_t.T * HD**-0.5
            grad_ref[base:count, :] = turn(
                grad, cos_ref[0, base:count], -sin_ref[0, base:count], lane[base:count]
            ).astype(BF)

    @pl.when(step == last)
    def _():
        key_sum = grad_keys[...] + pltpu.roll(grad_keys[...], HD, 1)
        value_sum = grad_values[...] + pltpu.roll(grad_values[...], HD, 1)
        turned = turn(key_sum, cos_ref[0], -sin_ref[0], lane)
        grad_ref[...] = jnp.where(lane < HD, turned, value_sum).astype(BF)


VMEM = 48 * 1024 * 1024


def hidden_kernel(
    own_ref, other_ref, gate_ref, gate_other_ref, up_ref, up_other_ref, given_ref,
    act_ref, grad_gate_ref, grad_up_ref,
):
    own, other = own_ref[...], other_ref[...]
    gate = dot_nn(own, gate_ref[...]) + dot_nn(other, gate_other_ref[...])
    up = dot_nn(own, up_ref[...]) + dot_nn(other, up_other_ref[...])
    given = given_ref[...].astype(F32)
    bent = 1.0 / (1.0 + jnp.exp(-gate))
    silu = gate * bent
    act_ref[...] = (silu * up).astype(BF)
    grad_gate_ref[...] = (given * up * bent * (1.0 + gate * (1.0 - bent))).astype(BF)
    grad_up_ref[...] = (given * silu).astype(BF)


def hidden_part(own, other, gate, gate_other, up, up_other, given):
    tokens, width = own.shape
    hidden = gate.shape[1]
    rows = lambda columns: pl.BlockSpec((ROWS, columns), lambda i: (i, 0))
    whole = pl.BlockSpec((width, hidden), lambda i: (0, 0))
    return pl.pallas_call(
        hidden_kernel,
        grid=(tokens // ROWS,),
        in_specs=[rows(width), rows(width), whole, whole, whole, whole, rows(hidden)],
        out_specs=[rows(hidden)] * 3,
        out_shape=[jax.ShapeDtypeStruct((tokens, hidden), BF)] * 3,
        compiler_params=pltpu.CompilerParams(vmem_limit_bytes=VMEM),
        cost_estimate=pl.CostEstimate(
            flops=8 * tokens * width * hidden, bytes_accessed=24 * 2**20, transcendentals=0
        ),
        name="hidden_part",
    )(own, other, gate, gate_other, up, up_other, given)


def back_kernel(grad_gate_ref, grad_up_ref, gate_ref, gate_other_ref, up_ref, up_other_ref, own_ref, other_ref):
    grad_gate, grad_up = grad_gate_ref[...], grad_up_ref[...]
    own_ref[...] = (dot_nt(grad_gate, gate_ref[...]) + dot_nt(grad_up, up_ref[...])).astype(BF)
    other_ref[...] = (
        dot_nt(grad_gate, gate_other_ref[...]) + dot_nt(grad_up, up_other_ref[...])
    ).astype(BF)


def back_part(grad_gate, grad_up, gate, gate_other, up, up_other, half):
    hidden = grad_gate.shape[1]
    tokens = grad_gate.shape[0] // 2
    width = gate.shape[0]
    steps = tokens // ROWS
    rows = pl.BlockSpec((ROWS, hidden), lambda i: (i + half * steps, 0))
    whole = pl.BlockSpec((width, hidden), lambda i: (0, 0))
    return pl.pallas_call(
        back_kernel,
        grid=(steps,),
        in_specs=[rows, rows, whole, whole, whole, whole],
        out_specs=[pl.BlockSpec((ROWS, width), lambda i: (i, 0))] * 2,
        out_shape=[jax.ShapeDtypeStruct((tokens, width), BF)] * 2,
        compiler_params=pltpu.CompilerParams(vmem_limit_bytes=VMEM),
        cost_estimate=pl.CostEstimate(
            flops=8 * tokens * width * hidden, bytes_accessed=12 * 2**20, transcendentals=0
        ),
        name="back_part",
    )(grad_gate, grad_up, gate, gate_other, up, up_other)


def attention_forward(kept, sent, cosine, sine, starts, anchors=()):
    sequences, _, length = starts.shape
    pairs = kept.shape[1] // PAIR - 1
    here = lambda s, i: (s, i)
    kv_at = lambda s, i: (s, pairs)
    table = pl.BlockSpec((1, length, PAIR), lambda s, i: (s, 0, 0))
    return pl.pallas_call(
        lambda *refs: forward_kernel(*refs, anchors=len(anchors)),
        grid=(sequences, pairs),
        in_specs=[
            pl.BlockSpec((length, PAIR), here),
            pl.BlockSpec((length, PAIR), here),
            pl.BlockSpec((length, PAIR), kv_at),
            pl.BlockSpec((length, PAIR), kv_at),
            table,
            table,
            pl.BlockSpec((1, 1, length), lambda s, i: (s, 0, 0)),
        ]
        + [pl.BlockSpec(memory_space=pl.ANY)] * len(anchors),
        out_specs=[
            pl.BlockSpec((length, PAIR), here),
            pl.BlockSpec((length, PAIR), here),
            pl.BlockSpec((length, PAIR), lambda s, i: (s, 0)),
            pl.BlockSpec((1, 2, length), lambda s, i: (s * pairs + i, 0, 0)),
        ],
        out_shape=[
            jax.ShapeDtypeStruct((sequences * length, pairs * PAIR), BF),
            jax.ShapeDtypeStruct((sequences * length, pairs * PAIR), BF),
            jax.ShapeDtypeStruct((sequences * length, PAIR), BF),
            jax.ShapeDtypeStruct((sequences * pairs, 2, length), F32),
        ],
        scratch_shapes=[
            pltpu.VMEM((2, length, PAIR), BF),
            pltpu.VMEM((2, PAIR, length), BF),
            pltpu.VMEM((length, length), F32),
        ],
        compiler_params=pltpu.CompilerParams(vmem_limit_bytes=VMEM),
        cost_estimate=pl.CostEstimate(
            flops=20 * 10**9, bytes_accessed=8 * 2**20, transcendentals=0
        ),
        name="attention_forward",
    )(kept, sent, kept, sent, cosine, sine, starts, *anchors)


def attention_backward(kept, sent, queries, kv, log_totals, cosine, sine, starts, anchors=()):
    sequences, _, length = starts.shape
    pairs = queries.shape[1] // PAIR
    here = lambda s, i: (s, jnp.minimum(i, pairs - 1))
    table = pl.BlockSpec((1, length, PAIR), lambda s, i: (s, 0, 0))
    return pl.pallas_call(
        lambda *refs: backward_kernel(*refs, anchors=len(anchors)),
        grid=(sequences, pairs + 1),
        in_specs=[
            pl.BlockSpec((length, PAIR), here),
            pl.BlockSpec((length, PAIR), here),
            pl.BlockSpec((length, PAIR), here),
            pl.BlockSpec((length, PAIR), lambda s, i: (s, 0)),
            pl.BlockSpec(
                (1, 2, length), lambda s, i: (s * pairs + jnp.minimum(i, pairs - 1), 0, 0)
            ),
            table,
            table,
            pl.BlockSpec((1, 1, length), lambda s, i: (s, 0, 0)),
        ]
        + [pl.BlockSpec(memory_space=pl.ANY)] * len(anchors),
        out_specs=pl.BlockSpec((length, PAIR), lambda s, i: (s, i)),
        out_shape=jax.ShapeDtypeStruct((sequences * length, (pairs + 1) * PAIR), BF),
        scratch_shapes=[
            pltpu.VMEM((2, length, PAIR), BF),
            pltpu.VMEM((2, PAIR, length), BF),
            pltpu.VMEM((2, length, PAIR), BF),
            pltpu.VMEM((length, length), F32),
            pltpu.VMEM((length, PAIR), F32),
            pltpu.VMEM((length, PAIR), F32),
        ],
        compiler_params=pltpu.CompilerParams(vmem_limit_bytes=VMEM),
        cost_estimate=pl.CostEstimate(
            flops=40 * 10**9, bytes_accessed=8 * 2**20, transcendentals=0
        ),
        name="attention_backward",
    )(kept, sent, queries, kv, log_totals, cosine, sine, starts, *anchors)


def body(
    inputs,
    segments,
    norm1_gain,
    query_weight,
    key_weight,
    value_weight,
    out_weight,
    norm2_gain,
    gate_weight,
    up_weight,
    down_weight,
    cotangent,
):
    columns = lax.axis_size("col")
    full_width = norm1_gain.shape[0] * columns
    query_width = query_weight.shape[1]
    pair_width = key_weight.shape[1]
    hidden_width = gate_weight.shape[1]
    per_column = segments.shape[0] // columns
    seq_length = segments.shape[1]
    local_tokens = per_column * seq_length
    column = lax.axis_index("col")
    first_column = column == 0
    part = hidden_width // 2
    line = LineSum()

    def cut(weight, axis):
        low = lax.slice_in_dim(weight, 0, part, axis=axis)
        high = lax.slice_in_dim(weight, part, 2 * part, axis=axis)
        return jnp.where(first_column, low, high), jnp.where(first_column, high, low)

    even = lax.axis_size("dp") % 2 == 0
    low_plane = (lax.axis_index("dp") & 1) == 0

    def cross(sent):
        if not even:
            return swap(sent, "col", 1)
        half = sent.shape[0] // 2
        return swap(jnp.where(low_plane, sent[:half], sent[half:]), "col", 1)

    def share(got):
        if not even:
            return got
        return pair_up(got, swap(got, "dp", 1), low_plane, 0)

    def rows_of(whole, index):
        return lax.dynamic_slice_in_dim(whole, index * local_tokens, local_tokens, 0)

    def gather_col(block):
        return pair_up(block, swap(block, "col", 1), first_column, 0)

    features = inputs.astype(F32)
    gain_one = norm1_gain.astype(F32)
    gain_two = norm2_gain.astype(F32)
    normed_one, scale_one, hidden_one = norm_forward(features, gain_one, full_width)
    hidden_one_all = gather_row(hidden_one)
    gate, gate_sent = cut(gate_weight, 1)
    up, up_sent = cut(up_weight, 1)
    down, down_sent = cut(down_weight, 0)
    gate_got, down_got, up_got = cross(gate_sent), cross(down_sent), cross(up_sent)

    qkv_weight = jnp.concatenate([query_weight, key_weight, value_weight], 1)
    local_segments = lax.dynamic_slice_in_dim(segments, column * per_column, per_column, 0)
    positions = jax.vmap(positions_of)(local_segments)
    cosine, sine = rotary_tables(positions)
    starts = (jnp.arange(seq_length, dtype=jnp.int32) - positions)[:, None, :]

    hidden_one_all, gate_got = order(hidden_one_all, gate_got)
    leaving = contract(rows_of(hidden_one_all, 1 - column), qkv_weight).astype(BF)
    leaving, cotangent, down_got, up_got = order(leaving, cotangent, down_got, up_got)
    sent = swap(leaving, "col", 1)
    kept = contract(rows_of(hidden_one_all, column), qkv_weight)
    cot_plane = gather_plane(cotangent)
    cot_flight = next(cot_plane)
    kept, sent, *cot_flight = order(kept, sent, *cot_flight)
    cot_flight = cot_plane.send(cot_flight)
    gate_other, down_other, up_other = share(gate_got), share(down_got), share(up_got)
    attended, queries, kv, log_totals = attention_forward(kept, sent, cosine, sine, starts)
    attended, gate_other, down_other, *cot_flight = order(
        attended, gate_other, down_other, *cot_flight
    )
    cot_own, cot_other = cot_plane.send(cot_flight)
    attended_all = gather_col(attended)
    attended_all, up_other, cot_own, cot_other = order(attended_all, up_other, cot_own, cot_other)
    attn_branch = scatter_row(attended_all, lambda rows: contract(rows, out_weight))
    grad_activated = (
        contract_flipped(cot_own, down) + contract_flipped(cot_other, down_other)
    ).astype(BF)
    attn_branch, grad_activated = order(attn_branch, grad_activated)
    middle = features + attn_branch
    normed_two, scale_two, hidden_two = norm_forward(middle, gain_two, full_width)
    two_plane = gather_plane(hidden_two)
    two_own, two_other = two_plane.send(two_plane.send(next(two_plane)))
    activated, grad_gate_part, grad_up_part = hidden_part(
        two_own, two_other, gate, gate_other, up, up_other, grad_activated
    )

    done = {}

    def reduce(name, values):
        line.add(values, lambda total: done.__setitem__(name, total))

    down_grad = outer_sum(activated, cot_own)
    grad_gate_part, grad_up_part, down_grad = order(grad_gate_part, grad_up_part, down_grad)
    reduce("down_own", down_grad)
    line.step()
    leaving = back_part(grad_gate_part, grad_up_part, gate, gate_other, up, up_other, 1)
    down_away = outer_sum(activated, cot_other)
    *leaving, down_away = order(*leaving, down_away)
    down_away = swap(down_away, "col", 1)
    staying = back_part(grad_gate_part, grad_up_part, gate, gate_other, up, up_other, 0)
    plane = scatter_plane(staying, leaving)
    flight = next(plane)
    gate_grad = outer_sum(grad_gate_part, two_own)
    up_grad = outer_sum(grad_up_part, two_own)
    gate_other_grad = outer_sum(grad_gate_part, two_other)
    reduce("gate_own", gate_grad)
    *flight, up_grad, gate_other_grad = line.step(*flight, up_grad, gate_other_grad)
    grad_hidden_two = plane.send(flight)
    up_other_grad = outer_sum(grad_up_part, two_other)
    grad_hidden_two, up_other_grad = order(grad_hidden_two, up_other_grad)
    grad_norm_two, grad_gain_two = norm_backward(
        grad_hidden_two, normed_two, scale_two, gain_two, full_width
    )
    grad_middle = cotangent.astype(F32) + grad_norm_two
    branch_low = grad_middle.astype(BF)
    reduce("down_other", down_away)
    branch_low, gate_other_grad = line.step(branch_low, gate_other_grad)
    gate_away = swap(gate_other_grad, "col", 1)
    branch_all = gather_row(branch_low)
    reduce("up_own", up_grad)
    branch_all, gate_away = line.step(branch_all, gate_away)
    leaving = contract_flipped(rows_of(branch_all, 1 - column), out_weight).astype(BF)
    grad_sent = swap(leaving, "col", 1)
    grad_kept = contract_flipped(rows_of(branch_all, column), out_weight)
    out_grad = outer_sum(attended_all, branch_all)
    reduce("gate_other", gate_away)
    grad_sent, out_grad, up_other_grad = line.step(grad_sent, out_grad, up_other_grad)
    up_away = swap(up_other_grad, "col", 1)
    grad_projected = attention_backward(
        grad_kept, grad_sent, queries, kv, log_totals, cosine, sine, starts
    )
    reduce("out", out_grad)
    (grad_projected,) = line.step(grad_projected)
    projected_got = swap(grad_projected, "col", 1)
    lower = activated.shape[0] // 2
    out_staying = [contract(activated[:lower], weight).astype(BF) for weight in (down, down_other)]
    out_leaving = [contract(activated[lower:], weight).astype(BF) for weight in (down, down_other)]
    reduce("up_other", up_away)
    projected_got, *out_parts = line.step(projected_got, *out_staying, *out_leaving)
    out_plane = scatter_plane(out_parts[:2], out_parts[2:])
    out_flight = next(out_plane)
    projected_all = pair_up(grad_projected, projected_got, first_column, 0)
    qkv_grad = outer_sum(hidden_one_all, projected_all)
    grad_hidden_one = scatter_row(projected_all, lambda rows: contract_flipped(rows, qkv_weight))
    reduce("qkv", qkv_grad)
    (grad_hidden_one,) = line.step(grad_hidden_one)
    grad_norm_one, grad_gain_one = norm_backward(
        grad_hidden_one, normed_one, scale_one, gain_one, full_width
    )
    grad_inputs = grad_middle + grad_norm_one
    gain_grads = jnp.stack([grad_gain_one, grad_gain_two])
    bit = 1
    while bit < lax.axis_size("row"):
        gain_grads = gain_grads + swap(gain_grads, "row", bit)
        bit *= 2
    reduce("gains", gain_grads)
    out_flight = line.step(*out_flight, grad_inputs)
    grad_inputs = out_flight[3]
    branch = out_plane.send(out_flight[:3])
    (branch,) = line.step(branch)
    outputs = (middle + branch).astype(BF)
    line.drain()

    def rows_in(name):
        return pair_up(done[name + "_own"], done[name + "_other"], first_column, 0)

    grad_gate = rows_in("gate").T.astype(F32)
    grad_up = rows_in("up").T.astype(F32)
    grad_down = rows_in("down").astype(F32)
    grad_out = done["out"].astype(F32)
    grad_qkv = done["qkv"].astype(F32)
    gain_grads = done["gains"]
    return (
        outputs,
        grad_inputs,
        gain_grads[0],
        grad_qkv[:, :query_width],
        grad_qkv[:, query_width : query_width + pair_width],
        grad_qkv[:, query_width + pair_width :],
        grad_out,
        gain_grads[1],
        grad_gate,
        grad_up,
        grad_down,
    )


def solution(mesh):
    in_specs = (
        P(("dp", "row"), "col"),
        P("dp", None),
        P("col"),
        P("col", "row"),
        P("col", "row"),
        P("col", "row"),
        P("row", "col"),
        P("col"),
        P("col", "row"),
        P("col", "row"),
        P("row", "col"),
        P(("dp", "row"), "col"),
    )
    out_specs = (
        P(("dp", "row"), "col"),
        P(("dp", "row"), "col"),
        P("col"),
        P("col", "row"),
        P("col", "row"),
        P("col", "row"),
        P("row", "col"),
        P("col"),
        P("col", "row"),
        P("col", "row"),
        P("row", "col"),
    )
    return jax.shard_map(body, mesh=mesh, in_specs=in_specs, out_specs=out_specs, check_vma=False)
```

time: 1110 us -> 789 us (0.71)
  matrix products: 214 us -> 83.6 us
  waiting for transfers between devices: 464 us -> 342 us
  Pallas kernels: 0 us -> 81.5 us
  other arithmetic: 169 us -> 102 us
  blocking collectives: 42 us -> 0 us
  local copies, waits for them, and re-layouts: 95.1 us -> 54.6 us
    ppermute x24 -> x27, waiting for transfers between devices: 173 us -> 72.1 us  [step(): item[:3] = [stage + 1, values, lax.ppermute(values, 'dp', pairs)]]
    dot_general x11 -> x8, matrix products: 117 us -> 24.1 us  [contract(): return jnp.dot(leading, weight, preferred_element_type=F32)]
    pallas_call x0 -> x5, Pallas kernels: none -> 81.5 us  [the longest x1 22.5 us: attention_backward(): pl.pallas_call(lambda *refs: backward_kernel(*refs, anchors=len(anchors))...]
    psum x1 -> x0, blocking collectives: 42 us -> none  [body(): gain_grads = lax.psum((grad_gain_one, grad_gain_two), ('dp', 'row'))]
    another operation x6, other arithmetic: 42.7 us -> 1.13 us
    dot_general x5 -> x6, matrix products: 53.9 us -> 22 us  [contract_flipped(): lax.dot_general(leading, weight, (((1,), (1,)), ((), ())), preferred_elem...]
    unnamed x202 -> x174, local copies, waits for them, and re-layouts: 49.4 us -> 27.4 us
    ppermute x50 -> x55, waiting for transfers between devices: 290 us -> 270 us  [swap(): return lax.ppermute(values, axis, pairs)]
  transfers between devices with their start and end apart: 74 -> 82, of which waited for: 27 -> 35; matrix products, arithmetic and copies ran while one was open for 31% -> 25% of each run, Pallas kernels for 0% -> 8%
where the time goes in v2:
time: 789 us; the launch traced here: 780 us
  waiting for transfers between devices  342 us (43%)
  starting transfers between devices  113 us (14%)
  other arithmetic  102 us (13%)
  matrix products  83.6 us (11%)
  Pallas kernels  81.5 us (10%)
  local copies, waits for them, and re-layouts  54.6 us (7%)
    ppermute x55, waiting for transfers between devices, swap(): return lax.ppermute(values, axis, pairs)  270 us
    ppermute x27, waiting for transfers between devices, step(): item[:3] = [stage + 1, values, lax.ppermute(values, 'dp', pairs)]  72.1 us
    ppermute x27, starting transfers between devices, step(): item[:3] = [stage + 1, values, lax.ppermute(values, 'dp', pairs)]  60.6 us
    ppermute x55, starting transfers between devices, swap(): return lax.ppermute(values, axis, pairs)  51.9 us
    dot_general x8, matrix products, outer_sum(): lax.dot_general(leading, trailing, (((0,), (0,)), ((), ())), preferred_el...  37.4 us
    unnamed x174, local copies, waits for them, and re-layouts  27.4 us
    dot_general x8, matrix products, contract(): return jnp.dot(leading, weight, preferred_element_type=F32)  24.1 us
    pallas_call x1, Pallas kernels, attention_backward(): pl.pallas_call(lambda *refs: backward_kernel(*refs, anchors=len(anchors))...  22.5 us
  transfers between devices with their start and end apart: 82, of which 35 were waited for; matrix products, arithmetic and copies ran while one was open for 25% of the time, Pallas kernels for 8%

profile of v2, /device:TPU:0, one launch (start us, length us, event | category | flops | bytes accessed | tf_op | source)
XLA Modules:
  0.0 779.6 jit_solution(17696315893800440892)
XLA Ops:
  26.2 13.3 %collective-permute-done.1 = bf16[512,1024]{1,0:T(8,128)(2,1)} collective-permute-done((bf16[512,1024]{1,0:T(8,128)(2,1)}, bf16[512,1024]{1,0:T(8,128)(2,1)}, u32[]{:S(2)}, u32[]{:S(2)}) %collective-permute-start.1) | collective-permute-done | bytes 1048608 | tf_op jit(solution)/shard_map/ppermute | solution.py:37
  55.9 9.9 %collective-permute-done.5 = bf16[352,1024]{1,0:T(8,128)(2,1)} collective-permute-done((bf16[352,1024]{1,0:T(8,128)(2,1)S(1)}, bf16[352,1024]{1,0:T(8,128)(2,1)}, u32[]{:S(2)}, u32[]{:S(2)}) %collective-permute-start.5) | collective-permute-done | bytes 720928 | tf_op jit(solution)/shard_map/ppermute | solution.py:37
  85.3 12.7 %collective-permute-done.10 = bf16[512,704]{0,1:T(8,128)(2,1)} collective-permute-done((bf16[512,704]{0,1:T(8,128)(2,1)}, bf16[512,704]{0,1:T(8,128)(2,1)}, u32[]{:S(2)}, u32[]{:S(2)}) %collective-permute-start.10) | collective-permute-done | bytes 720928 | tf_op jit(solution)/shard_map/ppermute | solution.py:37
  106.6 12.5 %collective-permute-done.8 = bf16[512,1024]{1,0:T(8,128)(2,1)} collective-permute-done((bf16[512,1024]{1,0:T(8,128)(2,1)}, bf16[512,1024]{1,0:T(8,128)(2,1)}, u32[]{:S(2)}, u32[]{:S(2)}) %collective-permute-start.8) | collective-permute-done | bytes 1048608 | tf_op jit(solution)/shard_map/ppermute | solution.py:37
  125.4 20.7 %attention_forward.1 = (bf16[1024,512]{1,0:T(8,128)(2,1)}, bf16[1024,512]{1,0:T(8,128)(2,1)S(1)}, bf16[1024,128]{1,0:T(8,128)(2,1)S(1)}, f32[4,2,1024]{2,1,0:T(2,128)S(1)}) custom-call(f32[1024,640]{1,0:T(8,128)} %fusion.18.refs_0_.refs_2_, bf16[1024,640]{1,0:T(8,128)(2,1)} %collective-permute-done.7.refs_1_.refs_3_, f32[1024,640]{1,0:T(8,128)} %fusion.18.refs_0_.refs_2_, ...), custom_call_target="tpu_custom_call" | custom-call | flops 20000000000 | bytes 8388608 | tf_op jit(solution)/shard_map/attention_forward/pallas_call | solution.py:397
  159.0 16.6 %collective-permute-done.14 = bf16[1024,512]{1,0:T(8,128)(2,1)} collective-permute-done((bf16[1024,512]{1,0:T(8,128)(2,1)}, bf16[1024,512]{1,0:T(8,128)(2,1)}, u32[]{:S(2)}, u32[]{:S(2)}) %collective-permute-start.14) | collective-permute-done | bytes 1048608 | tf_op jit(solution)/shard_map/ppermute | solution.py:37
  208.3 14.7 %collective-permute-done.19 = bf16[512,1024]{1,0:T(8,128)(2,1)S(1)} collective-permute-done((bf16[512,1024]{1,0:T(8,128)(2,1)S(1)}, bf16[512,1024]{1,0:T(8,128)(2,1)S(1)}, u32[]{:S(2)}, u32[]{:S(2)}) %collective-permute-start.19) | collective-permute-done | bytes 1048608 | tf_op jit(solution)/shard_map/ppermute | solution.py:37
  230.8 20.3 %collective-permute-done.21 = bf16[512,1024]{1,0:T(8,128)(2,1)S(1)} collective-permute-done((bf16[512,1024]{1,0:T(8,128)(2,1)S(1)}, bf16[512,1024]{1,0:T(8,128)(2,1)S(1)}, u32[]{:S(2)}, u32[]{:S(2)}) %collective-permute-start.21) | collective-permute-done | bytes 1048608 | tf_op jit(solution)/shard_map/ppermute | solution.py:37
  254.5 9.0 %collective-permute-done.24 = bf16[256,1024]{1,0:T(8,128)(2,1)S(1)} collective-permute-done((bf16[256,1024]{1,0:T(8,128)(2,1)S(1)}, bf16[256,1024]{1,0:T(8,128)(2,1)S(1)}, u32[]{:S(2)}, u32[]{:S(2)}) %collective-permute-start.24) | collective-permute-done | bytes 524320 | tf_op jit(solution)/shard_map/ppermute | solution.py:37
  270.1 18.7 %hidden_part.1 = (bf16[2048,704]{1,0:T(8,128)(2,1)}, bf16[2048,704]{1,0:T(8,128)(2,1)}, bf16[2048,704]{1,0:T(8,128)(2,1)}) custom-call(bf16[2048,1024]{1,0:T(8,128)(2,1)} %pad_maximum_fusion.2.own_ref, bf16[2048,1024]{1,0:T(8,128)(2,1)} %copy-done.65, bf16[1024,704]{1,0:T(8,128)(2,1)S(1)} %copy-done.2, bf16[1024,704]{1,0:T(8,128)(2,1)S(1)} %copy-done.3, ...), custom_call_target="tpu_custom_call" | custom-call | flops 11811160064 | bytes 25165824 | tf_op jit(solution)/shard_map/hidden_part/pallas_call | solution.py:348
  307.5 9.8 %back_part.3 = (bf16[1024,1024]{1,0:T(8,128)(2,1)}, bf16[1024,1024]{1,0:T(8,128)(2,1)}) custom-call(bf16[2048,704]{1,0:T(8,128)(2,1)} %get-tuple-element.126.grad_gate_ref, bf16[2048,704]{1,0:T(8,128)(2,1)} %get-tuple-element.127.grad_up_ref, bf16[1024,704]{1,0:T(8,128)(2,1)S(1)} %copy-done.2, bf16[1024,704]{1,0:T(8,128)(2,1)S(1)} %copy-done.3, ...), custom_call_target="tpu_custom_call" | custom-call | flops 5905580032 | bytes 12582912 | tf_op jit(solution)/shard_map/back_part/pallas_call | solution.py:377
  327.9 9.8 %back_part.2 = (bf16[1024,1024]{1,0:T(8,128)(2,1)}, bf16[1024,1024]{1,0:T(8,128)(2,1)}) custom-call(bf16[2048,704]{1,0:T(8,128)(2,1)} %get-tuple-element.126.grad_gate_ref, bf16[2048,704]{1,0:T(8,128)(2,1)} %get-tuple-element.127.grad_up_ref, bf16[1024,704]{1,0:T(8,128)(2,1)S(1)} %copy-done.2, bf16[1024,704]{1,0:T(8,128)(2,1)S(1)} %copy-done.3, ...), custom_call_target="tpu_custom_call" | custom-call | flops 5905580032 | bytes 12582912 | tf_op jit(solution)/shard_map/back_part/pallas_call | solution.py:377
  356.7 11.8 %collective-permute-done.32 = bf16[704,1024]{1,0:T(8,128)(2,1)} collective-permute-done((bf16[704,1024]{1,0:T(8,128)(2,1)}, bf16[704,1024]{1,0:T(8,128)(2,1)}, u32[]{:S(2)}, u32[]{:S(2)}) %collective-permute-start.32) | collective-permute-done | bytes 1441824 | tf_op jit(solution)/shard_map/ppermute | solution.py:154
  378.7 35.5 %collective-permute-done.34 = bf16[256,1024]{1,0:T(8,128)(2,1)S(1)} collective-permute-done((bf16[256,1024]{1,0:T(8,128)(2,1)S(1)}, bf16[256,1024]{1,0:T(8,128)(2,1)S(1)}, u32[]{:S(2)}, u32[]{:S(2)}) %collective-permute-start.34) | collective-permute-done | bytes 524320 | tf_op jit(solution)/shard_map/ppermute | solution.py:37
  429.4 13.7 %collective-permute-done.38 = bf16[512,1024]{1,0:T(8,128)(2,1)S(1)} collective-permute-done((bf16[512,1024]{1,0:T(8,128)(2,1)S(1)}, bf16[512,1024]{1,0:T(8,128)(2,1)S(1)}, u32[]{:S(2)}, u32[]{:S(2)}) %collective-permute-start.38) | collective-permute-done | bytes 1048608 | tf_op jit(solution)/shard_map/ppermute | solution.py:37
  463.7 10.0 %collective-permute-done.41 = bf16[704,1024]{1,0:T(8,128)(2,1)S(1)} collective-permute-done((bf16[704,1024]{1,0:T(8,128)(2,1)S(1)}, bf16[704,1024]{1,0:T(8,128)(2,1)S(1)}, u32[]{:S(2)}, u32[]{:S(2)}) %collective-permute-start.41) | collective-permute-done | bytes 1441824 | tf_op jit(solution)/shard_map/ppermute | solution.py:37
  518.3 22.5 %attention_backward.1 = bf16[1024,640]{1,0:T(8,128)(2,1)S(1)} custom-call(f32[1024,512]{1,0:T(8,128)} %fusion.14.refs_0_, bf16[1024,512]{1,0:T(8,128)(2,1)S(1)} %collective-permute-done.46.refs_1_, bf16[1024,512]{1,0:T(8,128)(2,1)S(1)} %copy-done.7, bf16[1024,128]{1,0:T(8,128)(2,1)S(1)} %get-tuple-element.153.refs_3_, ...), custom_call_target="tpu_custom_call" | custom-call | flops 40000000000 | bytes 8388608 | tf_op jit(solution)/shard_map/attention_backward/pallas_call | solution.py:440
  567.5 8.8 %collective-permute-done.56 = bf16[512,1024]{1,0:T(8,128)(2,1)S(1)} collective-permute-done((bf16[512,1024]{1,0:T(8,128)(2,1)S(1)}, bf16[512,1024]{1,0:T(8,128)(2,1)S(1)}, u32[]{:S(2)}, u32[]{:S(2)}) %collective-permute-start.56) | collective-permute-done | bytes 1048608 | tf_op jit(solution)/shard_map/ppermute | solution.py:154
  576.2 15.4 %collective-permute-done.53 = bf16[1024,640]{1,0:T(8,128)(2,1)S(1)} collective-permute-done((bf16[1024,640]{1,0:T(8,128)(2,1)S(1)}, bf16[1024,640]{1,0:T(8,128)(2,1)S(1)}, u32[]{:S(2)}, u32[]{:S(2)}) %collective-permute-start.53) | collective-permute-done | bytes 1310752 | tf_op jit(solution)/shard_map/ppermute | solution.py:37
  601.1 14.2 %collective-permute-done.66 = bf16[704,1024]{1,0:T(8,128)(2,1)S(1)} collective-permute-done((bf16[704,1024]{1,0:T(8,128)(2,1)S(1)}, bf16[704,1024]{1,0:T(8,128)(2,1)S(1)}, u32[]{:S(2)}, u32[]{:S(2)}) %collective-permute-start.66) | collective-permute-done | bytes 1441824 | tf_op jit(solution)/shard_map/ppermute | solution.py:37
  636.3 16.3 %collective-permute-done.63 = bf16[512,1024]{1,0:T(8,128)(2,1)S(1)} collective-permute-done((bf16[512,1024]{1,0:T(8,128)(2,1)S(1)}, bf16[512,1024]{1,0:T(8,128)(2,1)S(1)}, u32[]{:S(2)}, u32[]{:S(2)}) %collective-permute-start.63) | collective-permute-done | bytes 1048608 | tf_op jit(solution)/shard_map/ppermute | solution.py:37
  661.9 14.8 %collective-permute-done.68 = f32[512,1]{0,1:T(1,128)S(1)} collective-permute-done((f32[512,1]{0,1:T(1,128)S(1)}, f32[512,1]{0,1:T(1,128)S(1)}, u32[]{:S(2)}, u32[]{:S(2)}) %collective-permute-start.68) | collective-permute-done | bytes 2080 | tf_op jit(solution)/shard_map/ppermute | solution.py:37
  684.3 10.4 %collective-permute-done.61 = bf16[256,1024]{1,0:T(8,128)(2,1)S(1)} collective-permute-done((bf16[256,1024]{1,0:T(8,128)(2,1)S(1)}, bf16[256,1024]{1,0:T(8,128)(2,1)S(1)}, u32[]{:S(2)}, u32[]{:S(2)}) %collective-permute-start.61) | collective-permute-done | bytes 524320 | tf_op jit(solution)/shard_map/ppermute | solution.py:37
  760.3 12.5 %collective-permute-done.79 = bf16[1024,640]{0,1:T(8,128)(2,1)S(1)} collective-permute-done((bf16[1024,640]{0,1:T(8,128)(2,1)}, bf16[1024,640]{0,1:T(8,128)(2,1)S(1)}, u32[]{:S(2)}, u32[]{:S(2)}) %collective-permute-start.79) | collective-permute-done | bytes 1310752 | tf_op jit(solution)/shard_map/ppermute | solution.py:154
  (474 shorter events, 422.6 us)
Async XLA Ops:
  25.1 40.8 %collective-permute-start.5 = (bf16[352,1024]{1,0:T(8,128)(2,1)S(1)}, bf16[352,1024]{1,0:T(8,128)(2,1)}, u32[]{:S(2)}, u32[]{:S(2)}) collective-permute-start(bf16[352,1024]{1,0:T(8,128)(2,1)S(1)} %slice_select_fusion.2), channel_id=1, source_target_pairs={{0,1},{1,0},{2,3},{3,2},{4,5},{5,4},{6,7},{7,6},{8,9},{9,8},{10,11... | collective-permute-start | bytes 2162696 | tf_op jit(solution)/shard_map/ppermute | solution.py:37
  65.9 36.0 %collective-permute-start.11 = (bf16[352,1024]{1,0:T(8,128)(2,1)}, bf16[352,1024]{1,0:T(8,128)(2,1)}, u32[]{:S(2)}, u32[]{:S(2)}) collective-permute-start(bf16[352,1024]{1,0:T(8,128)(2,1)} %collective-permute-done.5), channel_id=1, source_target_pairs={{0,8},{8,0},{16,24},{24,16},{1,9},{9,1},{17,25},{25,17},{2,10},{10... | collective-permute-start | bytes 2162696 | tf_op jit(solution)/shard_map/ppermute | solution.py:37
  67.9 51.3 %collective-permute-start.7 = (bf16[1024,640]{1,0:T(8,128)(2,1)}, bf16[1024,640]{1,0:T(8,128)(2,1)}, u32[]{:S(2)}, u32[]{:S(2)}) collective-permute-start(bf16[1024,640]{1,0:T(8,128)(2,1)} %fusion.20), channel_id=1, source_target_pairs={{0,1},{1,0},{2,3},{3,2},{4,5},{5,4},{6,7},{7,6},{8,9},{9,8},{10,11... | collective-permute-start | bytes 3932168 | tf_op jit(solution)/shard_map/ppermute | solution.py:37
  78.0 41.1 %collective-permute-start.8 = (bf16[512,1024]{1,0:T(8,128)(2,1)}, bf16[512,1024]{1,0:T(8,128)(2,1)}, u32[]{:S(2)}, u32[]{:S(2)}) collective-permute-start(bf16[512,1024]{1,0:T(8,128)(2,1)} %param.23), channel_id=1, source_target_pairs={{0,1},{1,0},{2,3},{3,2},{4,5},{5,4},{6,7},{7,6},{8,9},{9,8},{10,11... | collective-permute-start | bytes 3145736 | tf_op jit(solution)/shard_map/ppermute | solution.py:37
  79.5 39.6 %collective-permute-start.9 = (bf16[512,1024]{1,0:T(8,128)(2,1)}, bf16[512,1024]{1,0:T(8,128)(2,1)}, u32[]{:S(2)}, u32[]{:S(2)}) collective-permute-start(bf16[512,1024]{1,0:T(8,128)(2,1)} %param.23), channel_id=1, source_target_pairs={{0,4},{2,6},{4,0},{6,2},{1,5},{3,7},{5,1},{7,3},{8,12},{10,14},{12... | collective-permute-start | bytes 3145736 | tf_op jit(solution)/shard_map/ppermute | solution.py:37
  98.0 55.9 %collective-permute-start.15 = (bf16[512,704]{0,1:T(8,128)(2,1)}, bf16[512,704]{0,1:T(8,128)(2,1)}, u32[]{:S(2)}, u32[]{:S(2)}) collective-permute-start(bf16[512,704]{0,1:T(8,128)(2,1)} %collective-permute-done.6), channel_id=1, source_target_pairs={{0,8},{8,0},{16,24},{24,16},{1,9},{9,1},{17,25},{25,17},{2,10},{10... | collective-permute-start | bytes 2162696 | tf_op jit(solution)/shard_map/ppermute | solution.py:37
  125.4 52.2 %collective-permute-start.16 = (bf16[1024,1024]{1,0:T(8,128)(2,1)}, bf16[1024,1024]{1,0:T(8,128)(2,1)}, u32[]{:S(2)}, u32[]{:S(2)}) collective-permute-start(bf16[1024,1024]{1,0:T(8,128)(2,1)} %pad_maximum_fusion.5), channel_id=1, source_target_pairs={{0,2},{2,0},{4,6},{6,4},{1,3},{3,1},{5,7},{7,5},{8,10},{10,8},{12,... | collective-permute-start | bytes 6291464 | tf_op jit(solution)/shard_map/ppermute | solution.py:37
  302.9 117.1 %collective-permute-start.37 = (bf16[704,1024]{1,0:T(8,128)(2,1)S(1)}, bf16[704,1024]{1,0:T(8,128)(2,1)}, u32[]{:S(2)}, u32[]{:S(2)}) collective-permute-start(bf16[704,1024]{1,0:T(8,128)(2,1)S(1)} %convolution_convert_fusion.6), channel_id=1, source_target_pairs={{0,8},{24,16},{1,9},{25,17},{2,10},{26,18},{3,11},{27,19},{4,12},{... | collective-permute-start | bytes 4325384 | tf_op jit(solution)/shard_map/ppermute | solution.py:154
  317.8 50.7 %collective-permute-start.32 = (bf16[704,1024]{1,0:T(8,128)(2,1)}, bf16[704,1024]{1,0:T(8,128)(2,1)}, u32[]{:S(2)}, u32[]{:S(2)}) collective-permute-start(bf16[704,1024]{1,0:T(8,128)(2,1)} %convolution_convert_fusion.11), channel_id=1, source_target_pairs={{0,8},{24,16},{1,9},{25,17},{2,10},{26,18},{3,11},{27,19},{4,12},{... | collective-permute-start | bytes 4325384 | tf_op jit(solution)/shard_map/ppermute | solution.py:154
  368.5 53.1 %collective-permute-start.44 = (bf16[704,1024]{1,0:T(8,128)(2,1)S(1)}, bf16[704,1024]{1,0:T(8,128)(2,1)S(1)}, u32[]{:S(2)}, u32[]{:S(2)}) collective-permute-start(bf16[704,1024]{1,0:T(8,128)(2,1)S(1)} %copy-done.76), channel_id=1, source_target_pairs={{0,1},{1,0},{2,3},{3,2},{4,5},{5,4},{6,7},{7,6},{8,9},{9,8},{10,11... | collective-permute-start | bytes 4325384 | tf_op jit(solution)/shard_map/ppermute | solution.py:37
  373.9 40.3 %collective-permute-start.34 = (bf16[256,1024]{1,0:T(8,128)(2,1)S(1)}, bf16[256,1024]{1,0:T(8,128)(2,1)S(1)}, u32[]{:S(2)}, u32[]{:S(2)}) collective-permute-start(bf16[256,1024]{1,0:T(8,128)(2,1)S(1)} %fusion.38), channel_id=1, source_target_pairs={{0,1},{1,0},{2,3},{3,2},{4,5},{5,4},{6,7},{7,6},{8,9},{9,8},{10,11... | collective-permute-start | bytes 1572872 | tf_op jit(solution)/shard_map/ppermute | solution.py:37
  375.2 39.3 %collective-permute-start.33 = (bf16[256,1024]{1,0:T(8,128)(2,1)S(1)}, bf16[256,1024]{1,0:T(8,128)(2,1)S(1)}, u32[]{:S(2)}, u32[]{:S(2)}) collective-permute-start(bf16[256,1024]{1,0:T(8,128)(2,1)S(1)} %fusion.43), channel_id=1, source_target_pairs={{0,4},{2,6},{4,0},{6,2},{1,5},{3,7},{5,1},{7,3},{8,12},{10,14},{12... | collective-permute-start | bytes 1572872 | tf_op jit(solution)/shard_map/ppermute | solution.py:37
  378.0 42.0 %collective-permute-start.36 = (bf16[704,1024]{1,0:T(8,128)(2,1)S(1)}, bf16[704,1024]{1,0:T(8,128)(2,1)S(1)}, u32[]{:S(2)}, u32[]{:S(2)}) collective-permute-start(bf16[704,1024]{1,0:T(8,128)(2,1)S(1)} %add_convert_fusion.12), channel_id=1, source_target_pairs={{8,16},{16,8},{9,17},{17,9},{10,18},{18,10},{11,19},{19,11},{12,20... | collective-permute-start | bytes 4325384 | tf_op jit(solution)/shard_map/ppermute | solution.py:154
  428.1 35.6 %collective-permute-start.42 = (bf16[704,1024]{1,0:T(8,128)(2,1)S(1)}, bf16[704,1024]{1,0:T(8,128)(2,1)S(1)}, u32[]{:S(2)}, u32[]{:S(2)}) collective-permute-start(bf16[704,1024]{1,0:T(8,128)(2,1)S(1)} %add_convert_fusion.11), channel_id=1, source_target_pairs={{8,0},{16,24},{9,1},{17,25},{10,2},{18,26},{11,3},{19,27},{12,4},{... | collective-permute-start | bytes 4325384 | tf_op jit(solution)/shard_map/ppermute | solution.py:154
  447.3 49.4 %collective-permute-start.49 = (bf16[704,1024]{1,0:T(8,128)(2,1)}, bf16[704,1024]{1,0:T(8,128)(2,1)}, u32[]{:S(2)}, u32[]{:S(2)}) collective-permute-start(bf16[704,1024]{1,0:T(8,128)(2,1)} %convolution_convert_fusion.9), channel_id=1, source_target_pairs={{0,8},{24,16},{1,9},{25,17},{2,10},{26,18},{3,11},{27,19},{4,12},{... | collective-permute-start | bytes 4325384 | tf_op jit(solution)/shard_map/ppermute | solution.py:154
  484.1 56.7 %collective-permute-start.52 = (bf16[704,1024]{1,0:T(8,128)(2,1)}, bf16[704,1024]{1,0:T(8,128)(2,1)S(1)}, u32[]{:S(2)}, u32[]{:S(2)}) collective-permute-start(bf16[704,1024]{1,0:T(8,128)(2,1)} %copy-done.51), channel_id=1, source_target_pairs={{0,8},{24,16},{1,9},{25,17},{2,10},{26,18},{3,11},{27,19},{4,12},{... | collective-permute-start | bytes 4325384 | tf_op jit(solution)/shard_map/ppermute | solution.py:154
  547.9 43.8 %collective-permute-start.55 = (bf16[704,1024]{1,0:T(8,128)(2,1)S(1)}, bf16[704,1024]{1,0:T(8,128)(2,1)S(1)}, u32[]{:S(2)}, u32[]{:S(2)}) collective-permute-start(bf16[704,1024]{1,0:T(8,128)(2,1)S(1)} %add_convert_fusion.4), channel_id=1, source_target_pairs={{8,16},{16,8},{9,17},{17,9},{10,18},{18,10},{11,19},{19,11},{12,20... | collective-permute-start | bytes 4325384 | tf_op jit(solution)/shard_map/ppermute | solution.py:154
  549.4 42.3 %collective-permute-start.54 = (bf16[704,1024]{1,0:T(8,128)(2,1)S(1)}, bf16[704,1024]{1,0:T(8,128)(2,1)}, u32[]{:S(2)}, u32[]{:S(2)}) collective-permute-start(bf16[704,1024]{1,0:T(8,128)(2,1)S(1)} %add_convert_fusion.5), channel_id=1, source_target_pairs={{8,0},{16,24},{9,1},{17,25},{10,2},{18,26},{11,3},{19,27},{12,4},{... | collective-permute-start | bytes 4325384 | tf_op jit(solution)/shard_map/ppermute | solution.py:154
  566.9 48.4 %collective-permute-start.66 = (bf16[704,1024]{1,0:T(8,128)(2,1)S(1)}, bf16[704,1024]{1,0:T(8,128)(2,1)S(1)}, u32[]{:S(2)}, u32[]{:S(2)}) collective-permute-start(bf16[704,1024]{1,0:T(8,128)(2,1)S(1)} %copy-done.74), channel_id=1, source_target_pairs={{0,1},{1,0},{2,3},{3,2},{4,5},{5,4},{6,7},{7,6},{8,9},{9,8},{10,11... | collective-permute-start | bytes 4325384 | tf_op jit(solution)/shard_map/ppermute | solution.py:37
  615.3 39.3 %collective-permute-start.67 = (bf16[704,1024]{1,0:T(8,128)(2,1)S(1)}, bf16[704,1024]{1,0:T(8,128)(2,1)S(1)}, u32[]{:S(2)}, u32[]{:S(2)}) collective-permute-start(bf16[704,1024]{1,0:T(8,128)(2,1)S(1)} %collective-permute-done.66), channel_id=1, source_target_pairs={{0,8},{24,16},{1,9},{25,17},{2,10},{26,18},{3,11},{27,19},{4,12},{... | collective-permute-start | bytes 4325384 | tf_op jit(solution)/shard_map/ppermute | solution.py:154
  617.3 37.3 %collective-permute-start.65 = (bf16[512,1024]{1,0:T(8,128)(2,1)S(1)}, bf16[512,1024]{1,0:T(8,128)(2,1)S(1)}, u32[]{:S(2)}, u32[]{:S(2)}) collective-permute-start(bf16[512,1024]{1,0:T(8,128)(2,1)S(1)} %add_convert_fusion.17), channel_id=1, source_target_pairs={{8,16},{16,8},{9,17},{17,9},{10,18},{18,10},{11,19},{19,11},{12,20... | collective-permute-start | bytes 3145736 | tf_op jit(solution)/shard_map/ppermute | solution.py:154
  630.6 49.2 %collective-permute-start.71 = (bf16[1024,640]{0,1:T(8,128)(2,1)S(1)}, bf16[1024,640]{0,1:T(8,128)(2,1)S(1)}, u32[]{:S(2)}, u32[]{:S(2)}) collective-permute-start(bf16[1024,640]{0,1:T(8,128)(2,1)S(1)} %convolution_convert_fusion.12), channel_id=1, source_target_pairs={{0,8},{24,16},{1,9},{25,17},{2,10},{26,18},{3,11},{27,19},{4,12},{... | collective-permute-start | bytes 3932168 | tf_op jit(solution)/shard_map/ppermute | solution.py:154
  652.6 50.5 %collective-permute-start.59 = (bf16[2,256,1024]{2,1,0:T(8,128)(2,1)S(1)}, bf16[2,256,1024]{2,1,0:T(8,128)(2,1)S(1)}, u32[]{:S(2)}, u32[]{:S(2)}) collective-permute-start(bf16[2,256,1024]{2,1,0:T(8,128)(2,1)S(1)} %slice.211), channel_id=1, source_target_pairs={{0,1},{1,0},{2,3},{3,2},{4,5},{5,4},{6,7},{7,6},{8,9},{9,8},{10,11... | collective-permute-start | bytes 3145736 | tf_op jit(solution)/shard_map/ppermute | solution.py:37
  659.2 44.0 %collective-permute-start.70 = (bf16[704,1024]{1,0:T(8,128)(2,1)S(1)}, bf16[704,1024]{1,0:T(8,128)(2,1)S(1)}, u32[]{:S(2)}, u32[]{:S(2)}) collective-permute-start(bf16[704,1024]{1,0:T(8,128)(2,1)S(1)} %add_convert_fusion.2), channel_id=1, source_target_pairs={{8,16},{16,8},{9,17},{17,9},{10,18},{18,10},{11,19},{19,11},{12,20... | collective-permute-start | bytes 4325384 | tf_op jit(solution)/shard_map/ppermute | solution.py:154
  (141 other events, 2311.3 us)

commit v3 on v2

--- a/solution.py
+++ b/solution.py
@@ -49,47 +49,42 @@
     return jnp.concatenate([jnp.where(first, own, other), jnp.where(first, other, own)], axis)
 
 
-def gather_row(block):
-    size = lax.axis_size("row")
-    blocks = {0: block}
-    bit = size // 2
-    while bit:
-        for offset in list(blocks):
-            blocks[offset | bit] = swap(blocks[offset], "row", bit)
-        bit //= 2
+def gather_row(block, between=lambda far: far):
     me = lax.axis_index("row")
-    whole = jnp.zeros((size * block.shape[0],) + block.shape[1:], block.dtype)
-    for offset, part in blocks.items():
-        whole = lax.dynamic_update_slice_in_dim(whole, part, (me ^ offset) * block.shape[0], 0)
-    return whole
-
-
-def scatter_row(leading, product):
+    far = swap(block, "row", 2)
+    sibling = swap(block, "row", 1)
+    far = between(far)
+    even = (me & 1) == 0
+    near_pair = pair_up(block, sibling, even, 0)
+    far_pair = pair_up(far, swap(far, "row", 1), even, 0)
+    mine = (me >> 1) == lax.axis_index("col")
+    return jnp.where(mine, near_pair, far_pair), jnp.where(mine, far_pair, near_pair)
+
+
+def scatter_row(sequences, product):
     me = lax.axis_index("row")
-    block = leading.shape[0] // 4
-    split = leading.reshape(2, 2, block, leading.shape[1])
-    sent = product(pick(split, 1 - (me & 1), 1).reshape(2 * block, -1)).astype(BF)
+    parity = me & 1
+    block = sequences[0].shape[0] // 2
+
+    def rows(index):
+        parts = [lax.dynamic_slice_in_dim(rows, index * block, block, 0) for rows in sequences]
+        return jnp.concatenate(parts, 0)
+
+    sent = product(rows(1 - parity)).astype(BF)
     arrived = swap(sent, "row", 1)
-    kept = product(pick(split, me & 1, 1).reshape(2 * block, -1))
+    kept = product(rows(parity))
     both = (kept + arrived.astype(F32)).reshape(2, block, -1)
-    return pick(both, me >> 1, 0) + swap(
-        pick(both, 1 - (me >> 1), 0).astype(BF), "row", 2
-    ).astype(F32)
+    where = (me >> 1) ^ lax.axis_index("col")
+    return pick(both, where, 0) + swap(pick(both, 1 - where, 0).astype(BF), "row", 2).astype(F32)
 
 
 def gather_plane(block):
     half = block.shape[0] // 2
-    across, along = yield (swap(block, "col", 1), swap(block, "row", 2))
-    corner_first, corner_second = yield (
-        swap(along[:half], "col", 1),
-        swap(across[half:], "row", 2),
-    )
+    across, along = swap(block, "col", 1), swap(block, "row", 2)
+    corner = swap(along[:half], "col", 1), swap(across[half:], "row", 2)
     own = jnp.concatenate([block, along], 0)
-    other = jnp.concatenate([across, corner_first, corner_second], 0)
-    yield (
-        jnp.concatenate([own, swap(own, "row", 1)], 0),
-        jnp.concatenate([other, swap(other, "row", 1)], 0),
-    )
+    other = jnp.concatenate([across, *corner], 0)
+    return (own, swap(own, "row", 1)), (other, swap(other, "row", 1))
 
 
 def scatter_plane(kept, sent):
@@ -100,59 +95,69 @@
     ]
     half = own.shape[1] // 2
     first_own, first_other = own[:, :half], other[:, :half].astype(BF)
-    second_own, second_other = own[:, half:], other[:, half:]
-    first_got = swap(first_other, "col", 1)
-    second_got_own = swap(second_own[1].astype(BF), "row", 2)
-    second_got_other = swap(second_other[1].astype(BF), "row", 2)
-    first_got, second_got_own, second_got_other = yield (
-        first_got,
-        second_got_own,
-        second_got_other,
-    )
+    second_own, second_other = own[0, half:], other[0, half:]
+    leaving = first_other, own[1, half:].astype(BF), other[1, half:].astype(BF)
+    leaving = yield leaving
+    got = swap(leaving[0], "col", 1), swap(leaving[1], "row", 2), swap(leaving[2], "row", 2)
+    first_got, second_got_own, second_got_other = yield got
     first_sum = first_own + first_got.astype(F32)
-    second_mine = second_own[0] + second_got_own.astype(F32)
-    second_theirs = (second_other[0] + second_got_other.astype(F32)).astype(BF)
+    second_mine = second_own + second_got_own.astype(F32)
+    second_theirs = (second_other + second_got_other.astype(F32)).astype(BF)
     first_sum = first_sum[0] + swap(first_sum[1].astype(BF), "row", 2).astype(F32)
     second_sum = second_mine + swap(second_theirs, "col", 1).astype(F32)
     yield jnp.concatenate([first_sum, second_sum], 0)
 
 
+def scatter_late(own, across):
+    both = (own + across.astype(F32)).reshape(2, -1, own.shape[1])
+    return both[0] + swap(both[1].astype(BF), "row", 2).astype(F32)
+
+
 def order(*values):
     return lax.optimization_barrier(values)
 
 
 class LineSum:
+    stages = ([(0, 1), (3, 2)], [(1, 2), (2, 1)], [(1, 0), (2, 3)])
+
     def __init__(self):
         self.line = lax.axis_size("dp") == 4
         self.flight = []
 
     def add(self, values, finish):
         if self.line:
-            self.flight.append([0, values, None, finish])
+            self.flight.append([1, values, lax.ppermute(values, "dp", self.stages[0]), finish])
         else:
-            if values.dtype == F32:
-                finish(lax.psum(values, "dp"))
-                return
             mine = lax.psum_scatter(values, "dp", scatter_dimension=0, tiled=True)
             finish(lax.all_gather(mine, "dp", axis=0, tiled=True))
 
-    def step(self, *anchors):
-        moving = [item for item in self.flight if item[2] is not None]
-        results = order(*anchors, *[item[2] for item in moving])
-        for item, got in zip(moving, results[len(anchors) :]):
-            item[2] = got
+    def step(self, *anchors, late=()):
+        moving = list(self.flight)
+        results = order(*anchors, *late, *[item[2] for item in moving])
+        kept, late, got = (
+            results[: len(anchors)],
+            results[len(anchors) : len(anchors) + len(late)],
+            results[len(anchors) + len(late) :],
+        )
         place = lax.axis_index("dp")
-        for item in list(self.flight):
-            stage, values, got, finish = item
+        going = []
+        for item, arrived in zip(moving, got):
+            stage, values, _, finish = item
             if stage == 3:
-                finish(jnp.where((place == 0) | (place == 3), got, values))
+                finish(jnp.where((place == 0) | (place == 3), arrived, values))
                 self.flight.remove(item)
                 continue
-            if stage:
-                values = (values.astype(F32) + got.astype(F32)).astype(values.dtype)
-            pairs = ([(0, 1), (3, 2)], [(1, 2), (2, 1)], [(1, 0), (2, 3)])[stage]
-            item[:3] = [stage + 1, values, lax.ppermute(values, "dp", pairs)]
-        return results[: len(anchors)]
+            item[1] = (values.astype(F32) + arrived.astype(F32)).astype(values.dtype)
+            going.append(item)
+        if late:
+            results = order(*late, *[item[1] for item in going])
+            late = results[: len(late)]
+            for item, values in zip(going, results[len(late) :]):
+                item[1] = values
+        for item in going:
+            item[2] = lax.ppermute(item[1], "dp", self.stages[item[0]])
+            item[0] += 1
+        return (*kept, *late)
 
     def drain(self):
         while self.flight:
@@ -326,37 +331,52 @@
 
 
 def hidden_kernel(
-    own_ref, other_ref, gate_ref, gate_other_ref, up_ref, up_other_ref, given_ref,
+    own_ref, own_sibling_ref, other_ref, other_sibling_ref,
+    gate_ref, gate_other_ref, up_ref, up_other_ref, given_ref,
     act_ref, grad_gate_ref, grad_up_ref,
 ):
-    own, other = own_ref[...], other_ref[...]
-    gate = dot_nn(own, gate_ref[...]) + dot_nn(other, gate_other_ref[...])
-    up = dot_nn(own, up_ref[...]) + dot_nn(other, up_other_ref[...])
-    given = given_ref[...].astype(F32)
-    bent = 1.0 / (1.0 + jnp.exp(-gate))
-    silu = gate * bent
-    act_ref[...] = (silu * up).astype(BF)
-    grad_gate_ref[...] = (given * up * bent * (1.0 + gate * (1.0 - bent))).astype(BF)
-    grad_up_ref[...] = (given * silu).astype(BF)
+    def tile(own_ref, other_ref):
+        own, other = own_ref[...], other_ref[...]
+        gate = dot_nn(own, gate_ref[...]) + dot_nn(other, gate_other_ref[...])
+        up = dot_nn(own, up_ref[...]) + dot_nn(other, up_other_ref[...])
+        given = given_ref[...].astype(F32)
+        bent = 1.0 / (1.0 + jnp.exp(-gate))
+        silu = gate * bent
+        act_ref[...] = (silu * up).astype(BF)
+        grad_gate_ref[...] = (given * up * bent * (1.0 + gate * (1.0 - bent))).astype(BF)
+        grad_up_ref[...] = (given * silu).astype(BF)
+
+    near = pl.program_id(0) < pl.num_programs(0) // 2
+
+    @pl.when(near)
+    def _():
+        tile(own_ref, other_ref)
+
+    @pl.when(jnp.logical_not(near))
+    def _():
+        tile(own_sibling_ref, other_sibling_ref)
 
 
 def hidden_part(own, other, gate, gate_other, up, up_other, given):
-    tokens, width = own.shape
-    hidden = gate.shape[1]
-    rows = lambda columns: pl.BlockSpec((ROWS, columns), lambda i: (i, 0))
+    tokens, hidden = given.shape
+    width = gate.shape[0]
+    half = tokens // ROWS // 2
+    rows = pl.BlockSpec((ROWS, hidden), lambda i: (i, 0))
+    near = pl.BlockSpec((ROWS, width), lambda i: (jnp.minimum(i, half - 1), 0))
+    sibling = pl.BlockSpec((ROWS, width), lambda i: (jnp.maximum(i - half, 0), 0))
     whole = pl.BlockSpec((width, hidden), lambda i: (0, 0))
     return pl.pallas_call(
         hidden_kernel,
-        grid=(tokens // ROWS,),
-        in_specs=[rows(width), rows(width), whole, whole, whole, whole, rows(hidden)],
-        out_specs=[rows(hidden)] * 3,
+        grid=(2 * half,),
+        in_specs=[near, sibling, near, sibling, whole, whole, whole, whole, rows],
+        out_specs=[rows] * 3,
         out_shape=[jax.ShapeDtypeStruct((tokens, hidden), BF)] * 3,
         compiler_params=pltpu.CompilerParams(vmem_limit_bytes=VMEM),
         cost_estimate=pl.CostEstimate(
             flops=8 * tokens * width * hidden, bytes_accessed=24 * 2**20, transcendentals=0
         ),
         name="hidden_part",
-    )(own, other, gate, gate_other, up, up_other, given)
+    )(*own, *other, gate, gate_other, up, up_other, given)
 
 
 def back_kernel(grad_gate_ref, grad_up_ref, gate_ref, gate_other_ref, up_ref, up_other_ref, own_ref, other_ref):
@@ -506,32 +526,36 @@
     even = lax.axis_size("dp") % 2 == 0
     low_plane = (lax.axis_index("dp") & 1) == 0
 
-    def cross(sent):
+    def half_of(sent):
         if not even:
-            return swap(sent, "col", 1)
+            return sent
         half = sent.shape[0] // 2
-        return swap(jnp.where(low_plane, sent[:half], sent[half:]), "col", 1)
+        return jnp.where(low_plane, sent[:half], sent[half:])
 
     def share(got):
-        if not even:
-            return got
-        return pair_up(got, swap(got, "dp", 1), low_plane, 0)
-
-    def rows_of(whole, index):
-        return lax.dynamic_slice_in_dim(whole, index * local_tokens, local_tokens, 0)
-
-    def gather_col(block):
-        return pair_up(block, swap(block, "col", 1), first_column, 0)
+        return swap(got, "dp", 1) if even else got
+
+    def shared(got, more):
+        return pair_up(got, more, low_plane, 0) if even else got
 
     features = inputs.astype(F32)
     gain_one = norm1_gain.astype(F32)
     gain_two = norm2_gain.astype(F32)
     normed_one, scale_one, hidden_one = norm_forward(features, gain_one, full_width)
-    hidden_one_all = gather_row(hidden_one)
     gate, gate_sent = cut(gate_weight, 1)
     up, up_sent = cut(up_weight, 1)
     down, down_sent = cut(down_weight, 0)
-    gate_got, down_got, up_got = cross(gate_sent), cross(down_sent), cross(up_sent)
+    gate_got, down_got, up_got = [
+        swap(half_of(part), "col", 1) for part in (gate_sent, down_sent, up_sent)
+    ]
+
+    def beside_gather(far):
+        nonlocal gate_got
+        far, gate_got = order(far, gate_got)
+        return far
+
+    one_mine, one_other = gather_row(hidden_one, beside_gather)
+    one_other, down_got = order(one_other, down_got)
 
     qkv_weight = jnp.concatenate([query_weight, key_weight, value_weight], 1)
     local_segments = lax.dynamic_slice_in_dim(segments, column * per_column, per_column, 0)
@@ -539,32 +563,39 @@
     cosine, sine = rotary_tables(positions)
     starts = (jnp.arange(seq_length, dtype=jnp.int32) - positions)[:, None, :]
 
-    hidden_one_all, gate_got = order(hidden_one_all, gate_got)
-    leaving = contract(rows_of(hidden_one_all, 1 - column), qkv_weight).astype(BF)
-    leaving, cotangent, down_got, up_got = order(leaving, cotangent, down_got, up_got)
+    leaving = contract(one_other, qkv_weight).astype(BF)
+    leaving, cotangent = order(leaving, cotangent)
     sent = swap(leaving, "col", 1)
-    kept = contract(rows_of(hidden_one_all, column), qkv_weight)
-    cot_plane = gather_plane(cotangent)
-    cot_flight = next(cot_plane)
-    kept, sent, *cot_flight = order(kept, sent, *cot_flight)
-    cot_flight = cot_plane.send(cot_flight)
-    gate_other, down_other, up_other = share(gate_got), share(down_got), share(up_got)
+    kept = contract(one_mine, qkv_weight)
+    along = swap(cotangent, "row", 2)
+    kept, sent, along, up_got, cotangent = order(kept, sent, along, up_got, cotangent)
+    across = swap(cotangent, "col", 1)
+    gate_more, down_more, up_more = share(gate_got), share(down_got), share(up_got)
     attended, queries, kv, log_totals = attention_forward(kept, sent, cosine, sine, starts)
-    attended, gate_other, down_other, *cot_flight = order(
-        attended, gate_other, down_other, *cot_flight
-    )
-    cot_own, cot_other = cot_plane.send(cot_flight)
-    attended_all = gather_col(attended)
-    attended_all, up_other, cot_own, cot_other = order(attended_all, up_other, cot_own, cot_other)
-    attn_branch = scatter_row(attended_all, lambda rows: contract(rows, out_weight))
+    attended, across, gate_more, down_more = order(attended, across, gate_more, down_more)
+    half = cotangent.shape[0] // 2
+    corner_second = swap(across[half:], "row", 2)
+    cot_near = jnp.concatenate([cotangent, along], 0)
+    cot_own = jnp.concatenate([cot_near, swap(cot_near, "row", 1)], 0)
+    attended_got = swap(attended, "col", 1)
+    attended_got, corner_second, along, up_more = order(attended_got, corner_second, along, up_more)
+
+    corner = [swap(along[:half], "col", 1), corner_second]
+    attn_branch = scatter_row((attended, attended_got), lambda rows: contract(rows, out_weight))
+    gate_other = shared(gate_got, gate_more)
+    down_other = shared(down_got, down_more)
+    up_other = shared(up_got, up_more)
+    cot_near = jnp.concatenate([across, *corner], 0)
+    cot_other = jnp.concatenate([cot_near, swap(cot_near, "row", 1)], 0)
     grad_activated = (
         contract_flipped(cot_own, down) + contract_flipped(cot_other, down_other)
     ).astype(BF)
-    attn_branch, grad_activated = order(attn_branch, grad_activated)
+    attn_branch, grad_activated, gate_other, up_other, cot_own, cot_other = order(
+        attn_branch, grad_activated, gate_other, up_other, cot_own, cot_other
+    )
     middle = features + attn_branch
     normed_two, scale_two, hidden_two = norm_forward(middle, gain_two, full_width)
-    two_plane = gather_plane(hidden_two)
-    two_own, two_other = two_plane.send(two_plane.send(next(two_plane)))
+    two_own, two_other = gather_plane(hidden_two)
     activated, grad_gate_part, grad_up_part = hidden_part(
         two_own, two_other, gate, gate_other, up, up_other, grad_activated
     )
@@ -575,75 +606,100 @@
         line.add(values, lambda total: done.__setitem__(name, total))
 
     down_grad = outer_sum(activated, cot_own)
-    grad_gate_part, grad_up_part, down_grad = order(grad_gate_part, grad_up_part, down_grad)
+    down_away = outer_sum(activated, cot_other)
+    grad_gate_part, grad_up_part, down_grad, down_away = order(
+        grad_gate_part, grad_up_part, down_grad, down_away
+    )
     reduce("down_own", down_grad)
-    line.step()
+    down_away = swap(down_away, "col", 1)
     leaving = back_part(grad_gate_part, grad_up_part, gate, gate_other, up, up_other, 1)
-    down_away = outer_sum(activated, cot_other)
-    *leaving, down_away = order(*leaving, down_away)
-    down_away = swap(down_away, "col", 1)
     staying = back_part(grad_gate_part, grad_up_part, gate, gate_other, up, up_other, 0)
     plane = scatter_plane(staying, leaving)
-    flight = next(plane)
-    gate_grad = outer_sum(grad_gate_part, two_own)
-    up_grad = outer_sum(grad_up_part, two_own)
-    gate_other_grad = outer_sum(grad_gate_part, two_other)
+    *plane_leaving, down_away, grad_gate_part, grad_up_part, activated = order(
+        *next(plane), down_away, grad_gate_part, grad_up_part, activated
+    )
+    flight = plane.send(plane_leaving)
+    down_away, grad_gate_part, grad_up_part = line.step(down_away, grad_gate_part, grad_up_part)
+    reduce("down_other", down_away)
+    own = jnp.concatenate(two_own, 0)
+    other = jnp.concatenate(two_other, 0)
+    gate_grad = outer_sum(grad_gate_part, own)
+    gate_other_grad = outer_sum(grad_gate_part, other)
+    *flight, gate_grad = line.step(*flight, gate_grad)
     reduce("gate_own", gate_grad)
-    *flight, up_grad, gate_other_grad = line.step(*flight, up_grad, gate_other_grad)
     grad_hidden_two = plane.send(flight)
-    up_other_grad = outer_sum(grad_up_part, two_other)
-    grad_hidden_two, up_other_grad = order(grad_hidden_two, up_other_grad)
+    up_grad = outer_sum(grad_up_part, own)
+    grad_hidden_two, gate_other_grad, up_grad = order(grad_hidden_two, gate_other_grad, up_grad)
     grad_norm_two, grad_gain_two = norm_backward(
         grad_hidden_two, normed_two, scale_two, gain_two, full_width
     )
     grad_middle = cotangent.astype(F32) + grad_norm_two
     branch_low = grad_middle.astype(BF)
-    reduce("down_other", down_away)
-    branch_low, gate_other_grad = line.step(branch_low, gate_other_grad)
+    branch_low, up_grad, gate_other_grad = line.step(branch_low, up_grad, gate_other_grad)
+    reduce("up_own", up_grad)
     gate_away = swap(gate_other_grad, "col", 1)
-    branch_all = gather_row(branch_low)
-    reduce("up_own", up_grad)
-    branch_all, gate_away = line.step(branch_all, gate_away)
-    leaving = contract_flipped(rows_of(branch_all, 1 - column), out_weight).astype(BF)
+    branch_mine, branch_other = gather_row(branch_low)
+    up_other_grad = outer_sum(grad_up_part, other)
+    branch_mine, branch_other, gate_away, up_other_grad = line.step(
+        branch_mine, branch_other, gate_away, up_other_grad
+    )
+    reduce("gate_other", gate_away)
+    leaving = contract_flipped(branch_other, out_weight).astype(BF)
     grad_sent = swap(leaving, "col", 1)
-    grad_kept = contract_flipped(rows_of(branch_all, column), out_weight)
-    out_grad = outer_sum(attended_all, branch_all)
-    reduce("gate_other", gate_away)
+    grad_kept = contract_flipped(branch_mine, out_weight)
+    out_grad = outer_sum(
+        jnp.concatenate([attended, attended_got], 0),
+        jnp.concatenate([branch_mine, branch_other], 0),
+    )
     grad_sent, out_grad, up_other_grad = line.step(grad_sent, out_grad, up_other_grad)
+    reduce("out", out_grad)
     up_away = swap(up_other_grad, "col", 1)
     grad_projected = attention_backward(
         grad_kept, grad_sent, queries, kv, log_totals, cosine, sine, starts
     )
-    reduce("out", out_grad)
-    (grad_projected,) = line.step(grad_projected)
+    grad_projected, up_away, activated = line.step(grad_projected, up_away, late=(activated,))
+    reduce("up_other", up_away)
     projected_got = swap(grad_projected, "col", 1)
     lower = activated.shape[0] // 2
-    out_staying = [contract(activated[:lower], weight).astype(BF) for weight in (down, down_other)]
-    out_leaving = [contract(activated[lower:], weight).astype(BF) for weight in (down, down_other)]
-    reduce("up_other", up_away)
-    projected_got, *out_parts = line.step(projected_got, *out_staying, *out_leaving)
-    out_plane = scatter_plane(out_parts[:2], out_parts[2:])
-    out_flight = next(out_plane)
-    projected_all = pair_up(grad_projected, projected_got, first_column, 0)
-    qkv_grad = outer_sum(hidden_one_all, projected_all)
-    grad_hidden_one = scatter_row(projected_all, lambda rows: contract_flipped(rows, qkv_weight))
+    out_other = contract(activated[:lower], down_other) + swap(
+        contract(activated[lower:], down_other).astype(BF), "row", 1
+    ).astype(F32)
+    out_own = contract(activated[:lower], down) + swap(
+        contract(activated[lower:], down).astype(BF), "row", 1
+    ).astype(F32)
+    projected_got, out_other, out_own, one_mine = line.step(
+        projected_got, out_other.astype(BF), late=(out_own, one_mine)
+    )
+    out_across = swap(out_other, "col", 1)
+    qkv_grad = outer_sum(
+        jnp.concatenate([one_mine, one_other], 0),
+        jnp.concatenate([grad_projected, projected_got], 0),
+    )
     reduce("qkv", qkv_grad)
-    (grad_hidden_one,) = line.step(grad_hidden_one)
+    grad_hidden_one = scatter_row(
+        (grad_projected, projected_got), lambda rows: contract_flipped(rows, qkv_weight)
+    )
+    finished = sorted(done)
+    grad_hidden_one, *rest = line.step(grad_hidden_one, *[done[name] for name in finished])
+    done.update(zip(finished, rest))
     grad_norm_one, grad_gain_one = norm_backward(
         grad_hidden_one, normed_one, scale_one, gain_one, full_width
     )
     grad_inputs = grad_middle + grad_norm_one
     gain_grads = jnp.stack([grad_gain_one, grad_gain_two])
-    bit = 1
-    while bit < lax.axis_size("row"):
-        gain_grads = gain_grads + swap(gain_grads, "row", bit)
-        bit *= 2
-    reduce("gains", gain_grads)
-    out_flight = line.step(*out_flight, grad_inputs)
-    grad_inputs = out_flight[3]
-    branch = out_plane.send(out_flight[:3])
-    (branch,) = line.step(branch)
-    outputs = (middle + branch).astype(BF)
+    for axis in ("row", "dp"):
+        size = lax.axis_size(axis)
+        if size & (size - 1):
+            gain_grads = lax.psum(gain_grads, axis)
+            continue
+        bit = 1
+        while bit < size:
+            got = swap(gain_grads, axis, bit)
+            if axis == "dp" and bit == 1:
+                out_across, got = line.step(out_across, got)
+            gain_grads = gain_grads + got
+            bit *= 2
+    outputs = (middle + scatter_late(out_own, out_across)).astype(BF)
     line.drain()
 
     def rows_in(name):
@@ -654,7 +710,6 @@
     grad_down = rows_in("down").astype(F32)
     grad_out = done["out"].astype(F32)
     grad_qkv = done["qkv"].astype(F32)
-    gain_grads = done["gains"]
     return (
         outputs,
         grad_inputs,

time: 789 us -> 730 us (0.925)
  waiting for transfers between devices: 342 us -> 292 us
  other arithmetic: 102 us -> 90.9 us
  local copies, waits for them, and re-layouts: 54.6 us -> 64.8 us
  matrix products: 83.6 us -> 75.7 us
    ppermute x55 -> x54, waiting for transfers between devices: 270 us -> 221 us  [swap(): return lax.ppermute(values, axis, pairs)]
    convert_element_type x19 -> x17, other arithmetic: 23.3 us -> 15.7 us  [the longest x16 15.5 us: step(): item[1] = (values.astype(F32) + arrived.astype(F32)).astype(values.dtype)]
    unnamed x174 -> x231, local copies, waits for them, and re-layouts: 27.4 us -> 34.9 us
    ppermute x27 -> x24, starting transfers between devices: 60.6 us -> 63.9 us  [the longest x8 45.4 us: add(): lax.ppermute(values, 'dp', self.stages[0])]
    ppermute x55 -> x54, starting transfers between devices: 51.9 us -> 48.9 us  [swap(): return lax.ppermute(values, axis, pairs)]
    ppermute x27 -> x24, waiting for transfers between devices: 72.1 us -> 70.4 us  [the longest x8 39.5 us: add(): lax.ppermute(values, 'dp', self.stages[0])]
  transfers between devices with their start and end apart: 82 -> 78, of which waited for: 35 -> 34; matrix products, arithmetic and copies ran while one was open for 25% -> 25% of each run, Pallas kernels for 8% -> 7%
where the time goes in v3:
time: 730 us; the launch traced here: 721 us
  waiting for transfers between devices  292 us (40%)
  starting transfers between devices  113 us (15%)
  other arithmetic  90.9 us (12%)
  Pallas kernels  81.7 us (11%)
  matrix products  75.7 us (10%)
  local copies, waits for them, and re-layouts  64.8 us (9%)
    ppermute x54, waiting for transfers between devices, swap(): return lax.ppermute(values, axis, pairs)  221 us
    ppermute x54, starting transfers between devices, swap(): return lax.ppermute(values, axis, pairs)  48.9 us
    ppermute x8, starting transfers between devices, add(): lax.ppermute(values, 'dp', self.stages[0])  45.4 us
    ppermute x8, waiting for transfers between devices, add(): lax.ppermute(values, 'dp', self.stages[0])  39.5 us
    dot_general x8, matrix products, outer_sum(): lax.dot_general(leading, trailing, (((0,), (0,)), ((), ())), preferred_el...  35.6 us
    unnamed x231, local copies, waits for them, and re-layouts  34.9 us
    ppermute x16, waiting for transfers between devices, step(): item[2] = lax.ppermute(item[1], 'dp', self.stages[item[0]])  30.9 us
    pallas_call x1, Pallas kernels, attention_backward(): pl.pallas_call(lambda *refs: backward_kernel(*refs, anchors=len(anchors))...  22.2 us
  transfers between devices with their start and end apart: 78, of which 34 were waited for; matrix products, arithmetic and copies ran while one was open for 25% of the time, Pallas kernels for 7%

profile of v3, /device:TPU:0, one launch (start us, length us, event | category | flops | bytes accessed | tf_op | source)
XLA Modules:
  0.0 720.7 jit_solution(816684155866020548)
XLA Ops:
  25.4 12.0 %collective-permute-done.3 = bf16[512,704]{0,1:T(8,128)(2,1)S(1)} collective-permute-done((bf16[512,704]{0,1:T(8,128)(2,1)}, bf16[512,704]{0,1:T(8,128)(2,1)S(1)}, u32[]{:S(2)}, u32[]{:S(2)}) %collective-permute-start.3) | collective-permute-done | bytes 720928 | tf_op jit(solution)/shard_map/ppermute | solution.py:37
  73.2 11.7 %collective-permute-done.7 = bf16[512,1024]{1,0:T(8,128)(2,1)S(1)} collective-permute-done((bf16[512,1024]{1,0:T(8,128)(2,1)S(1)}, bf16[512,1024]{1,0:T(8,128)(2,1)S(1)}, u32[]{:S(2)}, u32[]{:S(2)}) %collective-permute-start.7) | collective-permute-done | bytes 1048608 | tf_op jit(solution)/shard_map/ppermute | solution.py:37
  84.9 15.7 %collective-permute-done.6.refs_1_.refs_3_ = bf16[1024,640]{1,0:T(8,128)(2,1)S(1)} collective-permute-done((bf16[1024,640]{1,0:T(8,128)(2,1)S(1)}, bf16[1024,640]{1,0:T(8,128)(2,1)S(1)}, u32[]{:S(2)}, u32[]{:S(2)}) %collective-permute-start.6) | collective-permute-done | bytes 1310752 | tf_op jit(solution)/shard_map/ppermute | solution.py:37
  102.1 20.8 %attention_forward.1 = (bf16[1024,512]{1,0:T(8,128)(2,1)}, bf16[1024,512]{1,0:T(8,128)(2,1)S(1)}, bf16[1024,128]{1,0:T(8,128)(2,1)S(1)}, f32[4,2,1024]{2,1,0:T(2,128)S(1)}) custom-call(f32[1024,640]{1,0:T(8,128)} %fusion.96.refs_0_.refs_2_, bf16[1024,640]{1,0:T(8,128)(2,1)S(1)} %collective-permute-done.6.refs_1_.refs_3_, ...), custom_call_target="tpu_custom_call" | custom-call | flops 20000000000 | bytes 8388608 | tf_op jit(solution)/shard_map/attention_forward/pallas_call | solution.py:417
  198.0 14.1 %collective-permute-done.16 = bf16[512,1024]{1,0:T(8,128)(2,1)S(1)} collective-permute-done((bf16[512,1024]{1,0:T(8,128)(2,1)S(1)}, bf16[512,1024]{1,0:T(8,128)(2,1)S(1)}, u32[]{:S(2)}, u32[]{:S(2)}) %collective-permute-start.16) | collective-permute-done | bytes 1048608 | tf_op jit(solution)/shard_map/ppermute | solution.py:37
  217.7 22.3 %collective-permute-done.21 = bf16[512,1024]{1,0:T(8,128)(2,1)S(1)} collective-permute-done((bf16[512,1024]{1,0:T(8,128)(2,1)S(1)}, bf16[512,1024]{1,0:T(8,128)(2,1)S(1)}, u32[]{:S(2)}, u32[]{:S(2)}) %collective-permute-start.21) | collective-permute-done | bytes 1048608 | tf_op jit(solution)/shard_map/ppermute | solution.py:37
  243.8 7.7 %collective-permute-done.24 = bf16[256,1024]{1,0:T(8,128)(2,1)S(1)} collective-permute-done((bf16[256,1024]{1,0:T(8,128)(2,1)S(1)}, bf16[256,1024]{1,0:T(8,128)(2,1)S(1)}, u32[]{:S(2)}, u32[]{:S(2)}) %collective-permute-start.24) | collective-permute-done | bytes 524320 | tf_op jit(solution)/shard_map/ppermute | solution.py:37
  257.4 18.7 %hidden_part.1 = (bf16[2048,704]{1,0:T(8,128)(2,1)}, bf16[2048,704]{1,0:T(8,128)(2,1)}, bf16[2048,704]{1,0:T(8,128)(2,1)}) custom-call(bf16[1024,1024]{1,0:T(8,128)(2,1)} %copy-done.40, bf16[1024,1024]{1,0:T(8,128)(2,1)} %copy-done.100, bf16[1024,1024]{1,0:T(8,128)(2,1)} %copy-done.77, bf16[1024,1024]{1,0:T(8,128)(2,1)} %copy-done.38, ...), custom_call_target="tpu_custom_call" | custom-call | flops 11811160064 | bytes 25165824 | tf_op jit(solution)/shard_map/hidden_part/pallas_call | solution.py:368
  276.1 7.6 %convolution_convert_fusion.6 = bf16[704,1024]{1,0:T(8,128)(2,1)} fusion(bf16[2048,704]{1,0:T(8,128)(2,1)} %get-tuple-element.203, bf16[2048,1024]{1,0:T(8,128)(2,1)} %copy-done.88), kind=kOutput, calls=%fused_computation.93 | convolution fusion | flops 2953510912 | bytes 8519680 | tf_op jit(solution)/shard_map/dot_general | solution.py:194
  288.0 9.8 %back_part.3 = (bf16[1024,1024]{1,0:T(8,128)(2,1)}, bf16[1024,1024]{1,0:T(8,128)(2,1)}) custom-call(bf16[2048,704]{1,0:T(8,128)(2,1)} %get-tuple-element.166.grad_gate_ref, bf16[2048,704]{1,0:T(8,128)(2,1)} %get-tuple-element.172.grad_up_ref, bf16[1024,704]{1,0:T(8,128)(2,1)S(1)} %copy-done.2, bf16[1024,704]{1,0:T(8,128)(2,1)S(1)} %copy-done.3, ...), custom_call_target="tpu_custom_call" | custom-call | flops 5905580032 | bytes 12582912 | tf_op jit(solution)/shard_map/back_part/pallas_call | solution.py:397
  304.2 10.2 %back_part.2 = (bf16[1024,1024]{1,0:T(8,128)(2,1)}, bf16[1024,1024]{1,0:T(8,128)(2,1)}) custom-call(bf16[2048,704]{1,0:T(8,128)(2,1)} %get-tuple-element.166.grad_gate_ref, bf16[2048,704]{1,0:T(8,128)(2,1)} %get-tuple-element.172.grad_up_ref, bf16[1024,704]{1,0:T(8,128)(2,1)S(1)} %copy-done.2, bf16[1024,704]{1,0:T(8,128)(2,1)S(1)} %copy-done.3, ...), custom_call_target="tpu_custom_call" | custom-call | flops 5905580032 | bytes 12582912 | tf_op jit(solution)/shard_map/back_part/pallas_call | solution.py:397
  322.2 9.9 %collective-permute-done.29 = bf16[704,1024]{1,0:T(8,128)(2,1)S(1)} collective-permute-done((bf16[704,1024]{1,0:T(8,128)(2,1)}, bf16[704,1024]{1,0:T(8,128)(2,1)S(1)}, u32[]{:S(2)}, u32[]{:S(2)}) %collective-permute-start.29) | collective-permute-done | bytes 1441824 | tf_op jit(solution)/shard_map/ppermute | solution.py:37
  361.8 14.3 %collective-permute-done.35 = bf16[704,1024]{1,0:T(8,128)(2,1)S(1)} collective-permute-done((bf16[704,1024]{1,0:T(8,128)(2,1)S(1)}, bf16[704,1024]{1,0:T(8,128)(2,1)S(1)}, u32[]{:S(2)}, u32[]{:S(2)}) %collective-permute-start.35) | collective-permute-done | bytes 1441824 | tf_op jit(solution)/shard_map/ppermute | solution.py:129
  394.5 17.1 %collective-permute-done.39 = bf16[704,1024]{1,0:T(8,128)(2,1)S(1)} collective-permute-done((bf16[704,1024]{1,0:T(8,128)(2,1)S(1)}, bf16[704,1024]{1,0:T(8,128)(2,1)S(1)}, u32[]{:S(2)}, u32[]{:S(2)}) %collective-permute-start.39) | collective-permute-done | bytes 1441824 | tf_op jit(solution)/shard_map/ppermute | solution.py:158
  421.2 14.6 %collective-permute-done.43 = bf16[512,1024]{1,0:T(8,128)(2,1)S(1)} collective-permute-done((bf16[512,1024]{1,0:T(8,128)(2,1)S(1)}, bf16[512,1024]{1,0:T(8,128)(2,1)S(1)}, u32[]{:S(2)}, u32[]{:S(2)}) %collective-permute-start.43) | collective-permute-done | bytes 1048608 | tf_op jit(solution)/shard_map/ppermute | solution.py:37
  445.2 8.1 %collective-permute-done.46 = bf16[704,1024]{1,0:T(8,128)(2,1)S(1)} collective-permute-done((bf16[704,1024]{1,0:T(8,128)(2,1)S(1)}, bf16[704,1024]{1,0:T(8,128)(2,1)S(1)}, u32[]{:S(2)}, u32[]{:S(2)}) %collective-permute-start.46) | collective-permute-done | bytes 1441824 | tf_op jit(solution)/shard_map/ppermute | solution.py:158
  453.4 12.1 %collective-permute-done.48 = bf16[704,1024]{1,0:T(8,128)(2,1)S(1)} collective-permute-done((bf16[704,1024]{1,0:T(8,128)(2,1)S(1)}, bf16[704,1024]{1,0:T(8,128)(2,1)S(1)}, u32[]{:S(2)}, u32[]{:S(2)}) %collective-permute-start.48) | collective-permute-done | bytes 1441824 | tf_op jit(solution)/shard_map/ppermute | solution.py:129
  468.7 7.5 %collective-permute-start.52 = (bf16[704,1024]{1,0:T(8,128)(2,1)S(1)}, bf16[704,1024]{1,0:T(8,128)(2,1)S(1)}, u32[]{:S(2)}, u32[]{:S(2)}) collective-permute-start(bf16[704,1024]{1,0:T(8,128)(2,1)S(1)} %collective-permute-done.45), channel_id=1, source_target_pairs={{0,8},{24,16},{1,9},{25,17},{2,10},{26,18},{3,11},{27,19},{4,12},{... | collective-permute-start | bytes 4325384 | tf_op jit(solution)/shard_map/ppermute | solution.py:129
  484.8 10.5 %collective-permute-done.49.refs_1_ = bf16[1024,512]{1,0:T(8,128)(2,1)S(1)} collective-permute-done((bf16[1024,512]{1,0:T(8,128)(2,1)S(1)}, bf16[1024,512]{1,0:T(8,128)(2,1)S(1)}, u32[]{:S(2)}, u32[]{:S(2)}) %collective-permute-start.49) | collective-permute-done | bytes 1048608 | tf_op jit(solution)/shard_map/ppermute | solution.py:37
  511.2 22.2 %attention_backward.1 = bf16[1024,640]{1,0:T(8,128)(2,1)S(1)} custom-call(f32[1024,512]{1,0:T(8,128)} %fusion.100.refs_0_, bf16[1024,512]{1,0:T(8,128)(2,1)S(1)} %collective-permute-done.49.refs_1_, bf16[1024,512]{1,0:T(8,128)(2,1)S(1)} %copy-done.11, bf16[1024,128]{1,0:T(8,128)(2,1)S(1)} %get-tuple-element.192.refs_3_, ...), custom_call_target="tpu_custom_call" | custom-call | flops 40000000000 | bytes 8388608 | tf_op jit(solution)/shard_map/attention_backward/pallas_call | solution.py:460
  558.1 21.2 %collective-permute-done.57 = bf16[1024,640]{1,0:T(8,128)(2,1)S(1)} collective-permute-done((bf16[1024,640]{1,0:T(8,128)(2,1)S(1)}, bf16[1024,640]{1,0:T(8,128)(2,1)S(1)}, u32[]{:S(2)}, u32[]{:S(2)}) %collective-permute-start.57) | collective-permute-done | bytes 1310752 | tf_op jit(solution)/shard_map/ppermute | solution.py:37
  607.3 19.8 %collective-permute-done.65 = bf16[512,1024]{1,0:T(8,128)(2,1)S(1)} collective-permute-done((bf16[512,1024]{1,0:T(8,128)(2,1)S(1)}, bf16[512,1024]{1,0:T(8,128)(2,1)S(1)}, u32[]{:S(2)}, u32[]{:S(2)}) %collective-permute-start.65) | collective-permute-done | bytes 1048608 | tf_op jit(solution)/shard_map/ppermute | solution.py:37
  659.3 15.8 %collective-permute-done.71 = f32[2,1024]{1,0:T(2,128)S(1)} collective-permute-done((f32[2,1024]{1,0:T(2,128)S(1)}, f32[2,1024]{1,0:T(2,128)S(1)}, u32[]{:S(2)}, u32[]{:S(2)}) %collective-permute-start.71) | collective-permute-done | bytes 8224 | tf_op jit(solution)/shard_map/ppermute | solution.py:37
  696.9 11.6 %collective-permute-done.74 = bf16[512,1024]{1,0:T(8,128)(2,1)} collective-permute-done((bf16[512,1024]{1,0:T(8,128)(2,1)}, bf16[512,1024]{1,0:T(8,128)(2,1)}, u32[]{:S(2)}, u32[]{:S(2)}) %collective-permute-start.74) | collective-permute-done | bytes 1048608 | tf_op jit(solution)/shard_map/ppermute | solution.py:37
  (508 shorter events, 382.8 us)
Async XLA Ops:
  43.2 30.0 %collective-permute-start.8 = (bf16[512,704]{0,1:T(8,128)(2,1)}, bf16[512,704]{0,1:T(8,128)(2,1)}, u32[]{:S(2)}, u32[]{:S(2)}) collective-permute-start(bf16[512,704]{0,1:T(8,128)(2,1)} %copy.57), channel_id=1, source_target_pairs={{0,1},{1,0},{2,3},{3,2},{4,5},{5,4},{6,7},{7,6},{8,9},{9,8},{10,11... | collective-permute-start | bytes 2162696 | tf_op jit(solution)/shard_map/ppermute | solution.py:37
  59.6 41.0 %collective-permute-start.6 = (bf16[1024,640]{1,0:T(8,128)(2,1)S(1)}, bf16[1024,640]{1,0:T(8,128)(2,1)S(1)}, u32[]{:S(2)}, u32[]{:S(2)}) collective-permute-start(bf16[1024,640]{1,0:T(8,128)(2,1)S(1)} %convolution_convert_fusion.8), channel_id=1, source_target_pairs={{0,1},{1,0},{2,3},{3,2},{4,5},{5,4},{6,7},{7,6},{8,9},{9,8},{10,11... | collective-permute-start | bytes 3932168 | tf_op jit(solution)/shard_map/ppermute | solution.py:37
  64.6 59.3 %collective-permute-start.10 = (bf16[512,704]{0,1:T(8,128)(2,1)S(1)}, bf16[512,704]{0,1:T(8,128)(2,1)S(1)}, u32[]{:S(2)}, u32[]{:S(2)}) collective-permute-start(bf16[512,704]{0,1:T(8,128)(2,1)S(1)} %copy-done.68), channel_id=1, source_target_pairs={{0,8},{8,0},{16,24},{24,16},{1,9},{9,1},{17,25},{25,17},{2,10},{10... | collective-permute-start | bytes 2162696 | tf_op jit(solution)/shard_map/ppermute | solution.py:37
  66.3 57.6 %collective-permute-start.11 = (bf16[352,1024]{1,0:T(8,128)(2,1)}, bf16[352,1024]{1,0:T(8,128)(2,1)S(1)}, u32[]{:S(2)}, u32[]{:S(2)}) collective-permute-start(bf16[352,1024]{1,0:T(8,128)(2,1)} %collective-permute-done.5), channel_id=1, source_target_pairs={{0,8},{8,0},{16,24},{24,16},{1,9},{9,1},{17,25},{25,17},{2,10},{10... | collective-permute-start | bytes 2162696 | tf_op jit(solution)/shard_map/ppermute | solution.py:37
  135.0 43.6 %collective-permute-start.17 = (bf16[1024,1024]{1,0:T(8,128)(2,1)}, bf16[1024,1024]{1,0:T(8,128)(2,1)}, u32[]{:S(2)}, u32[]{:S(2)}) collective-permute-start(bf16[1024,1024]{1,0:T(8,128)(2,1)} %pad_maximum_fusion.3), channel_id=1, source_target_pairs={{0,2},{2,0},{4,6},{6,4},{1,3},{3,1},{5,7},{7,5},{8,10},{10,8},{12,... | collective-permute-start | bytes 6291464 | tf_op jit(solution)/shard_map/ppermute | solution.py:37
  298.3 33.8 %collective-permute-start.29 = (bf16[704,1024]{1,0:T(8,128)(2,1)}, bf16[704,1024]{1,0:T(8,128)(2,1)S(1)}, u32[]{:S(2)}, u32[]{:S(2)}) collective-permute-start(bf16[704,1024]{1,0:T(8,128)(2,1)} %convolution_convert_fusion.6), channel_id=1, source_target_pairs={{0,1},{1,0},{2,3},{3,2},{4,5},{5,4},{6,7},{7,6},{8,9},{9,8},{10,11... | collective-permute-start | bytes 4325384 | tf_op jit(solution)/shard_map/ppermute | solution.py:37
  299.6 34.7 %collective-permute-start.33 = (bf16[704,1024]{1,0:T(8,128)(2,1)}, bf16[704,1024]{1,0:T(8,128)(2,1)}, u32[]{:S(2)}, u32[]{:S(2)}) collective-permute-start(bf16[704,1024]{1,0:T(8,128)(2,1)} %convolution_convert_fusion.7), channel_id=1, source_target_pairs={{0,8},{24,16},{1,9},{25,17},{2,10},{26,18},{3,11},{27,19},{4,12},{... | collective-permute-start | bytes 4325384 | tf_op jit(solution)/shard_map/ppermute | solution.py:129
  339.9 36.1 %collective-permute-start.35 = (bf16[704,1024]{1,0:T(8,128)(2,1)S(1)}, bf16[704,1024]{1,0:T(8,128)(2,1)S(1)}, u32[]{:S(2)}, u32[]{:S(2)}) collective-permute-start(bf16[704,1024]{1,0:T(8,128)(2,1)S(1)} %collective-permute-done.29), channel_id=1, source_target_pairs={{0,8},{24,16},{1,9},{25,17},{2,10},{26,18},{3,11},{27,19},{4,12},{... | collective-permute-start | bytes 4325384 | tf_op jit(solution)/shard_map/ppermute | solution.py:129
  379.6 32.0 %collective-permute-start.39 = (bf16[704,1024]{1,0:T(8,128)(2,1)S(1)}, bf16[704,1024]{1,0:T(8,128)(2,1)S(1)}, u32[]{:S(2)}, u32[]{:S(2)}) collective-permute-start(bf16[704,1024]{1,0:T(8,128)(2,1)S(1)} %add_convert_fusion.12), channel_id=1, source_target_pairs={{8,0},{16,24},{9,1},{17,25},{10,2},{18,26},{11,3},{19,27},{12,4},{... | collective-permute-start | bytes 4325384 | tf_op jit(solution)/shard_map/ppermute | solution.py:158
  381.5 30.1 %collective-permute-start.40 = (bf16[704,1024]{1,0:T(8,128)(2,1)S(1)}, bf16[704,1024]{1,0:T(8,128)(2,1)S(1)}, u32[]{:S(2)}, u32[]{:S(2)}) collective-permute-start(bf16[704,1024]{1,0:T(8,128)(2,1)S(1)} %add_convert_fusion.11), channel_id=1, source_target_pairs={{8,16},{16,8},{9,17},{17,9},{10,18},{18,10},{11,19},{19,11},{12,20... | collective-permute-start | bytes 4325384 | tf_op jit(solution)/shard_map/ppermute | solution.py:158
  382.2 33.3 %collective-permute-start.41 = (bf16[704,1024]{1,0:T(8,128)(2,1)S(1)}, bf16[704,1024]{1,0:T(8,128)(2,1)S(1)}, u32[]{:S(2)}, u32[]{:S(2)}) collective-permute-start(bf16[704,1024]{1,0:T(8,128)(2,1)S(1)} %fusion.30), channel_id=1, source_target_pairs={{0,8},{24,16},{1,9},{25,17},{2,10},{26,18},{3,11},{27,19},{4,12},{... | collective-permute-start | bytes 4325384 | tf_op jit(solution)/shard_map/ppermute | solution.py:129
  417.1 36.3 %collective-permute-start.46 = (bf16[704,1024]{1,0:T(8,128)(2,1)S(1)}, bf16[704,1024]{1,0:T(8,128)(2,1)S(1)}, u32[]{:S(2)}, u32[]{:S(2)}) collective-permute-start(bf16[704,1024]{1,0:T(8,128)(2,1)S(1)} %add_convert_fusion.10), channel_id=1, source_target_pairs={{8,0},{16,24},{9,1},{17,25},{10,2},{18,26},{11,3},{19,27},{12,4},{... | collective-permute-start | bytes 4325384 | tf_op jit(solution)/shard_map/ppermute | solution.py:158
  418.6 34.7 %collective-permute-start.45 = (bf16[704,1024]{1,0:T(8,128)(2,1)S(1)}, bf16[704,1024]{1,0:T(8,128)(2,1)S(1)}, u32[]{:S(2)}, u32[]{:S(2)}) collective-permute-start(bf16[704,1024]{1,0:T(8,128)(2,1)S(1)} %convolution_convert_fusion.5), channel_id=1, source_target_pairs={{0,1},{1,0},{2,3},{3,2},{4,5},{5,4},{6,7},{7,6},{8,9},{9,8},{10,11... | collective-permute-start | bytes 4325384 | tf_op jit(solution)/shard_map/ppermute | solution.py:37
  420.5 32.9 %collective-permute-start.47 = (bf16[704,1024]{1,0:T(8,128)(2,1)S(1)}, bf16[704,1024]{1,0:T(8,128)(2,1)S(1)}, u32[]{:S(2)}, u32[]{:S(2)}) collective-permute-start(bf16[704,1024]{1,0:T(8,128)(2,1)S(1)} %add_convert_fusion.9), channel_id=1, source_target_pairs={{8,16},{16,8},{9,17},{17,9},{10,18},{18,10},{11,19},{19,11},{12,20... | collective-permute-start | bytes 4325384 | tf_op jit(solution)/shard_map/ppermute | solution.py:158
  468.7 33.5 %collective-permute-start.52 = (bf16[704,1024]{1,0:T(8,128)(2,1)S(1)}, bf16[704,1024]{1,0:T(8,128)(2,1)S(1)}, u32[]{:S(2)}, u32[]{:S(2)}) collective-permute-start(bf16[704,1024]{1,0:T(8,128)(2,1)S(1)} %collective-permute-done.45), channel_id=1, source_target_pairs={{0,8},{24,16},{1,9},{25,17},{2,10},{26,18},{3,11},{27,19},{4,12},{... | collective-permute-start | bytes 4325384 | tf_op jit(solution)/shard_map/ppermute | solution.py:129
  541.0 38.2 %collective-permute-start.60 = (bf16[704,1024]{1,0:T(8,128)(2,1)S(1)}, bf16[704,1024]{1,0:T(8,128)(2,1)S(1)}, u32[]{:S(2)}, u32[]{:S(2)}) collective-permute-start(bf16[704,1024]{1,0:T(8,128)(2,1)S(1)} %add_convert_fusion.4), channel_id=1, source_target_pairs={{8,0},{16,24},{9,1},{17,25},{10,2},{18,26},{11,3},{19,27},{12,4},{... | collective-permute-start | bytes 4325384 | tf_op jit(solution)/shard_map/ppermute | solution.py:158
  542.3 37.4 %collective-permute-start.62 = (bf16[704,1024]{1,0:T(8,128)(2,1)S(1)}, bf16[704,1024]{1,0:T(8,128)(2,1)S(1)}, u32[]{:S(2)}, u32[]{:S(2)}) collective-permute-start(bf16[704,1024]{1,0:T(8,128)(2,1)S(1)} %collective-permute-done.53), channel_id=1, source_target_pairs={{0,8},{24,16},{1,9},{25,17},{2,10},{26,18},{3,11},{27,19},{4,12},{... | collective-permute-start | bytes 4325384 | tf_op jit(solution)/shard_map/ppermute | solution.py:129
  548.7 30.5 %collective-permute-start.57 = (bf16[1024,640]{1,0:T(8,128)(2,1)S(1)}, bf16[1024,640]{1,0:T(8,128)(2,1)S(1)}, u32[]{:S(2)}, u32[]{:S(2)}) collective-permute-start(bf16[1024,640]{1,0:T(8,128)(2,1)S(1)} %attention_backward.1), channel_id=1, source_target_pairs={{0,1},{1,0},{2,3},{3,2},{4,5},{5,4},{6,7},{7,6},{8,9},{9,8},{10,11... | collective-permute-start | bytes 3932168 | tf_op jit(solution)/shard_map/ppermute | solution.py:37
  593.1 37.5 %collective-permute-start.68 = (bf16[1024,640]{0,1:T(8,128)(2,1)S(1)}, bf16[1024,640]{0,1:T(8,128)(2,1)S(1)}, u32[]{:S(2)}, u32[]{:S(2)}) collective-permute-start(bf16[1024,640]{0,1:T(8,128)(2,1)S(1)} %fusion.32), channel_id=1, source_target_pairs={{0,8},{24,16},{1,9},{25,17},{2,10},{26,18},{3,11},{27,19},{4,12},{... | collective-permute-start | bytes 3932168 | tf_op jit(solution)/shard_map/ppermute | solution.py:129
  597.3 33.3 %collective-permute-start.67 = (bf16[704,1024]{1,0:T(8,128)(2,1)S(1)}, bf16[704,1024]{1,0:T(8,128)(2,1)S(1)}, u32[]{:S(2)}, u32[]{:S(2)}) collective-permute-start(bf16[704,1024]{1,0:T(8,128)(2,1)S(1)} %add_convert_fusion.3), channel_id=1, source_target_pairs={{8,16},{16,8},{9,17},{17,9},{10,18},{18,10},{11,19},{19,11},{12,20... | collective-permute-start | bytes 4325384 | tf_op jit(solution)/shard_map/ppermute | solution.py:158
  605.5 53.8 %collective-permute-start.63 = (bf16[1024,1024]{1,0:T(8,128)(2,1)}, bf16[1024,1024]{1,0:T(8,128)(2,1)}, u32[]{:S(2)}, u32[]{:S(2)}) collective-permute-start(bf16[1024,1024]{1,0:T(8,128)(2,1)} %add_convert_fusion.1), channel_id=1, source_target_pairs={{0,1},{1,0},{2,3},{3,2},{4,5},{5,4},{6,7},{7,6},{8,9},{9,8},{10,11... | collective-permute-start | bytes 6291464 | tf_op jit(solution)/shard_map/ppermute | solution.py:37
  636.1 39.0 %collective-permute-start.73 = (bf16[1024,640]{0,1:T(8,128)(2,1)}, bf16[1024,640]{0,1:T(8,128)(2,1)}, u32[]{:S(2)}, u32[]{:S(2)}) collective-permute-start(bf16[1024,640]{0,1:T(8,128)(2,1)} %add_convert_fusion.15), channel_id=1, source_target_pairs={{8,16},{16,8},{9,17},{17,9},{10,18},{18,10},{11,19},{19,11},{12,20... | collective-permute-start | bytes 3932168 | tf_op jit(solution)/shard_map/ppermute | solution.py:158
  637.8 37.3 %collective-permute-start.72 = (bf16[704,1024]{1,0:T(8,128)(2,1)}, bf16[704,1024]{1,0:T(8,128)(2,1)}, u32[]{:S(2)}, u32[]{:S(2)}) collective-permute-start(bf16[704,1024]{1,0:T(8,128)(2,1)} %add_convert_fusion.2), channel_id=1, source_target_pairs={{8,0},{16,24},{9,1},{17,25},{10,2},{18,26},{11,3},{19,27},{12,4},{... | collective-permute-start | bytes 4325384 | tf_op jit(solution)/shard_map/ppermute | solution.py:158
  683.8 32.4 %collective-permute-start.77 = (bf16[1024,640]{0,1:T(8,128)(2,1)}, bf16[1024,640]{0,1:T(8,128)(2,1)}, u32[]{:S(2)}, u32[]{:S(2)}) collective-permute-start(bf16[1024,640]{0,1:T(8,128)(2,1)} %add_convert_fusion.14), channel_id=1, source_target_pairs={{8,0},{16,24},{9,1},{17,25},{10,2},{18,26},{11,3},{19,27},{12,4},{... | collective-permute-start | bytes 3932168 | tf_op jit(solution)/shard_map/ppermute | solution.py:158
  (163 other events, 2268.9 us)

commit v4 on v3

--- a/solution.py
+++ b/solution.py
@@ -635,7 +635,7 @@
     )
     grad_middle = cotangent.astype(F32) + grad_norm_two
     branch_low = grad_middle.astype(BF)
-    branch_low, up_grad, gate_other_grad = line.step(branch_low, up_grad, gate_other_grad)
+    up_grad, gate_other_grad = line.step(up_grad, gate_other_grad)
     reduce("up_own", up_grad)
     gate_away = swap(gate_other_grad, "col", 1)
     branch_mine, branch_other = gather_row(branch_low)

time: 730 us -> 718 us (0.984)
  waiting for transfers between devices: 292 us -> 276 us
    ppermute x54, waiting for transfers between devices: 221 us -> 205 us  [swap(): return lax.ppermute(values, axis, pairs)]
    ppermute x8, waiting for transfers between devices: 39.5 us -> 32.1 us  [add(): lax.ppermute(values, 'dp', self.stages[0])]
  transfers between devices with their start and end apart: 78 -> 78, of which waited for: 34 -> 33; matrix products, arithmetic and copies ran while one was open for 25% -> 26% of each run, Pallas kernels for 7% -> 8%
where the time goes in v4:
time: 718 us; the launch traced here: 708 us
  waiting for transfers between devices  276 us (38%)
  starting transfers between devices  116 us (16%)
  other arithmetic  90.9 us (13%)
  Pallas kernels  81.7 us (11%)
  matrix products  75.7 us (11%)
  local copies, waits for them, and re-layouts  65.5 us (9%)
    ppermute x54, waiting for transfers between devices, swap(): return lax.ppermute(values, axis, pairs)  205 us
    ppermute x54, starting transfers between devices, swap(): return lax.ppermute(values, axis, pairs)  48.8 us
    ppermute x8, starting transfers between devices, add(): lax.ppermute(values, 'dp', self.stages[0])  48.5 us
    ppermute x16, waiting for transfers between devices, step(): item[2] = lax.ppermute(item[1], 'dp', self.stages[item[0]])  38.1 us
    dot_general x8, matrix products, outer_sum(): lax.dot_general(leading, trailing, (((0,), (0,)), ((), ())), preferred_el...  35.6 us
    unnamed x231, local copies, waits for them, and re-layouts  35.6 us
    ppermute x8, waiting for transfers between devices, add(): lax.ppermute(values, 'dp', self.stages[0])  32.1 us
    pallas_call x1, Pallas kernels, attention_backward(): pl.pallas_call(lambda *refs: backward_kernel(*refs, anchors=len(anchors))...  22.2 us
  transfers between devices with their start and end apart: 78, of which 33 were waited for; matrix products, arithmetic and copies ran while one was open for 26% of the time, Pallas kernels for 8%

profile of v4, /device:TPU:0, one launch (start us, length us, event | category | flops | bytes accessed | tf_op | source)
XLA Modules:
  0.0 708.0 jit_solution(17194061482738264785)
XLA Ops:
  25.4 12.0 %collective-permute-done.3 = bf16[512,704]{0,1:T(8,128)(2,1)S(1)} collective-permute-done((bf16[512,704]{0,1:T(8,128)(2,1)}, bf16[512,704]{0,1:T(8,128)(2,1)S(1)}, u32[]{:S(2)}, u32[]{:S(2)}) %collective-permute-start.3) | collective-permute-done | bytes 720928 | tf_op jit(solution)/shard_map/ppermute | solution.py:37
  73.2 11.7 %collective-permute-done.7 = bf16[512,1024]{1,0:T(8,128)(2,1)S(1)} collective-permute-done((bf16[512,1024]{1,0:T(8,128)(2,1)S(1)}, bf16[512,1024]{1,0:T(8,128)(2,1)S(1)}, u32[]{:S(2)}, u32[]{:S(2)}) %collective-permute-start.7) | collective-permute-done | bytes 1048608 | tf_op jit(solution)/shard_map/ppermute | solution.py:37
  84.9 15.7 %collective-permute-done.6.refs_1_.refs_3_ = bf16[1024,640]{1,0:T(8,128)(2,1)S(1)} collective-permute-done((bf16[1024,640]{1,0:T(8,128)(2,1)S(1)}, bf16[1024,640]{1,0:T(8,128)(2,1)S(1)}, u32[]{:S(2)}, u32[]{:S(2)}) %collective-permute-start.6) | collective-permute-done | bytes 1310752 | tf_op jit(solution)/shard_map/ppermute | solution.py:37
  102.1 20.8 %attention_forward.1 = (bf16[1024,512]{1,0:T(8,128)(2,1)}, bf16[1024,512]{1,0:T(8,128)(2,1)S(1)}, bf16[1024,128]{1,0:T(8,128)(2,1)S(1)}, f32[4,2,1024]{2,1,0:T(2,128)S(1)}) custom-call(f32[1024,640]{1,0:T(8,128)} %fusion.96.refs_0_.refs_2_, bf16[1024,640]{1,0:T(8,128)(2,1)S(1)} %collective-permute-done.6.refs_1_.refs_3_, ...), custom_call_target="tpu_custom_call" | custom-call | flops 20000000000 | bytes 8388608 | tf_op jit(solution)/shard_map/attention_forward/pallas_call | solution.py:417
  198.0 14.1 %collective-permute-done.16 = bf16[512,1024]{1,0:T(8,128)(2,1)S(1)} collective-permute-done((bf16[512,1024]{1,0:T(8,128)(2,1)S(1)}, bf16[512,1024]{1,0:T(8,128)(2,1)S(1)}, u32[]{:S(2)}, u32[]{:S(2)}) %collective-permute-start.16) | collective-permute-done | bytes 1048608 | tf_op jit(solution)/shard_map/ppermute | solution.py:37
  217.7 22.3 %collective-permute-done.21 = bf16[512,1024]{1,0:T(8,128)(2,1)S(1)} collective-permute-done((bf16[512,1024]{1,0:T(8,128)(2,1)S(1)}, bf16[512,1024]{1,0:T(8,128)(2,1)S(1)}, u32[]{:S(2)}, u32[]{:S(2)}) %collective-permute-start.21) | collective-permute-done | bytes 1048608 | tf_op jit(solution)/shard_map/ppermute | solution.py:37
  243.8 7.7 %collective-permute-done.24 = bf16[256,1024]{1,0:T(8,128)(2,1)S(1)} collective-permute-done((bf16[256,1024]{1,0:T(8,128)(2,1)S(1)}, bf16[256,1024]{1,0:T(8,128)(2,1)S(1)}, u32[]{:S(2)}, u32[]{:S(2)}) %collective-permute-start.24) | collective-permute-done | bytes 524320 | tf_op jit(solution)/shard_map/ppermute | solution.py:37
  257.4 18.7 %hidden_part.1 = (bf16[2048,704]{1,0:T(8,128)(2,1)}, bf16[2048,704]{1,0:T(8,128)(2,1)}, bf16[2048,704]{1,0:T(8,128)(2,1)}) custom-call(bf16[1024,1024]{1,0:T(8,128)(2,1)} %copy-done.40, bf16[1024,1024]{1,0:T(8,128)(2,1)} %copy-done.100, bf16[1024,1024]{1,0:T(8,128)(2,1)} %copy-done.77, bf16[1024,1024]{1,0:T(8,128)(2,1)} %copy-done.38, ...), custom_call_target="tpu_custom_call" | custom-call | flops 11811160064 | bytes 25165824 | tf_op jit(solution)/shard_map/hidden_part/pallas_call | solution.py:368
  276.1 7.6 %convolution_convert_fusion.6 = bf16[704,1024]{1,0:T(8,128)(2,1)} fusion(bf16[2048,704]{1,0:T(8,128)(2,1)} %get-tuple-element.201, bf16[2048,1024]{1,0:T(8,128)(2,1)} %copy-done.88), kind=kOutput, calls=%fused_computation.93 | convolution fusion | flops 2953510912 | bytes 8519680 | tf_op jit(solution)/shard_map/dot_general | solution.py:194
  288.0 9.8 %back_part.3 = (bf16[1024,1024]{1,0:T(8,128)(2,1)}, bf16[1024,1024]{1,0:T(8,128)(2,1)}) custom-call(bf16[2048,704]{1,0:T(8,128)(2,1)} %get-tuple-element.165.grad_gate_ref, bf16[2048,704]{1,0:T(8,128)(2,1)} %get-tuple-element.171.grad_up_ref, bf16[1024,704]{1,0:T(8,128)(2,1)S(1)} %copy-done.2, bf16[1024,704]{1,0:T(8,128)(2,1)S(1)} %copy-done.3, ...), custom_call_target="tpu_custom_call" | custom-call | flops 5905580032 | bytes 12582912 | tf_op jit(solution)/shard_map/back_part/pallas_call | solution.py:397
  304.2 10.2 %back_part.2 = (bf16[1024,1024]{1,0:T(8,128)(2,1)}, bf16[1024,1024]{1,0:T(8,128)(2,1)}) custom-call(bf16[2048,704]{1,0:T(8,128)(2,1)} %get-tuple-element.165.grad_gate_ref, bf16[2048,704]{1,0:T(8,128)(2,1)} %get-tuple-element.171.grad_up_ref, bf16[1024,704]{1,0:T(8,128)(2,1)S(1)} %copy-done.2, bf16[1024,704]{1,0:T(8,128)(2,1)S(1)} %copy-done.3, ...), custom_call_target="tpu_custom_call" | custom-call | flops 5905580032 | bytes 12582912 | tf_op jit(solution)/shard_map/back_part/pallas_call | solution.py:397
  322.2 9.9 %collective-permute-done.29 = bf16[704,1024]{1,0:T(8,128)(2,1)S(1)} collective-permute-done((bf16[704,1024]{1,0:T(8,128)(2,1)}, bf16[704,1024]{1,0:T(8,128)(2,1)S(1)}, u32[]{:S(2)}, u32[]{:S(2)}) %collective-permute-start.29) | collective-permute-done | bytes 1441824 | tf_op jit(solution)/shard_map/ppermute | solution.py:37
  339.9 7.2 %collective-permute-start.35 = (bf16[704,1024]{1,0:T(8,128)(2,1)S(1)}, bf16[704,1024]{1,0:T(8,128)(2,1)S(1)}, u32[]{:S(2)}, u32[]{:S(2)}) collective-permute-start(bf16[704,1024]{1,0:T(8,128)(2,1)S(1)} %collective-permute-done.29), channel_id=1, source_target_pairs={{0,8},{24,16},{1,9},{25,17},{2,10},{26,18},{3,11},{27,19},{4,12},{... | collective-permute-start | bytes 4325384 | tf_op jit(solution)/shard_map/ppermute | solution.py:129
  361.8 14.3 %collective-permute-done.35 = bf16[704,1024]{1,0:T(8,128)(2,1)S(1)} collective-permute-done((bf16[704,1024]{1,0:T(8,128)(2,1)S(1)}, bf16[704,1024]{1,0:T(8,128)(2,1)S(1)}, u32[]{:S(2)}, u32[]{:S(2)}) %collective-permute-start.35) | collective-permute-done | bytes 1441824 | tf_op jit(solution)/shard_map/ppermute | solution.py:129
  395.5 16.1 %collective-permute-done.42 = bf16[704,1024]{1,0:T(8,128)(2,1)S(1)} collective-permute-done((bf16[704,1024]{1,0:T(8,128)(2,1)S(1)}, bf16[704,1024]{1,0:T(8,128)(2,1)S(1)}, u32[]{:S(2)}, u32[]{:S(2)}) %collective-permute-start.42) | collective-permute-done | bytes 1441824 | tf_op jit(solution)/shard_map/ppermute | solution.py:158
  420.3 7.6 %collective-permute-start.48 = (bf16[704,1024]{1,0:T(8,128)(2,1)S(1)}, bf16[704,1024]{1,0:T(8,128)(2,1)S(1)}, u32[]{:S(2)}, u32[]{:S(2)}) collective-permute-start(bf16[704,1024]{1,0:T(8,128)(2,1)S(1)} %fusion.31), channel_id=1, source_target_pairs={{0,8},{24,16},{1,9},{25,17},{2,10},{26,18},{3,11},{27,19},{4,12},{... | collective-permute-start | bytes 4325384 | tf_op jit(solution)/shard_map/ppermute | solution.py:129
  432.9 14.3 %collective-permute-done.46 = bf16[704,1024]{1,0:T(8,128)(2,1)S(1)} collective-permute-done((bf16[704,1024]{1,0:T(8,128)(2,1)S(1)}, bf16[704,1024]{1,0:T(8,128)(2,1)S(1)}, u32[]{:S(2)}, u32[]{:S(2)}) %collective-permute-start.46) | collective-permute-done | bytes 1441824 | tf_op jit(solution)/shard_map/ppermute | solution.py:158
  471.6 10.0 %collective-permute-done.49.refs_1_ = bf16[1024,512]{1,0:T(8,128)(2,1)S(1)} collective-permute-done((bf16[1024,512]{1,0:T(8,128)(2,1)S(1)}, bf16[1024,512]{1,0:T(8,128)(2,1)S(1)}, u32[]{:S(2)}, u32[]{:S(2)}) %collective-permute-start.49) | collective-permute-done | bytes 1048608 | tf_op jit(solution)/shard_map/ppermute | solution.py:37
  498.0 22.2 %attention_backward.1 = bf16[1024,640]{1,0:T(8,128)(2,1)S(1)} custom-call(f32[1024,512]{1,0:T(8,128)} %fusion.100.refs_0_, bf16[1024,512]{1,0:T(8,128)(2,1)S(1)} %collective-permute-done.49.refs_1_, bf16[1024,512]{1,0:T(8,128)(2,1)S(1)} %copy-done.11, bf16[1024,128]{1,0:T(8,128)(2,1)S(1)} %get-tuple-element.190.refs_3_, ...), custom_call_target="tpu_custom_call" | custom-call | flops 40000000000 | bytes 8388608 | tf_op jit(solution)/shard_map/attention_backward/pallas_call | solution.py:460
  529.1 7.5 %collective-permute-start.62 = (bf16[704,1024]{1,0:T(8,128)(2,1)S(1)}, bf16[704,1024]{1,0:T(8,128)(2,1)S(1)}, u32[]{:S(2)}, u32[]{:S(2)}) collective-permute-start(bf16[704,1024]{1,0:T(8,128)(2,1)S(1)} %collective-permute-done.53), channel_id=1, source_target_pairs={{0,8},{24,16},{1,9},{25,17},{2,10},{26,18},{3,11},{27,19},{4,12},{... | collective-permute-start | bytes 4325384 | tf_op jit(solution)/shard_map/ppermute | solution.py:129
  545.6 21.6 %collective-permute-done.57 = bf16[1024,640]{1,0:T(8,128)(2,1)S(1)} collective-permute-done((bf16[1024,640]{1,0:T(8,128)(2,1)S(1)}, bf16[1024,640]{1,0:T(8,128)(2,1)S(1)}, u32[]{:S(2)}, u32[]{:S(2)}) %collective-permute-start.57) | collective-permute-done | bytes 1310752 | tf_op jit(solution)/shard_map/ppermute | solution.py:37
  595.1 20.0 %collective-permute-done.65 = bf16[512,1024]{1,0:T(8,128)(2,1)S(1)} collective-permute-done((bf16[512,1024]{1,0:T(8,128)(2,1)S(1)}, bf16[512,1024]{1,0:T(8,128)(2,1)S(1)}, u32[]{:S(2)}, u32[]{:S(2)}) %collective-permute-start.65) | collective-permute-done | bytes 1048608 | tf_op jit(solution)/shard_map/ppermute | solution.py:37
  646.5 15.2 %collective-permute-done.71 = f32[2,1024]{1,0:T(2,128)S(1)} collective-permute-done((f32[2,1024]{1,0:T(2,128)S(1)}, f32[2,1024]{1,0:T(2,128)S(1)}, u32[]{:S(2)}, u32[]{:S(2)}) %collective-permute-start.71) | collective-permute-done | bytes 8224 | tf_op jit(solution)/shard_map/ppermute | solution.py:37
  684.4 10.6 %collective-permute-done.74 = bf16[512,1024]{1,0:T(8,128)(2,1)} collective-permute-done((bf16[512,1024]{1,0:T(8,128)(2,1)}, bf16[512,1024]{1,0:T(8,128)(2,1)}, u32[]{:S(2)}, u32[]{:S(2)}) %collective-permute-start.74) | collective-permute-done | bytes 1048608 | tf_op jit(solution)/shard_map/ppermute | solution.py:37
  (508 shorter events, 378.3 us)
Async XLA Ops:
  59.6 41.0 %collective-permute-start.6 = (bf16[1024,640]{1,0:T(8,128)(2,1)S(1)}, bf16[1024,640]{1,0:T(8,128)(2,1)S(1)}, u32[]{:S(2)}, u32[]{:S(2)}) collective-permute-start(bf16[1024,640]{1,0:T(8,128)(2,1)S(1)} %convolution_convert_fusion.8), channel_id=1, source_target_pairs={{0,1},{1,0},{2,3},{3,2},{4,5},{5,4},{6,7},{7,6},{8,9},{9,8},{10,11... | collective-permute-start | bytes 3932168 | tf_op jit(solution)/shard_map/ppermute | solution.py:37
  64.6 59.3 %collective-permute-start.10 = (bf16[512,704]{0,1:T(8,128)(2,1)S(1)}, bf16[512,704]{0,1:T(8,128)(2,1)S(1)}, u32[]{:S(2)}, u32[]{:S(2)}) collective-permute-start(bf16[512,704]{0,1:T(8,128)(2,1)S(1)} %copy-done.68), channel_id=1, source_target_pairs={{0,8},{8,0},{16,24},{24,16},{1,9},{9,1},{17,25},{25,17},{2,10},{10... | collective-permute-start | bytes 2162696 | tf_op jit(solution)/shard_map/ppermute | solution.py:37
  66.3 57.6 %collective-permute-start.11 = (bf16[352,1024]{1,0:T(8,128)(2,1)}, bf16[352,1024]{1,0:T(8,128)(2,1)S(1)}, u32[]{:S(2)}, u32[]{:S(2)}) collective-permute-start(bf16[352,1024]{1,0:T(8,128)(2,1)} %collective-permute-done.5), channel_id=1, source_target_pairs={{0,8},{8,0},{16,24},{24,16},{1,9},{9,1},{17,25},{25,17},{2,10},{10... | collective-permute-start | bytes 2162696 | tf_op jit(solution)/shard_map/ppermute | solution.py:37
  135.0 43.6 %collective-permute-start.17 = (bf16[1024,1024]{1,0:T(8,128)(2,1)}, bf16[1024,1024]{1,0:T(8,128)(2,1)}, u32[]{:S(2)}, u32[]{:S(2)}) collective-permute-start(bf16[1024,1024]{1,0:T(8,128)(2,1)} %pad_maximum_fusion.3), channel_id=1, source_target_pairs={{0,2},{2,0},{4,6},{6,4},{1,3},{3,1},{5,7},{7,5},{8,10},{10,8},{12,... | collective-permute-start | bytes 6291464 | tf_op jit(solution)/shard_map/ppermute | solution.py:37
  298.3 33.8 %collective-permute-start.29 = (bf16[704,1024]{1,0:T(8,128)(2,1)}, bf16[704,1024]{1,0:T(8,128)(2,1)S(1)}, u32[]{:S(2)}, u32[]{:S(2)}) collective-permute-start(bf16[704,1024]{1,0:T(8,128)(2,1)} %convolution_convert_fusion.6), channel_id=1, source_target_pairs={{0,1},{1,0},{2,3},{3,2},{4,5},{5,4},{6,7},{7,6},{8,9},{9,8},{10,11... | collective-permute-start | bytes 4325384 | tf_op jit(solution)/shard_map/ppermute | solution.py:37
  299.6 34.7 %collective-permute-start.33 = (bf16[704,1024]{1,0:T(8,128)(2,1)}, bf16[704,1024]{1,0:T(8,128)(2,1)}, u32[]{:S(2)}, u32[]{:S(2)}) collective-permute-start(bf16[704,1024]{1,0:T(8,128)(2,1)} %convolution_convert_fusion.7), channel_id=1, source_target_pairs={{0,8},{24,16},{1,9},{25,17},{2,10},{26,18},{3,11},{27,19},{4,12},{... | collective-permute-start | bytes 4325384 | tf_op jit(solution)/shard_map/ppermute | solution.py:129
  339.9 36.1 %collective-permute-start.35 = (bf16[704,1024]{1,0:T(8,128)(2,1)S(1)}, bf16[704,1024]{1,0:T(8,128)(2,1)S(1)}, u32[]{:S(2)}, u32[]{:S(2)}) collective-permute-start(bf16[704,1024]{1,0:T(8,128)(2,1)S(1)} %collective-permute-done.29), channel_id=1, source_target_pairs={{0,8},{24,16},{1,9},{25,17},{2,10},{26,18},{3,11},{27,19},{4,12},{... | collective-permute-start | bytes 4325384 | tf_op jit(solution)/shard_map/ppermute | solution.py:129
  379.6 32.0 %collective-permute-start.42 = (bf16[704,1024]{1,0:T(8,128)(2,1)S(1)}, bf16[704,1024]{1,0:T(8,128)(2,1)S(1)}, u32[]{:S(2)}, u32[]{:S(2)}) collective-permute-start(bf16[704,1024]{1,0:T(8,128)(2,1)S(1)} %add_convert_fusion.12), channel_id=1, source_target_pairs={{8,0},{16,24},{9,1},{17,25},{10,2},{18,26},{11,3},{19,27},{12,4},{... | collective-permute-start | bytes 4325384 | tf_op jit(solution)/shard_map/ppermute | solution.py:158
  381.5 30.1 %collective-permute-start.43 = (bf16[704,1024]{1,0:T(8,128)(2,1)S(1)}, bf16[704,1024]{1,0:T(8,128)(2,1)S(1)}, u32[]{:S(2)}, u32[]{:S(2)}) collective-permute-start(bf16[704,1024]{1,0:T(8,128)(2,1)S(1)} %add_convert_fusion.11), channel_id=1, source_target_pairs={{8,16},{16,8},{9,17},{17,9},{10,18},{18,10},{11,19},{19,11},{12,20... | collective-permute-start | bytes 4325384 | tf_op jit(solution)/shard_map/ppermute | solution.py:158
  382.2 33.3 %collective-permute-start.44 = (bf16[704,1024]{1,0:T(8,128)(2,1)S(1)}, bf16[704,1024]{1,0:T(8,128)(2,1)S(1)}, u32[]{:S(2)}, u32[]{:S(2)}) collective-permute-start(bf16[704,1024]{1,0:T(8,128)(2,1)S(1)} %fusion.30), channel_id=1, source_target_pairs={{0,8},{24,16},{1,9},{25,17},{2,10},{26,18},{3,11},{27,19},{4,12},{... | collective-permute-start | bytes 4325384 | tf_op jit(solution)/shard_map/ppermute | solution.py:129
  395.5 32.4 %collective-permute-start.39 = (bf16[512,1024]{1,0:T(8,128)(2,1)S(1)}, bf16[512,1024]{1,0:T(8,128)(2,1)S(1)}, u32[]{:S(2)}, u32[]{:S(2)}) collective-permute-start(bf16[512,1024]{1,0:T(8,128)(2,1)S(1)} %fusion.95), channel_id=1, source_target_pairs={{0,2},{2,0},{4,6},{6,4},{1,3},{3,1},{5,7},{7,5},{8,10},{10,8},{12,... | collective-permute-start | bytes 3145736 | tf_op jit(solution)/shard_map/ppermute | solution.py:37
  416.2 31.0 %collective-permute-start.46 = (bf16[704,1024]{1,0:T(8,128)(2,1)S(1)}, bf16[704,1024]{1,0:T(8,128)(2,1)S(1)}, u32[]{:S(2)}, u32[]{:S(2)}) collective-permute-start(bf16[704,1024]{1,0:T(8,128)(2,1)S(1)} %add_convert_fusion.10), channel_id=1, source_target_pairs={{8,0},{16,24},{9,1},{17,25},{10,2},{18,26},{11,3},{19,27},{12,4},{... | collective-permute-start | bytes 4325384 | tf_op jit(solution)/shard_map/ppermute | solution.py:158
  420.3 32.7 %collective-permute-start.48 = (bf16[704,1024]{1,0:T(8,128)(2,1)S(1)}, bf16[704,1024]{1,0:T(8,128)(2,1)S(1)}, u32[]{:S(2)}, u32[]{:S(2)}) collective-permute-start(bf16[704,1024]{1,0:T(8,128)(2,1)S(1)} %fusion.31), channel_id=1, source_target_pairs={{0,8},{24,16},{1,9},{25,17},{2,10},{26,18},{3,11},{27,19},{4,12},{... | collective-permute-start | bytes 4325384 | tf_op jit(solution)/shard_map/ppermute | solution.py:129
  456.3 32.3 %collective-permute-start.52 = (bf16[704,1024]{1,0:T(8,128)(2,1)S(1)}, bf16[704,1024]{1,0:T(8,128)(2,1)S(1)}, u32[]{:S(2)}, u32[]{:S(2)}) collective-permute-start(bf16[704,1024]{1,0:T(8,128)(2,1)S(1)} %collective-permute-done.45), channel_id=1, source_target_pairs={{0,8},{24,16},{1,9},{25,17},{2,10},{26,18},{3,11},{27,19},{4,12},{... | collective-permute-start | bytes 4325384 | tf_op jit(solution)/shard_map/ppermute | solution.py:129
  489.9 30.3 %collective-permute-start.56 = (bf16[512,1024]{1,0:T(8,128)(2,1)S(1)}, bf16[512,1024]{1,0:T(8,128)(2,1)S(1)}, u32[]{:S(2)}, u32[]{:S(2)}) collective-permute-start(bf16[512,1024]{1,0:T(8,128)(2,1)S(1)} %fusion.37), channel_id=1, source_target_pairs={{0,8},{24,16},{1,9},{25,17},{2,10},{26,18},{3,11},{27,19},{4,12},{... | collective-permute-start | bytes 3145736 | tf_op jit(solution)/shard_map/ppermute | solution.py:129
  527.8 39.4 %collective-permute-start.60 = (bf16[704,1024]{1,0:T(8,128)(2,1)S(1)}, bf16[704,1024]{1,0:T(8,128)(2,1)S(1)}, u32[]{:S(2)}, u32[]{:S(2)}) collective-permute-start(bf16[704,1024]{1,0:T(8,128)(2,1)S(1)} %add_convert_fusion.4), channel_id=1, source_target_pairs={{8,0},{16,24},{9,1},{17,25},{10,2},{18,26},{11,3},{19,27},{12,4},{... | collective-permute-start | bytes 4325384 | tf_op jit(solution)/shard_map/ppermute | solution.py:158
  529.1 38.5 %collective-permute-start.62 = (bf16[704,1024]{1,0:T(8,128)(2,1)S(1)}, bf16[704,1024]{1,0:T(8,128)(2,1)S(1)}, u32[]{:S(2)}, u32[]{:S(2)}) collective-permute-start(bf16[704,1024]{1,0:T(8,128)(2,1)S(1)} %collective-permute-done.53), channel_id=1, source_target_pairs={{0,8},{24,16},{1,9},{25,17},{2,10},{26,18},{3,11},{27,19},{4,12},{... | collective-permute-start | bytes 4325384 | tf_op jit(solution)/shard_map/ppermute | solution.py:129
  536.7 30.5 %collective-permute-start.57 = (bf16[1024,640]{1,0:T(8,128)(2,1)S(1)}, bf16[1024,640]{1,0:T(8,128)(2,1)S(1)}, u32[]{:S(2)}, u32[]{:S(2)}) collective-permute-start(bf16[1024,640]{1,0:T(8,128)(2,1)S(1)} %attention_backward.1), channel_id=1, source_target_pairs={{0,1},{1,0},{2,3},{3,2},{4,5},{5,4},{6,7},{7,6},{8,9},{9,8},{10,11... | collective-permute-start | bytes 3932168 | tf_op jit(solution)/shard_map/ppermute | solution.py:37
  581.0 37.5 %collective-permute-start.68 = (bf16[1024,640]{0,1:T(8,128)(2,1)S(1)}, bf16[1024,640]{0,1:T(8,128)(2,1)S(1)}, u32[]{:S(2)}, u32[]{:S(2)}) collective-permute-start(bf16[1024,640]{0,1:T(8,128)(2,1)S(1)} %fusion.32), channel_id=1, source_target_pairs={{0,8},{24,16},{1,9},{25,17},{2,10},{26,18},{3,11},{27,19},{4,12},{... | collective-permute-start | bytes 3932168 | tf_op jit(solution)/shard_map/ppermute | solution.py:129
  585.2 33.3 %collective-permute-start.67 = (bf16[704,1024]{1,0:T(8,128)(2,1)S(1)}, bf16[704,1024]{1,0:T(8,128)(2,1)S(1)}, u32[]{:S(2)}, u32[]{:S(2)}) collective-permute-start(bf16[704,1024]{1,0:T(8,128)(2,1)S(1)} %add_convert_fusion.3), channel_id=1, source_target_pairs={{8,16},{16,8},{9,17},{17,9},{10,18},{18,10},{11,19},{19,11},{12,20... | collective-permute-start | bytes 4325384 | tf_op jit(solution)/shard_map/ppermute | solution.py:158
  593.3 53.2 %collective-permute-start.63 = (bf16[1024,1024]{1,0:T(8,128)(2,1)}, bf16[1024,1024]{1,0:T(8,128)(2,1)}, u32[]{:S(2)}, u32[]{:S(2)}) collective-permute-start(bf16[1024,1024]{1,0:T(8,128)(2,1)} %add_convert_fusion.1), channel_id=1, source_target_pairs={{0,1},{1,0},{2,3},{3,2},{4,5},{5,4},{6,7},{7,6},{8,9},{9,8},{10,11... | collective-permute-start | bytes 6291464 | tf_op jit(solution)/shard_map/ppermute | solution.py:37
  623.7 38.0 %collective-permute-start.73 = (bf16[1024,640]{0,1:T(8,128)(2,1)}, bf16[1024,640]{0,1:T(8,128)(2,1)}, u32[]{:S(2)}, u32[]{:S(2)}) collective-permute-start(bf16[1024,640]{0,1:T(8,128)(2,1)} %add_convert_fusion.15), channel_id=1, source_target_pairs={{8,16},{16,8},{9,17},{17,9},{10,18},{18,10},{11,19},{19,11},{12,20... | collective-permute-start | bytes 3932168 | tf_op jit(solution)/shard_map/ppermute | solution.py:158
  625.4 36.3 %collective-permute-start.72 = (bf16[704,1024]{1,0:T(8,128)(2,1)}, bf16[704,1024]{1,0:T(8,128)(2,1)}, u32[]{:S(2)}, u32[]{:S(2)}) collective-permute-start(bf16[704,1024]{1,0:T(8,128)(2,1)} %add_convert_fusion.2), channel_id=1, source_target_pairs={{8,0},{16,24},{9,1},{17,25},{10,2},{18,26},{11,3},{19,27},{12,4},{... | collective-permute-start | bytes 4325384 | tf_op jit(solution)/shard_map/ppermute | solution.py:158
  671.3 32.2 %collective-permute-start.77 = (bf16[1024,640]{0,1:T(8,128)(2,1)}, bf16[1024,640]{0,1:T(8,128)(2,1)}, u32[]{:S(2)}, u32[]{:S(2)}) collective-permute-start(bf16[1024,640]{0,1:T(8,128)(2,1)} %add_convert_fusion.14), channel_id=1, source_target_pairs={{8,0},{16,24},{9,1},{17,25},{10,2},{18,26},{11,3},{19,27},{12,4},{... | collective-permute-start | bytes 3932168 | tf_op jit(solution)/shard_map/ppermute | solution.py:158
  (163 other events, 2260.1 us)
